TPU v7x, 256 devices: a whole 4x4x8 slice. The times are simulated.
256 devices in a mesh: pts: 32 (over x, z_hi, y), modes: 8 (over z_lo, core).
Axes of the slice: x: 4, y: 4, z: 8 (z_hi: 2, z_lo: 4; z = z_hi * 4 + z_lo), core: 2. Of those that a mesh axis runs over, the one named last changes fastest.
Arguments:
- density: bfloat16 [5120, 1024], P('pts'), may hold values from -6 to 6
- near_blocks: bfloat16 [27, 1024, 1024], P(None, 'modes'), may hold values from -0.09375 to 0.09375
- neighbour_atoms: int32 [5120, 27], P('pts'), may hold values from 0 to 5119, as said below
- neighbour_offsets: int32 [5120, 27], P('pts'), may hold values from 0 to 26, as said below
- neighbour_counts: int32 [5120], P('pts'), may hold values from 1 to 27, as said below
- centers: float32 [2, 5120], P(None, 'pts'), may hold values from -4 to 4
- local_points: float32 [2, 1024], replicated, may hold values from -0.5 to 0.5
- wavevectors: float32 [2, 16384], P(None, 'modes'), may hold values from -24 to 24
- spectral_weight: float32 [16384], P('modes'), may hold values from 0.1 to 4
Outputs:
- potential: float32 [5120, 1024], P('pts', 'modes')
Inputs may be any that keep to these rules, and one draw needn't show every extreme that they name: `neighbour_atoms`: each neighbour of an atom lies, cyclically over the 5120 atoms, among the 160 atoms before the aligned block of 160 atoms holding it, that block, or the 160 atoms after it; in every block both ends of that range are named. `neighbour_offsets`: each row names every offset class once. `neighbour_counts`: every aligned block of 160 atoms holds an atom with 27 live slots and one with 1.
All inputs are finite; a program needn't handle non-finite values.
Results may differ from a plain program's by a relative error of at most 0.0012.
Values may be sent and summed in bfloat16 or wider, within the bound.
No kernel may reach another device: no remote copies, remote signals or barrier semaphores. Data moves between devices by JAX's collectives and lax.ppermute only.
A program may use at most 128 MiB of HBM per device.

v0:
```python
import math

import jax
import jax.numpy as jnp
from jax import lax
from jax.sharding import PartitionSpec as P


def extended_2(block, sides, width):
    for axis, dim in sides:
        count = lax.axis_size(axis)
        forward = [(i, i + 1) for i in range(count - 1)]
        forward.append((count - 1, 0))
        backward = [(target, source) for source, target in forward]
        low = lax.ppermute(
            lax.slice_in_dim(block, block.shape[dim] - width, None, axis=dim), axis, forward
        )
        high = lax.ppermute(lax.slice_in_dim(block, 0, width, axis=dim), axis, backward)
        block = jnp.concatenate([low, block, high], axis=dim)
    return block


def phase_tables(point_pos, wave_pos):
    phase = (
        point_pos[0][:, None] * wave_pos[0][None, :] + point_pos[1][:, None] * wave_pos[1][None, :]
    )
    return jnp.concatenate([jnp.cos(phase), jnp.sin(phase)], axis=1).astype(jnp.bfloat16)


def center_phase(center_pos, wave_pos):
    return (
        center_pos[0][:, None] * wave_pos[0][None, :]
        + center_pos[1][:, None] * wave_pos[1][None, :]
    )


def spread_modes(weighted, cos_c, sin_c):
    real_part = weighted[0][None, :] * cos_c - weighted[1][None, :] * sin_c
    imag_part = weighted[0][None, :] * sin_c + weighted[1][None, :] * cos_c
    return jnp.concatenate([real_part, -imag_part], axis=1).astype(jnp.bfloat16)


def shards(
    density,
    near_blocks,
    neighbour_atoms,
    neighbour_offsets,
    neighbour_counts,
    centers,
    local_points,
    wavevectors,
    spectral_weight,
):
    atoms_here, points = density.shape
    groups = lax.axis_size("pts")
    mode_groups = lax.axis_size("modes")
    modes_here = wavevectors.shape[1]
    block_points = points // mode_groups
    block_index = lax.axis_index("modes")
    normalizer = 1.0 / math.sqrt(atoms_here * groups * points * modes_here * mode_groups)
    extended = extended_2(density, (("pts", 0),), atoms_here)
    tables = phase_tables(local_points, wavevectors)
    form_factors = jnp.dot(density, tables, preferred_element_type=jnp.float32)
    angles = center_phase(centers, wavevectors)
    cos_c = jnp.cos(angles)
    sin_c = jnp.sin(angles)
    form_cos = form_factors[:, :modes_here]
    form_sin = form_factors[:, modes_here:]
    real_part = jnp.sum(cos_c * form_cos - sin_c * form_sin, axis=0)
    imag_part = -jnp.sum(sin_c * form_cos + cos_c * form_sin, axis=0)
    structure = lax.psum(jnp.stack([real_part, imag_part]), "pts")
    weighted = structure * (spectral_weight * normalizer)[None, :]
    extended = jnp.concatenate([extended, jnp.zeros((1, points), extended.dtype)], axis=0)
    first_atom = lax.axis_index("pts") * atoms_here
    total_atoms = atoms_here * groups
    local_index = (neighbour_atoms - first_atom + atoms_here) % total_atoms
    slot_count = neighbour_atoms.shape[1]
    class_count = near_blocks.shape[0]
    live_slots = jnp.arange(slot_count)[None, :] < neighbour_counts[:, None]
    matches = (
        neighbour_offsets[:, :, None] == jnp.arange(class_count)[None, None, :]
    ) & live_slots[:, :, None]
    picked = jnp.sum(jnp.where(matches, local_index[:, :, None] + 1, 0), axis=1) - 1
    picked = jnp.where(picked < 0, 3 * atoms_here, picked)
    gathered = jnp.take(extended, picked, axis=0)
    near_field = jnp.einsum(
        "aoq,okq->ak", gathered, near_blocks, preferred_element_type=jnp.float32
    )
    spread = spread_modes(weighted, cos_c, sin_c)
    far_all = lax.dot_general(
        spread, tables, (((1,), (1,)), ((), ())), preferred_element_type=jnp.float32
    )
    far_field = lax.psum_scatter(far_all, "modes", scatter_dimension=1, tiled=True)
    own_density = lax.dynamic_slice_in_dim(
        density, block_index * block_points, block_points, 1
    ).astype(jnp.float32)
    return 0.5 * own_density + near_field + far_field


def solution(mesh):
    placed = (
        P("pts", None),
        P(None, "modes", None),
        P("pts", None),
        P("pts", None),
        P("pts"),
        P(None, "pts"),
        P(),
        P(None, "modes"),
        P("modes"),
    )
    return jax.shard_map(
        shards, mesh=mesh, in_specs=placed, out_specs=P("pts", "modes"), check_vma=False
    )
```

profile of v0, /device:TPU:32, one launch (start us, length us, event | category | flops | bytes accessed | tf_op | source)
XLA Modules:
  0.0 349.4 jit_solution(1908114065730199781)
XLA Ops:
  6.5 1.6 collective-permute-start
  8.1 9.4 %collective-permute-start.1 = (bf16[160,1024]{1,0:T(8,128)(2,1)}, bf16[160,1024]{1,0:T(8,128)(2,1)S(1)}, u32[]{:S(2)}, u32[]{:S(2)}) collective-permute-start(bf16[160,1024]{1,0:T(8,128)(2,1)} %param.9), channel_id=1, source_target_pairs={{8,0},{16,8},{24,16},{32,24},{40,32},{48,40},{56,48},{64,56},{72,6... | collective-permute-start | bytes 983048 | tf_op jit(solution)/shard_map/ppermute | solution.py:18
  17.5 0.8 fusion.24
  18.3 0.8 fusion.25
  19.1 0.8 fusion.26
  19.8 30.9 %cosine_convert_fusion = (bf16[1024,2048]{1,0:T(8,128)(2,1)S(1)}, bf16[1024,2048]{1,0:T(8,128)(2,1)S(1)}) fusion(f32[2048]{0:T(1024)S(1)} %bitcast.28, f32[1024]{0:T(1024)S(1)} %bitcast.36, f32[2048]{0:T(1024)S(1)} %bitcast.25, f32[1024]{0:T(1024)S(1)} %bitcast.35), kind=kLoop, calls=%fused_computation.6 | loop fusion | flops 10485760 | bytes 8413184 | tf_op jit(solution)/shard_map/convert.2
  50.8 1.6 fusion.4
  52.3 0.3 copy-done
  52.7 1.2 copy-done.1
  53.9 5.5 %subtract_reduce_fusion = (f32[2048]{0:T(1024)S(1)}, f32[2048]{0:T(1024)S(1)}) fusion(f32[160,4096]{1,0:T(8,128)S(1)} %fusion.4, f32[2048]{0:T(1024)S(1)} %bitcast.29, f32[160]{0:T(256)S(1)} %bitcast.39, f32[2048]{0:T(1024)S(1)} %bitcast.26, f32[160]{0:T(256)S(1)} %bitcast.37), kind=kLoop, calls=%fused_computation.17 | loop fusion | flops 3600384 | bytes 2655488 | tf_op jit(solution)/shard_map/reduce_sum | solution.py:69
  59.5 216.8 %psum.7 = f32[2,2048]{1,0:T(2,128)S(1)} all-reduce(f32[2,2048]{1,0:T(2,128)S(1)} %pad_maximum_fusion.5), channel_id=1, replica_groups=mesh['pts'=32,'modes'=8] {'pts'}, use_global_device_ids=true, to_apply=%region_3.4 | all-reduce | flops 4096 | bytes 32768 | tf_op jit(solution)/shard_map/psum | solution.py:71
  276.3 5.3 %subtract_convert_fusion = (bf16[160,2048]{1,0:T(8,128)(2,1)S(1)}, bf16[160,2048]{1,0:T(8,128)(2,1)S(1)}) fusion(f32[2048]{0:T(1024)S(1)} %bitcast.32, f32[2048]{0:T(1024)S(1)} %bitcast.31, f32[2048]{0:T(1024)S(1)} %bitcast.30, f32[160]{0:T(256)S(1)} %bitcast.40, f32[2048]{0:T(1024)S(1)} %bitcast.27, f32[160]{0:T(256)S(1)} %bitcast.38), kind=kLoop, calls=%fused_computation.15 | loop fusion | flops 3932160 | bytes 1344768 | tf_op jit(solution)/shard_map/convert
  281.6 7.2 %fusion.2 = f32[160,1024]{1,0:T(8,128)} fusion(bf16[1024,2048]{1,0:T(8,128)(2,1)} %copy-done.1, bf16[1024,2048]{1,0:T(8,128)(2,1)} %copy-done, bf16[160,2048]{1,0:T(8,128)(2,1)S(1)} %get-tuple-element.8, bf16[160,2048]{1,0:T(8,128)(2,1)S(1)} %get-tuple-element.7), kind=kOutput, calls=%fused_computation.8 | convolution fusion | flops 1361575936 | bytes 10354688 | tf_op jit(solution)/shard_map/dot_general | solution.py:90
  288.9 0.0 reduce-scatter.2.cloned.1.call-update
  289.0 0.2 select_reduce_fusion
  289.2 0.1 copy.19
  289.4 0.2 reshape.68
  289.6 0.1 copy.18
  289.7 0.1 pad.9.clone
  289.8 0.2 maximum_maximum_fusion
  290.1 14.1 %gather_fusion = bf16[4320,1024]{1,0:T(8,128)(2,1)} fusion(bf16[481,1024]{1,0:T(8,128)(2,1)S(1)} %maximum_maximum_fusion, s32[5120]{0:T(1024)S(1)} %pad_clamp_fusion), kind=kCustom, calls=%fused_computation | custom fusion | bytes 17712000 | tf_op jit(solution)/shard_map/jit(_take)/gather | solution.py:85
  304.2 11.3 %reshape.67 = bf16[160,27,1024]{2,1,0:T(8,128)(2,1)} reshape(bf16[4320,1024]{1,0:T(8,128)(2,1)} %gather_fusion) | data formatting | bytes 17694720 | tf_op jit(solution)/shard_map/jit(_take)/gather | solution.py:85
  315.5 10.1 %broadcast_select_fusion = bf16[160,27,1024]{2,1,0:T(8,128)(2,1)} fusion(bf16[160,27,1024]{2,1,0:T(8,128)(2,1)} %reshape.67, pred[160,27]{1,0:T(8,128)(4,1)S(1)} %copy.18), kind=kLoop, calls=%fused_computation.1 | loop fusion | flops 4423680 | bytes 17699040 | tf_op jit(solution)/shard_map/jit(_take)/select_n | solution.py:85
  325.6 17.0 %fusion.16 = f32[160,128]{1,0:T(8,128)} fusion(f32[160,128]{1,0:T(8,128)} %reduce-scatter.2.cloned.1.call-done, bf16[27,128,1024]{2,1,0:T(8,128)(2,1)} %param.10, bf16[160,27,1024]{2,1,0:T(8,128)(2,1)} %broadcast_select_fusion, bf16[160,1024]{1,0:T(8,128)(2,1)S(1)} %copy-done.2, s32[]{:T(128)S(6)} %select_n.49), kind=kOutput, calls=%fused_computation.23 | convolution fusion | flops 1132544000 | bytes 16130052 | tf_op jit(solution)/shard_map/aoq,okq->ak/dot_general | solution.py:86
  (26 shorter events, 0.2 us)
Async XLA Ops:
  6.5 319.1 %reduce-scatter.2.cloned.1.call-start = ((), (), s32[]{:S(2)}) async-start(), calls=%async_computation.1 | async-start | bytes 737280 | tf_op jit(solution)/shard_map/reduce_scatter | solution.py:93
  6.5 283.3 %collective-permute-start = (bf16[160,1024]{1,0:T(8,128)(2,1)}, bf16[160,1024]{1,0:T(8,128)(2,1)S(1)}, u32[]{:S(2)}, u32[]{:S(2)}) collective-permute-start(bf16[160,1024]{1,0:T(8,128)(2,1)} %param.9), channel_id=1, source_target_pairs={{0,8},{8,16},{16,24},{24,32},{32,40},{40,48},{48,56},{56,64},{64,7... | collective-permute-start | bytes 983048 | tf_op jit(solution)/shard_map/ppermute | solution.py:15
  8.1 281.7 %collective-permute-start.1 = (bf16[160,1024]{1,0:T(8,128)(2,1)}, bf16[160,1024]{1,0:T(8,128)(2,1)S(1)}, u32[]{:S(2)}, u32[]{:S(2)}) collective-permute-start(bf16[160,1024]{1,0:T(8,128)(2,1)} %param.9), channel_id=1, source_target_pairs={{8,0},{16,8},{24,16},{32,24},{40,32},{48,40},{56,48},{64,56},{72,6... | collective-permute-start | bytes 983048 | tf_op jit(solution)/shard_map/ppermute | solution.py:18
  19.8 30.9 %copy-start.2 = (bf16[160,1024]{1,0:T(8,128)(2,1)S(1)}, bf16[160,1024]{1,0:T(8,128)(2,1)}, u32[]{:S(2)}) copy-start(bf16[160,1024]{1,0:T(8,128)(2,1)} %param.9) | copy-start | bytes 983044
  50.7 2.0 copy-start
  50.7 3.2 copy-start.1
  50.7 225.5 %copy-start.5 = (f32[2048]{0:T(1024)S(1)}, f32[2048]{0:T(1024)}, u32[]{:S(2)}) copy-start(f32[2048]{0:T(1024)} %param.17) | copy-start | bytes 24580
  281.6 7.3 %copy-start.6 = (s32[160]{0:T(256)S(1)}, s32[160]{0:T(256)}, u32[]{:S(2)}) copy-start(s32[160]{0:T(256)} %param.13) | copy-start | bytes 1924
  281.6 7.3 %copy-start.3 = (s32[160,27]{0,1:T(8,128)S(1)}, s32[160,27]{0,1:T(8,128)}, u32[]{:S(2)}) copy-start(s32[160,27]{0,1:T(8,128)} %param.11) | copy-start | bytes 51844
  281.6 7.3 %copy-start.4 = (s32[160,27]{0,1:T(8,128)S(1)}, s32[160,27]{0,1:T(8,128)}, u32[]{:S(2)}) copy-start(s32[160,27]{0,1:T(8,128)} %param.12) | copy-start | bytes 51844
Sparse Core Ops, SparseCore 0:
  289.0 25.9 reduce-scatter.1
where the time goes:
time: 350 us; the launch traced here: 349 us
  blocking collectives  217 us (62%)
  other arithmetic  52.4 us (15%)
  local copies, waits for them, and re-layouts  29.9 us (9%)
  matrix products  25.8 us (7%)
  between operations  13.6 us (4%)
  starting transfers between devices  10.9 us (3%)
    psum x1, blocking collectives, shards(): structure = lax.psum(jnp.stack([real_part, imag_part]), 'pts')  217 us
    another operation x2, other arithmetic  36.2 us
    gather x2, local copies, waits for them, and re-layouts, shards(): gathered = jnp.take(extended, picked, axis=0)  25.4 us
    dot_general x1, matrix products, shards(): jnp.einsum('aoq,okq->ak', gathered, near_blocks, preferred_element_type=j...  17 us
    select_n x2, other arithmetic, shards(): gathered = jnp.take(extended, picked, axis=0)  10.1 us
    ppermute x1, starting transfers between devices, extended_2(): lax.ppermute(lax.slice_in_dim(block, 0, width, axis=dim), axis, backward)  9.36 us
    dot_general x1, matrix products, shards(): lax.dot_general(spread, tables, (((1,), (1,)), ((), ())), preferred_eleme...  7.22 us
  transfers between devices with their start and end apart: 3, of which 0 were waited for; matrix products, arithmetic and copies ran while one was open for 26% of the time, Pallas kernels for 0%

commit v1 on v0

v1 whole, which is shorter than its diff:
```python
import functools
import math

import jax
import jax.numpy as jnp
import numpy as np
from jax import lax
from jax.experimental import pallas as pl
from jax.experimental.pallas import tpu as pltpu
from jax.sharding import Mesh
from jax.sharding import PartitionSpec as P

BAND = 12.0
NODES = (
    0.04830766569, 0.1444719616, 0.2392873623, 0.3318686023, 0.4213512761, 0.5068999089, 0.5877157572, 0.6630442669, 0.7321821187, 0.794483796, 0.8493676137, 0.8963211558, 0.9349060759, 0.9647622556, 0.9856115115, 0.9972638618,
)
EVEN = (
    (0.264161544, 0.235683413, 0.1877892764, 0.1338856267, 0.08565638585, 0.04935936307, 0.02573553405, 0.01220462496, 0.005294905203, 0.00211445586, 0.0007820202318, 0.0002693802975, 8.679038294e-05, 2.6181341e-05, 7.331099629e-06, 1.708479253e-06),
    (0.1702613529, 0.08465650818, -0.04082940747, -0.1469360259, -0.1970030198, -0.1901061112, -0.1489564192, -0.09954602317, -0.05833865755, -0.03055765255, -0.01451635874, -0.006328267813, -0.002555179594, -0.0009609245647, -0.000333851875, -9.333966862e-05),
    (-0.1323973182, -0.02247601982, 0.1047497372, 0.1503633392, 0.08986991162, -0.02455938248, -0.1219371619, -0.1640572477, -0.1545048367, -0.1178161583, -0.07717100148, -0.0448976056, -0.02371842969, -0.01152257368, -0.005081924909, -0.001704677766),
    (-0.1038663831, 0.008772611212, 0.1112611228, 0.09900945939, -0.007887275225, -0.1049440761, -0.1157944762, -0.04697227583, 0.04443730952, 0.108316557, 0.1285622126, 0.1155652092, 0.08749662772, 0.05797221816, 0.03303595529, 0.01312861586),
    (-0.09524794649, 0.02681958951, 0.1142235556, 0.06137473355, -0.06159895528, -0.114537939, -0.05174444256, 0.05425346059, 0.1112188114, 0.08907465173, 0.01933187924, -0.05021028773, -0.08987667008, -0.09410761546, -0.0713193742, -0.03310624913),
    (0.1022051591, -0.05281704117, -0.1277713562, -0.0158252522, 0.116158395, 0.09060969529, -0.0463884297, -0.1239497875, -0.06822339825, 0.04641750905, 0.1115635062, 0.08861974282, 0.01440006111, -0.05133346873, -0.07076867034, -0.04114204128),
    (-0.1016349432, 0.081731359, 0.1180899649, -0.05213972209, -0.1310463958, 0.004828729775, 0.1285200703, 0.06026154641, -0.08513107212, -0.1134175056, -0.009982527353, 0.09053034847, 0.0894231339, 0.01200695961, -0.051135621, -0.04311496388),
    (-0.09691907606, 0.1086033655, 0.08463923718, -0.1138806091, -0.07938954229, 0.1091864505, 0.0866221684, -0.08980194788, -0.1037585862, 0.04854215716, 0.1134990489, 0.01271606801, -0.08781269714, -0.0609974537, 0.02562700126, 0.04324151356),
    (-0.08972912127, 0.1300425509, 0.03237330507, -0.1418919531, 0.02055363161, 0.132001602, -0.05367707241, -0.1161966312, 0.06348478865, 0.1052884638, -0.05273929295, -0.09804759123, 0.02676341234, 0.0825150306, 0.001318540609, -0.04206423821),
    (-0.0807528844, 0.1433856071, -0.02927536699, -0.1203274859, 0.113532529, 0.04297640002, -0.1359071454, 0.03217281435, 0.1131044363, -0.07497313561, -0.07767707065, 0.08565207726, 0.04832778656, -0.07373331536, -0.0262794175, 0.03977430954),
)
ODD = (
    (-0.06039643671, -0.1619285065, -0.2157655924, -0.2164663713, -0.179285157, -0.1273735765, -0.07932182359, -0.04395383706, -0.0219317145, -0.009956138688, -0.004149848215, -0.001600910605, -0.0005751981407, -0.0001930716936, -6.006259695e-05, -1.532579998e-05),
    (0.06770405989, 0.1570721263, 0.1434280287, 0.04295191184, -0.07879962265, -0.1610074452, -0.1820744199, -0.1564850599, -0.1117106857, -0.06911197019, -0.03803899989, -0.018976138, -0.008700246907, -0.003698004317, -0.001443221181, -0.0004421770918),
    (-0.06672308627, -0.1353009509, -0.07559650806, 0.05145652305, 0.1328476776, 0.1110923906, 0.01620622731, -0.08318512773, -0.1393111579, -0.1451173835, -0.1191406959, -0.08344766078, -0.05189716398, -0.02921471538, -0.01463357191, -0.005358686102),
    (-0.06188570509, -0.1120544487, -0.03164468805, 0.08318098917, 0.1076065769, 0.02554639647, -0.07633334629, -0.1130798134, -0.07076087078, 0.008202589998, 0.07547632887, 0.1077871043, 0.1068753005, 0.08546497618, 0.0555295236, 0.02380489812),
    (0.07294621453, 0.1170272587, 0.0005822684711, -0.1151664239, -0.08239886349, 0.04808258285, 0.1205972232, 0.06802484515, -0.04264531193, -0.1109041826, -0.09690224579, -0.0289313287, 0.0417153054, 0.07952536804, 0.07530043037, 0.03856509779),
    (0.08652145766, 0.1159240548, -0.04433348034, -0.1318825677, -0.0146605442, 0.1210590442, 0.0842447592, -0.05956973628, -0.1239316034, -0.0494564638, 0.06563154857, 0.1089604688, 0.06071412772, -0.01917666675, -0.06207287706, -0.04244003862),
    (0.09796928773, 0.1014768063, -0.091850156, -0.1080980874, 0.07605361357, 0.1198048209, -0.04229231028, -0.1286411677, -0.01461539232, 0.1112662457, 0.07892093947, -0.04457606115, -0.09810478366, -0.03937820657, 0.03879814661, 0.04335854939),
    (0.1083285032, 0.07708721735, -0.1285703026, -0.0450395491, 0.1354076647, 0.02413735124, -0.1328629117, -0.02187888439, 0.1235455303, 0.03873152733, -0.1025408614, -0.0647085451, 0.06221363399, 0.07559191195, -0.01210690766, -0.04280157103),
    (0.1177268554, 0.04504968521, -0.1441555522, 0.03839419971, 0.1212170689, -0.09675550887, -0.07572314606, 0.120135559, 0.03631601591, -0.1190390193, -0.01579049946, 0.1052262271, 0.01219152635, -0.08172301286, -0.01423910674, 0.04104943366),
    (0.126120285, 0.007979130802, -0.1328480522, 0.1116338241, 0.03421605314, -0.1374354291, 0.07279981158, 0.07996744654, -0.1205095327, -0.004441967651, 0.111290914, -0.04516234118, -0.07618300914, 0.05955705328, 0.03710370067, -0.03825468552),
)
EVEN_GAIN = (
    0.7236012542, -0.7236000597, 0.7230899637, -0.6794753044, 0.309908605, -0.04203461377, 0.003110230195, -0.0001597812355, 6.121678833e-06, -1.82449892e-07,
)
ODD_GAIN = (
    0.7236012257, -0.7235710907, 0.7176666509, -0.5402161025, 0.127514432, -0.01205222733, 0.0007337517912, -3.234542573e-05, 1.088270167e-06, -2.894614862e-08,
)
RANK = 10
TURN = 1.0 / (2.0 * math.pi)
SIN_COEFS = (
    6.283182818550517, -41.3414213986335, 81.59618387150637,
    -76.58010050946145, 41.20539479011024, -12.271262230884131,
)
COS_COEFS = (
    0.9999999891722597, -19.739204532088525, 64.93911898360994, -85.45016554540021,
    60.167831693053074, -25.96831316496443, 6.52961023180932,
)
MODE_TILE = 512
CLASS_TILE = 9
VMEM_LIMIT = 48 * 1024 * 1024
NT = (((1,), (1,)), ((), ()))
NN = (((1,), (0,)), ((), ()))


def horner(coefs, square):
    total = jnp.full_like(square, coefs[-1])
    for coef in coefs[-2::-1]:
        total = total * square + coef
    return total


def cos_sin(turns):
    rest = turns - jnp.round(turns)
    square = rest * rest
    return horner(COS_COEFS, square), rest * horner(SIN_COEFS, square)


def dot(a, b, dims=NN):
    return lax.dot_general(a, b, dims, preferred_element_type=jnp.float32)


def dot_wide(a, b):
    return lax.dot_general(
        a, b, NN, precision=lax.Precision.HIGHEST, preferred_element_type=jnp.float32
    )


def split(value):
    high = value.astype(jnp.bfloat16)
    return high, (value - high.astype(jnp.float32)).astype(jnp.bfloat16)


def dot_split(a, b, dims=NN):
    return dot(a[0], b[0], dims) + (dot(a[0], b[1], dims) + dot(a[1], b[0], dims))


def outer_rows(left, right):
    rows = [left[:8] * right[i : i + 1] for i in range(RANK)]
    rows += [left[i : i + 1] * right[:8] for i in range(8, RANK)]
    return jnp.concatenate(rows, axis=0)


def factors(first, second, nodes, even, odd):
    width = first.shape[1]
    cos_part, sin_part = cos_sin(nodes * jnp.concatenate([first, second], axis=1))
    evens = dot_wide(even, cos_part)
    odds = dot_wide(odd, sin_part)
    return evens[:, :width], odds[:, :width], evens[:, width:], odds[:, width:]


def as_column(row):
    count = row.shape[1]
    here = lax.broadcasted_iota(jnp.int32, (count, count), 0)
    there = lax.broadcasted_iota(jnp.int32, (count, count), 1)
    return jnp.sum(jnp.where(here == there, row, 0.0), axis=1, keepdims=True)


def structure_kernel(
    density, centers, points, waves, nodes, even_x, odd_x, even_k, odd_k,
    partial, cos_out, sin_out, wave_c_high, wave_c_low, wave_s_high, wave_s_low,
    point_c_high, point_c_low, point_s_high, point_s_low,
    form_c_high, form_c_low, form_s_high, form_s_low, center_x, center_y,
):
    @pl.when(pl.program_id(0) == 0)
    def prepare():
        evx, odx, evy, ody = factors(
            points[0:1, :] * (2.0 * BAND * TURN), points[1:2, :] * (2.0 * BAND * TURN),
            nodes[...], even_x[...], odd_x[...],
        )
        cos_rows = split(jnp.concatenate([outer_rows(evx, evy), -outer_rows(odx, ody)], axis=0))
        sin_rows = split(jnp.concatenate([outer_rows(odx, evy), outer_rows(evx, ody)], axis=0))
        point_c_high[...], point_c_low[...] = cos_rows
        point_s_high[...], point_s_low[...] = sin_rows
        dens = density[...]
        form_c_high[...], form_c_low[...] = split(
            dot(dens, cos_rows[0], NT) + dot(dens, cos_rows[1], NT)
        )
        form_s_high[...], form_s_low[...] = split(
            dot(dens, sin_rows[0], NT) + dot(dens, sin_rows[1], NT)
        )
        center_x[...] = as_column(centers[0:1, :])
        center_y[...] = as_column(centers[1:2, :])

    kx = waves[0:1, :] * TURN
    ky = waves[1:2, :] * TURN
    evx, odx, evy, ody = factors(
        kx * (BAND / 24.0), ky * (BAND / 24.0), nodes[...], even_k[...], odd_k[...]
    )
    cos_rows = split(jnp.concatenate([outer_rows(evx, evy), outer_rows(odx, ody)], axis=0))
    sin_rows = split(jnp.concatenate([outer_rows(odx, evy), outer_rows(evx, ody)], axis=0))
    wave_c_high[...], wave_c_low[...] = cos_rows
    wave_s_high[...], wave_s_low[...] = sin_rows
    cos_c, sin_c = cos_sin(center_x[...] * kx + center_y[...] * ky)
    cos_out[...] = cos_c
    sin_out[...] = sin_c
    form_cos = dot_split((form_c_high[...], form_c_low[...]), cos_rows)
    form_sin = dot_split((form_s_high[...], form_s_low[...]), sin_rows)
    partial[0:1, :] = jnp.sum(cos_c * form_cos - sin_c * form_sin, axis=0, keepdims=True)
    partial[1:2, :] = -jnp.sum(sin_c * form_cos + cos_c * form_sin, axis=0, keepdims=True)


def partial_structure(density, centers, points, waves):
    atoms, count = density.shape
    modes = waves.shape[1]
    rows = 2 * (8 * RANK + 8 * (RANK - 8))
    tile = min(MODE_TILE, modes)
    nodes = np.array(NODES, np.float32)[:, None]
    pad = ((0, 16 - RANK), (0, 0))
    even = np.pad(np.array(EVEN), pad).astype(np.float32)
    odd = np.pad(np.array(ODD), pad).astype(np.float32)
    even_k = np.pad(np.array(EVEN) / np.array(EVEN_GAIN)[:, None], pad).astype(np.float32)
    odd_k = np.pad(np.array(ODD) / np.array(ODD_GAIN)[:, None], pad).astype(np.float32)
    whole = lambda shape: pl.BlockSpec(shape, lambda i: (0, 0))
    tiled = lambda height: pl.BlockSpec((height, tile), lambda i: (0, i))
    bf16 = jnp.bfloat16
    out = lambda shape, kind: jax.ShapeDtypeStruct(shape, kind)
    return pl.pallas_call(
        structure_kernel,
        grid=(modes // tile,),
        in_specs=[
            whole((atoms, count)), whole((2, atoms)), whole((2, count)), tiled(2),
            whole((16, 1)), whole((16, 16)), whole((16, 16)), whole((16, 16)), whole((16, 16)),
        ],
        out_specs=[tiled(2), tiled(atoms), tiled(atoms)] + [tiled(rows)] * 4
        + [whole((rows, count))] * 4,
        out_shape=[out((2, modes), jnp.float32)] + [out((atoms, modes), jnp.float32)] * 2
        + [out((rows, modes), bf16)] * 4 + [out((rows, count), bf16)] * 4,
        scratch_shapes=[pltpu.VMEM((atoms, rows), bf16)] * 4
        + [pltpu.VMEM((atoms, 1), jnp.float32)] * 2,
        compiler_params=pltpu.CompilerParams(vmem_limit_bytes=VMEM_LIMIT),
        cost_estimate=pl.CostEstimate(
            flops=2 * atoms * rows * (count * 4 + modes * 6),
            bytes_accessed=8 * atoms * modes, transcendentals=0,
        ),
    )(density, centers, points, waves, nodes, even, odd, even_k, odd_k)


def far_kernel(
    place, first, second, weight, cos_c, sin_c,
    wave_c_high, wave_c_low, wave_s_high, wave_s_low,
    point_c_high, point_c_low, point_s_high, point_s_low,
    keep, send, held_c, held_s, field,
):
    step = pl.program_id(0)
    scaled = weight[...]
    real = (first[0:1, :] + second[0:1, :]) * scaled
    imag = (first[1:2, :] + second[1:2, :]) * scaled
    cosine, sine = cos_c[...], sin_c[...]
    spread_c = split(real * cosine - imag * sine)
    spread_s = split(-(real * sine + imag * cosine))
    part_c = dot_split(spread_c, (wave_c_high[...], wave_c_low[...]), NT)
    part_s = dot_split(spread_s, (wave_s_high[...], wave_s_low[...]), NT)

    @pl.when(step == 0)
    def begin():
        held_c[...] = part_c
        held_s[...] = part_s

    @pl.when(step > 0)
    def add():
        held_c[...] += part_c
        held_s[...] += part_s

    @pl.when(step == pl.num_programs(0) - 1)
    def finish():
        field[...] = dot_split(
            split(held_c[...]), (point_c_high[...], point_c_low[...])
        ) + dot_split(split(held_s[...]), (point_s_high[...], point_s_low[...]))
        chip, core = place[0], place[1]
        chips, _, width = keep.shape
        for ahead in range(chips):
            other = lax.rem(chip + ahead, chips)
            mine = pl.multiple_of((2 * other + core) * width, width)
            theirs = pl.multiple_of((2 * other + 1 - core) * width, width)
            keep[ahead] = field[:, pl.ds(mine, width)]
            send[ahead] = field[:, pl.ds(theirs, width)]


def far_partial(place, first, second, weight, cos_c, sin_c, waves, points, chips):
    atoms, modes = cos_c.shape
    rows, count = points[0].shape
    tile = min(MODE_TILE, modes)
    width = count // (2 * chips)
    whole = lambda shape: pl.BlockSpec(shape, lambda i, s: (0, 0))
    tiled = lambda height: pl.BlockSpec((height, tile), lambda i, s: (0, i))
    blocks = pl.BlockSpec((chips, atoms, width), lambda i, s: (0, 0, 0))
    return pl.pallas_call(
        far_kernel,
        grid_spec=pltpu.PrefetchScalarGridSpec(
            num_scalar_prefetch=1,
            grid=(modes // tile,),
            in_specs=[tiled(2), tiled(2), tiled(1), tiled(atoms), tiled(atoms)]
            + [tiled(rows)] * 4 + [whole((rows, count))] * 4,
            out_specs=[blocks, blocks],
            scratch_shapes=[pltpu.VMEM((atoms, rows), jnp.float32)] * 2
            + [pltpu.VMEM((atoms, count), jnp.float32)],
        ),
        out_shape=[jax.ShapeDtypeStruct((chips, atoms, width), jnp.float32)] * 2,
        compiler_params=pltpu.CompilerParams(vmem_limit_bytes=VMEM_LIMIT),
        cost_estimate=pl.CostEstimate(
            flops=2 * atoms * rows * 6 * (count + modes),
            bytes_accessed=8 * atoms * modes, transcendentals=0,
        ),
    )(place, first, second, weight, cos_c, sin_c, *waves, *points)


def near_kernel(bases, offsets, places, near, *rest):
    sources, (out, total) = rest[:-2], rest[-2:]
    step = pl.program_id(0)
    classes, width, count = near.shape
    dens = [source[...] for source in sources]
    if len(dens) > 1:
        dens = jnp.concatenate(dens, axis=0)
    else:
        dens = dens[0]
    made = dot(dens, near[...].reshape(classes * width, count), NT)
    atoms = offsets.shape[0]
    here = dens.shape[0] // len(sources)
    column = lax.broadcasted_iota(jnp.int32, (atoms, dens.shape[0]), 1)
    base = jnp.where(column < here, bases[0], bases[len(sources) - 1] - here * (len(sources) - 1))
    target = (column + base).astype(jnp.float32)
    of_slot = offsets[...]
    place_of_slot = places[...]
    result = jnp.zeros((atoms, 2 * width), jnp.float32)
    for one in range(classes):
        hit = of_slot == step * classes + one
        found = jnp.sum(jnp.where(hit, place_of_slot, 0.0), axis=1, keepdims=True)
        chosen = jnp.where(found == target, 1.0, 0.0).astype(jnp.bfloat16)
        value = jnp.concatenate(split(made[:, one * width : (one + 1) * width]), axis=1)
        result = result + dot(chosen, value)
    result = result[:, :width] + result[:, width:]

    @pl.when(step == 0)
    def begin():
        total[...] = result

    @pl.when(step > 0)
    def add():
        total[...] += result

    @pl.when(step == pl.num_programs(0) - 1)
    def finish():
        out[...] = total[...]


def near_part(bases, offsets, places, near, sources):
    atoms, slots = offsets.shape
    classes, width, count = near.shape
    group = CLASS_TILE if classes % CLASS_TILE == 0 else 1
    whole = lambda shape: pl.BlockSpec(shape, lambda i, s: (0, 0))
    rows = atoms * len(sources)
    return pl.pallas_call(
        near_kernel,
        grid_spec=pltpu.PrefetchScalarGridSpec(
            num_scalar_prefetch=1,
            grid=(classes // group,),
            in_specs=[
                whole((atoms, slots)), whole((atoms, slots)),
                pl.BlockSpec((group, width, count), lambda i, s: (i, 0, 0)),
            ] + [whole((atoms, count))] * len(sources),
            out_specs=whole((atoms, width)),
            scratch_shapes=[pltpu.VMEM((atoms, width), jnp.float32)],
        ),
        out_shape=jax.ShapeDtypeStruct((atoms, width), jnp.float32),
        compiler_params=pltpu.CompilerParams(vmem_limit_bytes=VMEM_LIMIT),
        cost_estimate=pl.CostEstimate(
            flops=2 * rows * classes * width * (count + 2 * atoms),
            bytes_accessed=2 * classes * width * count, transcendentals=0,
        ),
    )(bases, offsets, places, near, *sources)


def fold_kernel(keep, taken, *outs):
    for ahead, out in enumerate(outs):
        out[...] = keep[ahead] + taken[ahead]


def fold(keep, taken):
    chips, atoms, width = keep.shape
    return pl.pallas_call(
        fold_kernel,
        out_shape=[jax.ShapeDtypeStruct((atoms, width), jnp.float32)] * chips,
        compiler_params=pltpu.CompilerParams(vmem_limit_bytes=VMEM_LIMIT),
    )(keep, taken)


def shifted(value, axis, by):
    count = lax.axis_size(axis)
    return lax.ppermute(value, axis, [(i, (i + by) % count) for i in range(count)])


def sum_over(value, axis):
    count = lax.axis_size(axis)
    return value + sum(shifted(value, axis, by) for by in range(1, count))


BLOCK_AXES = ("x", "z_hi", "y")


def shards(
    density, near_blocks, neighbour_atoms, neighbour_offsets, neighbour_counts,
    centers, local_points, wavevectors, spectral_weight,
):
    atoms, points = density.shape
    blocks = lax.axis_size(BLOCK_AXES)
    modes = wavevectors.shape[1]
    chips, cores = lax.axis_size("z_lo"), lax.axis_size("core")
    core, chip, block = lax.axis_index("core"), lax.axis_index("z_lo"), lax.axis_index(BLOCK_AXES)
    width = points // (chips * cores)
    normalizer = 1.0 / math.sqrt(atoms * blocks * points * modes * chips * cores)

    halo_route = []
    for source in range(blocks):
        halo_route.append((2 * source, 2 * ((source + 1) % blocks)))
        halo_route.append((2 * source + 1, 2 * ((source - 1) % blocks) + 1))
    halo = lax.ppermute(density, BLOCK_AXES + ("core",), halo_route)

    partial, cos_c, sin_c, *tables = partial_structure(density, centers, local_points, wavevectors)

    total_atoms = atoms * blocks
    places = (neighbour_atoms - (block - 1) * atoms + total_atoms) % total_atoms
    live = jnp.arange(neighbour_atoms.shape[1])[None, :] < neighbour_counts[:, None]
    places = jnp.where(live, places, -1).astype(jnp.float32)
    places = places + 1.0
    one = jnp.ones((1,), jnp.int32)
    near_own = near_part(one * (atoms + 1), neighbour_offsets, places, near_blocks, [density])

    structure = sum_over(partial, "y")
    structure = sum_over(structure, "x")
    other_half = shifted(structure, "z_hi", 1)

    halo_other = lax.ppermute(halo, "core", [(0, 1), (1, 0)])
    low, high = 1, 2 * atoms + 1
    bases = jnp.stack([jnp.where(core == 0, low, high), jnp.where(core == 0, high, low)])
    near_halo = near_part(
        bases.astype(jnp.int32), neighbour_offsets, places, near_blocks, [halo, halo_other]
    )

    weight = (spectral_weight * normalizer)[None, :]
    place = jnp.stack([chip, core]).astype(jnp.int32)
    keep, send = far_partial(
        place, structure, other_half, weight, cos_c, sin_c, tables[:4], tables[4:], chips
    )
    taken = lax.ppermute(send, "core", [(0, 1), (1, 0)])
    pieces = fold(keep, taken)
    far_field = pieces[0]
    for by in range(1, chips):
        far_field = far_field + shifted(pieces[by], "z_lo", by)
    member = chip * cores + core
    own = lax.dynamic_slice_in_dim(density, member * width, width, 1).astype(jnp.float32)
    return 0.5 * own + near_own + near_halo + far_field


def solution(mesh):
    fine = Mesh(
        mesh.devices.reshape(4, 2, 4, 4, 2), ("x", "z_hi", "y", "z_lo", "core")
    )
    modes = ("z_lo", "core")
    placed = (
        P(BLOCK_AXES, None), P(None, modes, None), P(BLOCK_AXES, None), P(BLOCK_AXES, None),
        P(BLOCK_AXES), P(None, BLOCK_AXES), P(), P(None, modes), P(modes),
    )
    return jax.shard_map(
        shards, mesh=fine, in_specs=placed, out_specs=P(BLOCK_AXES, modes), check_vma=False
    )
```

time: 350 us -> 78.3 us (0.22)
  the two profiles are of different devices: /device:TPU:32 before, /device:TPU:24 now
where the time goes in v1:
time: 78.3 us; the launch traced here: 77.3 us
  starting transfers between devices  26.9 us (34%)
  Pallas kernels  25.2 us (32%)
  local copies, waits for them, and re-layouts  15.1 us (19%)
  other arithmetic  5.54 us (7%)
  waiting for transfers between devices  4.42 us (6%)
    ppermute x10, starting transfers between devices, shifted(): lax.ppermute(value, axis, [(i, (i + by) % count) for i in range(count)])  16.4 us
    unnamed x46, local copies, waits for them, and re-layouts  15.1 us
    pallas_call x2, Pallas kernels, near_part(): pl.pallas_call(near_kernel, grid_spec=pltpu.PrefetchScalarGridSpec(num_sc...  13.1 us
    ppermute x1, starting transfers between devices, shards(): halo = lax.ppermute(density, BLOCK_AXES + ('core',), halo_route)  9.86 us
    pallas_call x1, Pallas kernels, partial_structure(): pl.pallas_call(structure_kernel, grid=(modes // tile,), in_specs=[whole((...  6.84 us
    pallas_call x1, Pallas kernels, far_partial(): pl.pallas_call(far_kernel, grid_spec=pltpu.PrefetchScalarGridSpec(num_sca...  5.25 us
    ppermute x10, waiting for transfers between devices, shifted(): lax.ppermute(value, axis, [(i, (i + by) % count) for i in range(count)])  4.41 us
    add x2, other arithmetic, sum_over(): return value + sum((shifted(value, axis, by) for by in range(1, count)))  2.16 us
  transfers between devices with their start and end apart: 13, of which 3 were waited for; matrix products, arithmetic and copies ran while one was open for 9% of the time, Pallas kernels for 24%

profile of v1, /device:TPU:24, one launch (start us, length us, event | category | flops | bytes accessed | tf_op | source)
XLA Modules:
  0.0 77.3 jit_solution(4985459474810925965)
XLA Ops:
  5.6 6.8 %shard_map.138 = (f32[2,2048]{1,0:T(2,128)S(1)}, f32[160,2048]{1,0:T(8,128)}, f32[160,2048]{1,0:T(8,128)}, bf16[192,2048]{1,0:T(8,128)(2,1)S(1)}, bf16[192,2048]...) custom-call(bf16[160,1024]{1,0:T(8,128)(2,1)} %density.1, ...), custom_call_target="tpu_custom_call" | custom-call | flops 1006632960 | bytes 2621440 | tf_op jit(solution)/shard_map/pallas_call | solution.py:176
  14.6 2.0 %collective-permute-start.2 = (f32[2,2048]{1,0:T(2,128)S(1)}, f32[2,2048]{1,0:T(2,128)}, u32[]{:S(2)}, u32[]{:S(2)}) collective-permute-start(f32[2,2048]{1,0:T(2,128)S(1)} %get-tuple-element.22), channel_id=1, source_target_pairs={{0,8},{8,16},{16,24},{24,0},{1,9},{9,17},{17,25},{25,1},{2,10},{10... | collective-permute-start | bytes 49160 | tf_op jit(solution)/shard_map/ppermute | solution.py:348
  16.6 0.8 %collective-permute-start.3 = (f32[2,2048]{1,0:T(2,128)S(1)}, f32[2,2048]{1,0:T(2,128)}, u32[]{:S(2)}, u32[]{:S(2)}) collective-permute-start(f32[2,2048]{1,0:T(2,128)S(1)} %get-tuple-element.22), channel_id=1, source_target_pairs={{0,16},{8,24},{16,0},{24,8},{1,17},{9,25},{17,1},{25,9},{2,18},{10... | collective-permute-start | bytes 49160 | tf_op jit(solution)/shard_map/ppermute | solution.py:348
  17.5 9.9 %collective-permute-start = (bf16[160,1024]{1,0:T(8,128)(2,1)}, bf16[160,1024]{1,0:T(8,128)(2,1)}, u32[]{:S(2)}, u32[]{:S(2)}) collective-permute-start(bf16[160,1024]{1,0:T(8,128)(2,1)} %density.1), channel_id=1, source_target_pairs={{0,8},{1,249},{8,16},{9,1},{16,24},{17,9},{24,32},{25,17},{32,40},... | collective-permute-start | bytes 983048 | tf_op jit(solution)/shard_map/ppermute | solution.py:375
  27.9 1.4 %add_add_fusion.2 = f32[2,2048]{1,0:T(2,128)} fusion(f32[2,2048]{1,0:T(2,128)S(1)} %get-tuple-element.22, f32[2,2048]{1,0:T(2,128)} %collective-permute-done.4, f32[2,2048]{1,0:T(2,128)} %collective-permute-done.2, f32[2,2048]{1,0:T(2,128)} %collective-permute-done.3), kind=kLoop, calls=%fused_computation.8 | loop fusion | flops 12288 | bytes 81920 | tf_op jit(solution)/shard_map/add | solution.py:353
  29.3 1.5 %collective-permute-start.5 = (f32[2,2048]{1,0:T(2,128)}, f32[2,2048]{1,0:T(2,128)S(1)}, u32[]{:S(2)}, u32[]{:S(2)}) collective-permute-start(f32[2,2048]{1,0:T(2,128)} %add_add_fusion.2), channel_id=1, source_target_pairs={{0,64},{64,128},{128,192},{192,0},{1,65},{65,129},{129,193},{193,1... | collective-permute-start | bytes 49160 | tf_op jit(solution)/shard_map/ppermute | solution.py:348
  30.8 2.7 %collective-permute-start.6 = (f32[2,2048]{1,0:T(2,128)}, f32[2,2048]{1,0:T(2,128)}, u32[]{:S(2)}, u32[]{:S(2)}) collective-permute-start(f32[2,2048]{1,0:T(2,128)} %add_add_fusion.2), channel_id=1, source_target_pairs={{0,128},{64,192},{128,0},{192,64},{1,129},{65,193},{129,1},{193,65... | collective-permute-start | bytes 49160 | tf_op jit(solution)/shard_map/ppermute | solution.py:348
  33.5 1.4 %collective-permute-start.7 = (f32[2,2048]{1,0:T(2,128)}, f32[2,2048]{1,0:T(2,128)}, u32[]{:S(2)}, u32[]{:S(2)}) collective-permute-start(f32[2,2048]{1,0:T(2,128)} %add_add_fusion.2), channel_id=1, source_target_pairs={{0,192},{64,0},{128,64},{192,128},{1,193},{65,1},{129,65},{193,129... | collective-permute-start | bytes 49160 | tf_op jit(solution)/shard_map/ppermute | solution.py:348
  36.4 1.2 %collective-permute-done.7 = f32[2,2048]{1,0:T(2,128)} collective-permute-done((f32[2,2048]{1,0:T(2,128)}, f32[2,2048]{1,0:T(2,128)}, u32[]{:S(2)}, u32[]{:S(2)}) %collective-permute-start.7) | collective-permute-done | bytes 16416 | tf_op jit(solution)/shard_map/ppermute | solution.py:348
  37.6 0.8 %add_add_fusion.1.first = f32[2,2048]{1,0:T(2,128)S(1)} fusion(f32[2,2048]{1,0:T(2,128)} %add_add_fusion.2, f32[2,2048]{1,0:T(2,128)} %collective-permute-done.7, f32[2,2048]{1,0:T(2,128)} %copy-done.19, f32[2,2048]{1,0:T(2,128)} %collective-permute-done.6), kind=kLoop, calls=%fused_computation.7 | loop fusion | flops 12288 | bytes 81920 | tf_op jit(solution)/shard_map/add | solution.py:353
  38.4 1.9 %collective-permute-start.8 = (f32[2,2048]{1,0:T(2,128)S(1)}, f32[2,2048]{1,0:T(2,128)}, u32[]{:S(2)}, u32[]{:S(2)}) collective-permute-start(f32[2,2048]{1,0:T(2,128)S(1)} %add_add_fusion.1.first), channel_id=1, source_target_pairs={{0,32},{32,0},{1,33},{33,1},{2,34},{34,2},{3,35},{35,3},{4,36},{36... | collective-permute-start | bytes 49160 | tf_op jit(solution)/shard_map/ppermute | solution.py:348
  40.8 1.5 %copy.15 = s32[160,27]{1,0:T(8,128)} copy(s32[160,27]{0,1:T(8,128)} %param.16) | data formatting | bytes 34560 | tf_op args[2]
  42.3 1.5 %copy.16.offsets = s32[160,27]{1,0:T(8,128)} copy(s32[160,27]{0,1:T(8,128)} %param.17) | data formatting | bytes 34560 | tf_op args[3]
  43.8 2.4 %collective-permute-done.8.second = f32[2,2048]{1,0:T(2,128)} collective-permute-done((f32[2,2048]{1,0:T(2,128)S(1)}, f32[2,2048]{1,0:T(2,128)}, u32[]{:S(2)}, u32[]{:S(2)}) %collective-permute-start.8) | collective-permute-done | bytes 16416 | tf_op jit(solution)/shard_map/ppermute | solution.py:348
  46.2 1.0 %copy-done.1 = bf16[192,1024]{1,0:T(8,128)(2,1)S(1)} copy-done((bf16[192,1024]{1,0:T(8,128)(2,1)S(1)}, bf16[192,1024]{1,0:T(8,128)(2,1)}, u32[]{:S(2)}) %copy-start.1) | copy-done | bytes 393240
  47.2 1.0 %copy-done.3 = bf16[192,1024]{1,0:T(8,128)(2,1)S(1)} copy-done((bf16[192,1024]{1,0:T(8,128)(2,1)S(1)}, bf16[192,1024]{1,0:T(8,128)(2,1)}, u32[]{:S(2)}) %copy-start.3) | copy-done | bytes 393240
  48.2 1.0 %copy-done.5 = bf16[192,1024]{1,0:T(8,128)(2,1)S(1)} copy-done((bf16[192,1024]{1,0:T(8,128)(2,1)S(1)}, bf16[192,1024]{1,0:T(8,128)(2,1)}, u32[]{:S(2)}) %copy-start.5) | copy-done | bytes 393240
  50.6 5.3 %shard_map.139 = (f32[4,160,128]{2,1,0:T(8,128)S(1)}, f32[4,160,128]{2,1,0:T(8,128)S(1)}) custom-call(s32[2]{0:T(128)S(1)} %copy-done.8, f32[2,2048]{1,0:T(2,128)S(1)} %add_add_fusion.1.first, f32[2,2048]{1,0:T(2,128)} %collective-permute-done.8.second, f32[1,2048]{1,0:T(1,128)S(1)} %bitcast.5, f32[160,2048]{1,0:T(8,128)} %get-tuple-element.23.cos_c, ...), custom_call_target="tpu_custom_call" | custom-call | flops 1132462080 | bytes 2621440 | tf_op jit(solution)/shard_map/pallas_call | solution.py:246
  56.6 5.9 %shard_map.136 = f32[160,128]{1,0:T(8,128)S(1)} custom-call(s32[1]{0:T(128)} %constant.22.clone.1.bases, s32[160,27]{1,0:T(8,128)S(1)} %copy-done.6, f32[160,27]{1,0:T(8,128)S(1)} %fusion.2.places, bf16[27,128,1024]{2,1,0:T(8,128)(2,1)} %near.3, bf16[160,1024]{1,0:T(8,128)(2,1)} %density.1), custom_call_target="tpu_custom_call" | custom-call | flops 1486356480 | bytes 7077888 | tf_op jit(solution)/shard_map/pallas_call | solution.py:311
  62.5 1.1 %collective-permute-start.10 = (f32[160,128]{1,0:T(8,128)S(1)}, f32[160,128]{1,0:T(8,128)S(1)}, u32[]{:S(2)}, u32[]{:S(2)}) collective-permute-start(f32[160,128]{1,0:T(8,128)S(1)} %get-tuple-element.36), channel_id=1, source_target_pairs={{0,2},{2,4},{4,6},{6,0},{1,3},{3,5},{5,7},{7,1},{8,10},{10,12},{12... | collective-permute-start | bytes 245768 | tf_op jit(solution)/shard_map/ppermute | solution.py:348
  63.6 2.2 %collective-permute-start.11 = (f32[160,128]{1,0:T(8,128)S(1)}, f32[160,128]{1,0:T(8,128)S(1)}, u32[]{:S(2)}, u32[]{:S(2)}) collective-permute-start(f32[160,128]{1,0:T(8,128)S(1)} %get-tuple-element.37), channel_id=1, source_target_pairs={{0,4},{2,6},{4,0},{6,2},{1,5},{3,7},{5,1},{7,3},{8,12},{10,14},{12... | collective-permute-start | bytes 245768 | tf_op jit(solution)/shard_map/ppermute | solution.py:348
  65.8 2.8 %collective-permute-start.12 = (f32[160,128]{1,0:T(8,128)S(1)}, f32[160,128]{1,0:T(8,128)S(1)}, u32[]{:S(2)}, u32[]{:S(2)}) collective-permute-start(f32[160,128]{1,0:T(8,128)S(1)} %get-tuple-element.38), channel_id=1, source_target_pairs={{0,6},{2,0},{4,2},{6,4},{1,7},{3,1},{5,3},{7,5},{8,14},{10,8},{12,... | collective-permute-start | bytes 245768 | tf_op jit(solution)/shard_map/ppermute | solution.py:348
  68.6 7.2 %shard_map.137 = f32[160,128]{1,0:T(8,128)S(1)} custom-call(s32[2]{0:T(128)S(1)} %copy-done.12, s32[160,27]{1,0:T(8,128)S(1)} %copy-done.6, f32[160,27]{1,0:T(8,128)S(1)} %fusion.2.places, bf16[27,128,1024]{2,1,0:T(8,128)(2,1)} %near.3, bf16[160,1024]{1,0:T(8,128)(2,1)} %collective-permute-done.rest_0_, bf16[160,1024]{1,0:T(8,128)(2,1)S(1)} %collective-permute-done.1.rest_1_), custom_call_target="tpu_custom_call" | custom-call | flops 2972712960 | bytes 7077888 | tf_op jit(solution)/shard_map/pallas_call | solution.py:311
  75.8 1.5 %add_add_fusion = f32[160,128]{1,0:T(8,128)} fusion(f32[160,128]{1,0:T(8,128)S(1)} %collective-permute-done.12, f32[160,128]{1,0:T(8,128)S(1)} %collective-permute-done.11, f32[160,128]{1,0:T(8,128)S(1)} %get-tuple-element.35, f32[160,128]{1,0:T(8,128)S(1)} %collective-permute-done.10, f32[160,128]{1,0:T(8,128)S(1)} %shard_map.137, ...), kind=kLoop, calls=%fused_computation.4 | loop fusion | flops 163840 | bytes 614404 | tf_op jit(solution)/shard_map/add | solution.py:410
  (60 shorter events, 12.5 us)
Async XLA Ops:
  5.6 21.7 %copy-start.20 = (f32[2048]{0:T(1024)S(1)}, f32[2048]{0:T(1024)}, u32[]{:S(2)}) copy-start(f32[2048]{0:T(1024)} %param.22) | copy-start | bytes 24580
  12.4 0.7 copy-start
  13.9 0.7 copy-start.4
  14.6 13.3 %collective-permute-start.2 = (f32[2,2048]{1,0:T(2,128)S(1)}, f32[2,2048]{1,0:T(2,128)}, u32[]{:S(2)}, u32[]{:S(2)}) collective-permute-start(f32[2,2048]{1,0:T(2,128)S(1)} %get-tuple-element.22), channel_id=1, source_target_pairs={{0,8},{8,16},{16,24},{24,0},{1,9},{9,17},{17,25},{25,1},{2,10},{10... | collective-permute-start | bytes 49160 | tf_op jit(solution)/shard_map/ppermute | solution.py:348
  16.6 11.3 %collective-permute-start.3 = (f32[2,2048]{1,0:T(2,128)S(1)}, f32[2,2048]{1,0:T(2,128)}, u32[]{:S(2)}, u32[]{:S(2)}) collective-permute-start(f32[2,2048]{1,0:T(2,128)S(1)} %get-tuple-element.22), channel_id=1, source_target_pairs={{0,16},{8,24},{16,0},{24,8},{1,17},{9,25},{17,1},{25,9},{2,18},{10... | collective-permute-start | bytes 49160 | tf_op jit(solution)/shard_map/ppermute | solution.py:348
  17.5 10.5 %collective-permute-start.4 = (f32[2,2048]{1,0:T(2,128)S(1)}, f32[2,2048]{1,0:T(2,128)}, u32[]{:S(2)}, u32[]{:S(2)}) collective-permute-start(f32[2,2048]{1,0:T(2,128)S(1)} %get-tuple-element.22), channel_id=1, source_target_pairs={{0,24},{8,0},{16,8},{24,16},{1,25},{9,1},{17,9},{25,17},{2,26},{10... | collective-permute-start | bytes 49160 | tf_op jit(solution)/shard_map/ppermute | solution.py:348
  17.5 38.5 %collective-permute-start = (bf16[160,1024]{1,0:T(8,128)(2,1)}, bf16[160,1024]{1,0:T(8,128)(2,1)}, u32[]{:S(2)}, u32[]{:S(2)}) collective-permute-start(bf16[160,1024]{1,0:T(8,128)(2,1)} %density.1), channel_id=1, source_target_pairs={{0,8},{1,249},{8,16},{9,1},{16,24},{17,9},{24,32},{25,17},{32,40},... | collective-permute-start | bytes 983048 | tf_op jit(solution)/shard_map/ppermute | solution.py:375
  29.3 6.3 %collective-permute-start.5 = (f32[2,2048]{1,0:T(2,128)}, f32[2,2048]{1,0:T(2,128)S(1)}, u32[]{:S(2)}, u32[]{:S(2)}) collective-permute-start(f32[2,2048]{1,0:T(2,128)} %add_add_fusion.2), channel_id=1, source_target_pairs={{0,64},{64,128},{128,192},{192,0},{1,65},{65,129},{129,193},{193,1... | collective-permute-start | bytes 49160 | tf_op jit(solution)/shard_map/ppermute | solution.py:348
  30.8 5.6 %collective-permute-start.6 = (f32[2,2048]{1,0:T(2,128)}, f32[2,2048]{1,0:T(2,128)}, u32[]{:S(2)}, u32[]{:S(2)}) collective-permute-start(f32[2,2048]{1,0:T(2,128)} %add_add_fusion.2), channel_id=1, source_target_pairs={{0,128},{64,192},{128,0},{192,64},{1,129},{65,193},{129,1},{193,65... | collective-permute-start | bytes 49160 | tf_op jit(solution)/shard_map/ppermute | solution.py:348
  33.5 4.1 %collective-permute-start.7 = (f32[2,2048]{1,0:T(2,128)}, f32[2,2048]{1,0:T(2,128)}, u32[]{:S(2)}, u32[]{:S(2)}) collective-permute-start(f32[2,2048]{1,0:T(2,128)} %add_add_fusion.2), channel_id=1, source_target_pairs={{0,192},{64,0},{128,64},{192,128},{1,193},{65,1},{129,65},{193,129... | collective-permute-start | bytes 49160 | tf_op jit(solution)/shard_map/ppermute | solution.py:348
  35.6 0.7 copy-start.19
  38.4 7.8 %collective-permute-start.8 = (f32[2,2048]{1,0:T(2,128)S(1)}, f32[2,2048]{1,0:T(2,128)}, u32[]{:S(2)}, u32[]{:S(2)}) collective-permute-start(f32[2,2048]{1,0:T(2,128)S(1)} %add_add_fusion.1.first), channel_id=1, source_target_pairs={{0,32},{32,0},{1,33},{33,1},{2,34},{34,2},{3,35},{35,3},{4,36},{36... | collective-permute-start | bytes 49160 | tf_op jit(solution)/shard_map/ppermute | solution.py:348
  46.2 1.0 %copy-start.1 = (bf16[192,1024]{1,0:T(8,128)(2,1)S(1)}, bf16[192,1024]{1,0:T(8,128)(2,1)}, u32[]{:S(2)}) copy-start(bf16[192,1024]{1,0:T(8,128)(2,1)} %copy-done) | copy-start | bytes 1179652
  47.2 1.0 %copy-start.3 = (bf16[192,1024]{1,0:T(8,128)(2,1)S(1)}, bf16[192,1024]{1,0:T(8,128)(2,1)}, u32[]{:S(2)}) copy-start(bf16[192,1024]{1,0:T(8,128)(2,1)} %copy-done.2) | copy-start | bytes 1179652
  48.2 1.0 %copy-start.5 = (bf16[192,1024]{1,0:T(8,128)(2,1)S(1)}, bf16[192,1024]{1,0:T(8,128)(2,1)}, u32[]{:S(2)}) copy-start(bf16[192,1024]{1,0:T(8,128)(2,1)} %copy-done.4) | copy-start | bytes 1179652
  50.6 5.9 %copy-start.18 = (s32[160,27]{1,0:T(8,128)S(1)}, s32[160,27]{1,0:T(8,128)}, u32[]{:S(2)}) copy-start(s32[160,27]{1,0:T(8,128)} %copy.15) | copy-start | bytes 51844
  50.6 5.9 %copy-start.21 = (s32[160]{0:T(256)S(1)}, s32[160]{0:T(256)}, u32[]{:S(2)}) copy-start(s32[160]{0:T(256)} %param.18) | copy-start | bytes 1924
  50.6 6.0 %copy-start.6 = (s32[160,27]{1,0:T(8,128)S(1)}, s32[160,27]{1,0:T(8,128)}, u32[]{:S(2)}) copy-start(s32[160,27]{1,0:T(8,128)} %copy.16.offsets) | copy-start | bytes 51844
  55.8 6.6 %collective-permute-start.9 = (f32[4,160,128]{2,1,0:T(8,128)S(1)}, f32[4,160,128]{2,1,0:T(8,128)S(1)}, u32[]{:S(2)}, u32[]{:S(2)}) collective-permute-start(f32[4,160,128]{2,1,0:T(8,128)S(1)} %get-tuple-element.34), channel_id=1, source_target_pairs={{0,1},{1,0},{2,3},{3,2},{4,5},{5,4},{6,7},{7,6},{8,9},{9,8},{10,11... | collective-permute-start | bytes 983048 | tf_op jit(solution)/shard_map/ppermute | solution.py:403
  55.9 12.6 %collective-permute-start.1 = (bf16[160,1024]{1,0:T(8,128)(2,1)}, bf16[160,1024]{1,0:T(8,128)(2,1)S(1)}, u32[]{:S(2)}, u32[]{:S(2)}) collective-permute-start(bf16[160,1024]{1,0:T(8,128)(2,1)} %collective-permute-done.rest_0_), channel_id=1, source_target_pairs={{0,1},{1,0},{2,3},{3,2},{4,5},{5,4},{6,7},{7,6},{8,9},{9,8},{10,11... | collective-permute-start | bytes 983048 | tf_op jit(solution)/shard_map/ppermute | solution.py:391
  56.5 12.0 %copy-start.12 = (s32[2]{0:T(128)S(1)}, s32[2]{0:T(128)}, u32[]{:S(2)}) copy-start(s32[2]{0:T(128)} %pad_add_fusion.bases) | copy-start | bytes 28
  62.5 13.3 %collective-permute-start.10 = (f32[160,128]{1,0:T(8,128)S(1)}, f32[160,128]{1,0:T(8,128)S(1)}, u32[]{:S(2)}, u32[]{:S(2)}) collective-permute-start(f32[160,128]{1,0:T(8,128)S(1)} %get-tuple-element.36), channel_id=1, source_target_pairs={{0,2},{2,4},{4,6},{6,0},{1,3},{3,5},{5,7},{7,1},{8,10},{10,12},{12... | collective-permute-start | bytes 245768 | tf_op jit(solution)/shard_map/ppermute | solution.py:348
  63.6 12.2 %collective-permute-start.11 = (f32[160,128]{1,0:T(8,128)S(1)}, f32[160,128]{1,0:T(8,128)S(1)}, u32[]{:S(2)}, u32[]{:S(2)}) collective-permute-start(f32[160,128]{1,0:T(8,128)S(1)} %get-tuple-element.37), channel_id=1, source_target_pairs={{0,4},{2,6},{4,0},{6,2},{1,5},{3,7},{5,1},{7,3},{8,12},{10,14},{12... | collective-permute-start | bytes 245768 | tf_op jit(solution)/shard_map/ppermute | solution.py:348
  65.8 10.1 %collective-permute-start.12 = (f32[160,128]{1,0:T(8,128)S(1)}, f32[160,128]{1,0:T(8,128)S(1)}, u32[]{:S(2)}, u32[]{:S(2)}) collective-permute-start(f32[160,128]{1,0:T(8,128)S(1)} %get-tuple-element.38), channel_id=1, source_target_pairs={{0,6},{2,0},{4,2},{6,4},{1,7},{3,1},{5,3},{7,5},{8,14},{10,8},{12,... | collective-permute-start | bytes 245768 | tf_op jit(solution)/shard_map/ppermute | solution.py:348
  (11 other events, 7.7 us)

commit v2 on v1

v2 whole, which is shorter than its diff:
```python
import functools
import math

import jax
import jax.numpy as jnp
import numpy as np
from jax import lax
from jax.experimental import pallas as pl
from jax.experimental.pallas import tpu as pltpu
from jax.sharding import Mesh
from jax.sharding import PartitionSpec as P

BAND = 12.0
NODES = (
    0.04830766569, 0.1444719616, 0.2392873623, 0.3318686023, 0.4213512761, 0.5068999089, 0.5877157572, 0.6630442669, 0.7321821187, 0.794483796, 0.8493676137, 0.8963211558, 0.9349060759, 0.9647622556, 0.9856115115, 0.9972638618,
)
EVEN = (
    (0.264161544, 0.235683413, 0.1877892764, 0.1338856267, 0.08565638585, 0.04935936307, 0.02573553405, 0.01220462496, 0.005294905203, 0.00211445586, 0.0007820202318, 0.0002693802975, 8.679038294e-05, 2.6181341e-05, 7.331099629e-06, 1.708479253e-06),
    (0.1702613529, 0.08465650818, -0.04082940747, -0.1469360259, -0.1970030198, -0.1901061112, -0.1489564192, -0.09954602317, -0.05833865755, -0.03055765255, -0.01451635874, -0.006328267813, -0.002555179594, -0.0009609245647, -0.000333851875, -9.333966862e-05),
    (-0.1323973182, -0.02247601982, 0.1047497372, 0.1503633392, 0.08986991162, -0.02455938248, -0.1219371619, -0.1640572477, -0.1545048367, -0.1178161583, -0.07717100148, -0.0448976056, -0.02371842969, -0.01152257368, -0.005081924909, -0.001704677766),
    (-0.1038663831, 0.008772611212, 0.1112611228, 0.09900945939, -0.007887275225, -0.1049440761, -0.1157944762, -0.04697227583, 0.04443730952, 0.108316557, 0.1285622126, 0.1155652092, 0.08749662772, 0.05797221816, 0.03303595529, 0.01312861586),
    (-0.09524794649, 0.02681958951, 0.1142235556, 0.06137473355, -0.06159895528, -0.114537939, -0.05174444256, 0.05425346059, 0.1112188114, 0.08907465173, 0.01933187924, -0.05021028773, -0.08987667008, -0.09410761546, -0.0713193742, -0.03310624913),
    (0.1022051591, -0.05281704117, -0.1277713562, -0.0158252522, 0.116158395, 0.09060969529, -0.0463884297, -0.1239497875, -0.06822339825, 0.04641750905, 0.1115635062, 0.08861974282, 0.01440006111, -0.05133346873, -0.07076867034, -0.04114204128),
    (-0.1016349432, 0.081731359, 0.1180899649, -0.05213972209, -0.1310463958, 0.004828729775, 0.1285200703, 0.06026154641, -0.08513107212, -0.1134175056, -0.009982527353, 0.09053034847, 0.0894231339, 0.01200695961, -0.051135621, -0.04311496388),
    (-0.09691907606, 0.1086033655, 0.08463923718, -0.1138806091, -0.07938954229, 0.1091864505, 0.0866221684, -0.08980194788, -0.1037585862, 0.04854215716, 0.1134990489, 0.01271606801, -0.08781269714, -0.0609974537, 0.02562700126, 0.04324151356),
    (-0.08972912127, 0.1300425509, 0.03237330507, -0.1418919531, 0.02055363161, 0.132001602, -0.05367707241, -0.1161966312, 0.06348478865, 0.1052884638, -0.05273929295, -0.09804759123, 0.02676341234, 0.0825150306, 0.001318540609, -0.04206423821),
    (-0.0807528844, 0.1433856071, -0.02927536699, -0.1203274859, 0.113532529, 0.04297640002, -0.1359071454, 0.03217281435, 0.1131044363, -0.07497313561, -0.07767707065, 0.08565207726, 0.04832778656, -0.07373331536, -0.0262794175, 0.03977430954),
)
ODD = (
    (-0.06039643671, -0.1619285065, -0.2157655924, -0.2164663713, -0.179285157, -0.1273735765, -0.07932182359, -0.04395383706, -0.0219317145, -0.009956138688, -0.004149848215, -0.001600910605, -0.0005751981407, -0.0001930716936, -6.006259695e-05, -1.532579998e-05),
    (0.06770405989, 0.1570721263, 0.1434280287, 0.04295191184, -0.07879962265, -0.1610074452, -0.1820744199, -0.1564850599, -0.1117106857, -0.06911197019, -0.03803899989, -0.018976138, -0.008700246907, -0.003698004317, -0.001443221181, -0.0004421770918),
    (-0.06672308627, -0.1353009509, -0.07559650806, 0.05145652305, 0.1328476776, 0.1110923906, 0.01620622731, -0.08318512773, -0.1393111579, -0.1451173835, -0.1191406959, -0.08344766078, -0.05189716398, -0.02921471538, -0.01463357191, -0.005358686102),
    (-0.06188570509, -0.1120544487, -0.03164468805, 0.08318098917, 0.1076065769, 0.02554639647, -0.07633334629, -0.1130798134, -0.07076087078, 0.008202589998, 0.07547632887, 0.1077871043, 0.1068753005, 0.08546497618, 0.0555295236, 0.02380489812),
    (0.07294621453, 0.1170272587, 0.0005822684711, -0.1151664239, -0.08239886349, 0.04808258285, 0.1205972232, 0.06802484515, -0.04264531193, -0.1109041826, -0.09690224579, -0.0289313287, 0.0417153054, 0.07952536804, 0.07530043037, 0.03856509779),
    (0.08652145766, 0.1159240548, -0.04433348034, -0.1318825677, -0.0146605442, 0.1210590442, 0.0842447592, -0.05956973628, -0.1239316034, -0.0494564638, 0.06563154857, 0.1089604688, 0.06071412772, -0.01917666675, -0.06207287706, -0.04244003862),
    (0.09796928773, 0.1014768063, -0.091850156, -0.1080980874, 0.07605361357, 0.1198048209, -0.04229231028, -0.1286411677, -0.01461539232, 0.1112662457, 0.07892093947, -0.04457606115, -0.09810478366, -0.03937820657, 0.03879814661, 0.04335854939),
    (0.1083285032, 0.07708721735, -0.1285703026, -0.0450395491, 0.1354076647, 0.02413735124, -0.1328629117, -0.02187888439, 0.1235455303, 0.03873152733, -0.1025408614, -0.0647085451, 0.06221363399, 0.07559191195, -0.01210690766, -0.04280157103),
    (0.1177268554, 0.04504968521, -0.1441555522, 0.03839419971, 0.1212170689, -0.09675550887, -0.07572314606, 0.120135559, 0.03631601591, -0.1190390193, -0.01579049946, 0.1052262271, 0.01219152635, -0.08172301286, -0.01423910674, 0.04104943366),
    (0.126120285, 0.007979130802, -0.1328480522, 0.1116338241, 0.03421605314, -0.1374354291, 0.07279981158, 0.07996744654, -0.1205095327, -0.004441967651, 0.111290914, -0.04516234118, -0.07618300914, 0.05955705328, 0.03710370067, -0.03825468552),
)
EVEN_GAIN = (
    0.7236012542, -0.7236000597, 0.7230899637, -0.6794753044, 0.309908605, -0.04203461377, 0.003110230195, -0.0001597812355, 6.121678833e-06, -1.82449892e-07,
)
ODD_GAIN = (
    0.7236012257, -0.7235710907, 0.7176666509, -0.5402161025, 0.127514432, -0.01205222733, 0.0007337517912, -3.234542573e-05, 1.088270167e-06, -2.894614862e-08,
)
RANK = 10
TURN = 1.0 / (2.0 * math.pi)
SIN_COEFS = (
    6.283182818550517, -41.3414213986335, 81.59618387150637,
    -76.58010050946145, 41.20539479011024, -12.271262230884131,
)
COS_COEFS = (
    0.9999999891722597, -19.739204532088525, 64.93911898360994, -85.45016554540021,
    60.167831693053074, -25.96831316496443, 6.52961023180932,
)
MODE_TILE = 512
CLASS_TILE = 9
NT = (((1,), (1,)), ((), ()))
NN = (((1,), (0,)), ((), ()))
BLOCK_AXES = ("x", "z_hi", "y")
MIB = 1024 * 1024


def horner(coefs, square):
    total = jnp.full_like(square, coefs[-1])
    for coef in coefs[-2::-1]:
        total = total * square + coef
    return total


def cos_sin(turns):
    rest = turns - jnp.round(turns)
    square = rest * rest
    return horner(COS_COEFS, square), rest * horner(SIN_COEFS, square)


def dot(a, b, dims=NN):
    return lax.dot_general(a, b, dims, preferred_element_type=jnp.float32)


def split(value):
    high = value.astype(jnp.bfloat16)
    return high, (value - high.astype(jnp.float32)).astype(jnp.bfloat16)


def split3(value):
    high = value.astype(jnp.bfloat16)
    rest = value - high.astype(jnp.float32)
    middle = rest.astype(jnp.bfloat16)
    return high, middle, (rest - middle.astype(jnp.float32)).astype(jnp.bfloat16)


def dot_split(a, b, dims=NN):
    return dot(a[0], b[0], dims) + (dot(a[0], b[1], dims) + dot(a[1], b[0], dims))


def mixing_matrices():
    parts = []
    for matrix, gain in ((EVEN, None), (ODD, None), (EVEN, EVEN_GAIN), (ODD, ODD_GAIN)):
        matrix = np.array(matrix)
        if gain is not None:
            matrix = matrix / np.array(gain)[:, None]
        rest = np.pad(matrix, ((0, 16 - RANK), (0, 0))).astype(np.float32)
        pieces = []
        for _ in range(3):
            pieces.append(rest.astype(jnp.bfloat16))
            rest = rest - pieces[-1].astype(np.float32)
        first, second, third = pieces
        row = np.concatenate([first, first, second, second, first, third], axis=1)
        parts.append(np.pad(row, ((0, 0), (0, 128 - row.shape[1]))))
    return np.concatenate(parts, axis=1).astype(np.float32)


def mix(matrix, value):
    high, middle, low = split3(value)
    return dot(matrix, jnp.concatenate([high, middle, high, middle, low, high], axis=0))


def factors(first, second, mixing):
    width = first.shape[1]
    index = lax.broadcasted_iota(jnp.int32, (16, 1), 0)
    nodes = jnp.zeros((16, 1), jnp.float32)
    for i, node in enumerate(NODES):
        nodes = jnp.where(index == i, node, nodes)
    cos_part, sin_part = cos_sin(nodes * jnp.concatenate([first, second], axis=1))
    evens = mix(mixing[:, :96], cos_part)
    odds = mix(mixing[:, 128:224], sin_part)
    return evens[:, :width], odds[:, :width], evens[:, width:], odds[:, width:]


def outer_rows(left, right):
    for i in range(0, RANK, 2):
        yield jnp.concatenate([left[:8] * right[i : i + 1], left[:8] * right[i + 1 : i + 2]], axis=0)
    for i in range(8, RANK, 2):
        yield jnp.concatenate([left[i : i + 1] * right[:8], left[i + 1 : i + 2] * right[:8]], axis=0)


PAIR_ROWS = 8 * RANK + 8 * (RANK - 8)


def store_rows(high, low, columns, evx, odx, evy, ody, is_cos, sign):
    pairs = ((evx, evy, 1.0), (odx, ody, sign)) if is_cos else ((odx, evy, 1.0), (evx, ody, 1.0))
    row = 0
    for left, right, factor in pairs:
        if factor < 0:
            right = -right
        for value in outer_rows(left, right):
            part = split(value)
            high[row : row + 16, columns] = part[0]
            low[row : row + 16, columns] = part[1]
            row += 16


def as_column(row):
    count = row.shape[1]
    here = lax.broadcasted_iota(jnp.int32, (count, count), 0)
    there = lax.broadcasted_iota(jnp.int32, (count, count), 1)
    return jnp.sum(jnp.where(here == there, row, 0.0), axis=1, keepdims=True)


def structure_kernel(
    sizes, density_far, packed,
    partial, cos_out, sin_out, wave_c_high, wave_c_low, wave_s_high, wave_s_low,
    point_c_high, point_c_low, point_s_high, point_s_low,
    density, form_c, form_s, arrived,
):
    copy = pltpu.make_async_copy(density_far, density, arrived)
    copy.start()
    views, start = [], 0
    for size in sizes:
        padded = -(-size // 128) * 128
        views.append(packed.at[:, start : start + padded])
        start += padded
    waves, points, centers, mixing = views
    mixing = mixing[...].astype(jnp.bfloat16)
    every = slice(None)
    scale = 2.0 * BAND * TURN
    parts = factors(points[0:1, :] * scale, points[1:2, :] * scale, mixing[:, :256])
    store_rows(point_c_high, point_c_low, every, *parts, True, -1.0)
    store_rows(point_s_high, point_s_low, every, *parts, False, 1.0)
    copy.wait()
    dens = density[...]
    held_c = split(dot(dens, point_c_high[...], NT) + dot(dens, point_c_low[...], NT))
    held_s = split(dot(dens, point_s_high[...], NT) + dot(dens, point_s_low[...], NT))
    center_x = as_column(centers[0:1, :][:, : density.shape[0]])
    center_y = as_column(centers[1:2, :][:, : density.shape[0]])
    atoms, modes = cos_out.shape
    tile = min(MODE_TILE, modes)
    for start in range(0, modes, tile):
        here = slice(start, start + tile)
        kx = waves[0:1, here] * TURN
        ky = waves[1:2, here] * TURN
        parts = factors(kx * (BAND / 24.0), ky * (BAND / 24.0), mixing[:, 256:])
        store_rows(wave_c_high, wave_c_low, here, *parts, True, 1.0)
        store_rows(wave_s_high, wave_s_low, here, *parts, False, 1.0)
        form_c[:, here] = dot_split(held_c, (wave_c_high[:, here], wave_c_low[:, here]))
        form_s[:, here] = dot_split(held_s, (wave_s_high[:, here], wave_s_low[:, here]))
        real = jnp.zeros((16, tile), jnp.float32)
        imag = jnp.zeros((16, tile), jnp.float32)
        for row in range(0, atoms, 16):
            rows = slice(row, row + 16)
            cos_c, sin_c = cos_sin(center_x[rows] * kx + center_y[rows] * ky)
            cos_out[rows, here] = cos_c
            sin_out[rows, here] = sin_c
            cos_f, sin_f = form_c[rows, here], form_s[rows, here]
            real = real + (cos_c * cos_f - sin_c * sin_f)
            imag = imag + (sin_c * cos_f + cos_c * sin_f)
        partial[0:1, here] = jnp.sum(real, axis=0, keepdims=True)
        partial[1:2, here] = -jnp.sum(imag, axis=0, keepdims=True)


def partial_structure(density, centers, points, waves):
    atoms, count = density.shape
    modes = waves.shape[1]
    rows = 2 * PAIR_ROWS
    bf16, f32 = jnp.bfloat16, jnp.float32
    mixing = mixing_matrices()
    parts = [waves, points, centers, mixing]
    sizes = [part.shape[1] for part in parts]
    packed = jnp.concatenate(
        [jnp.pad(p, ((0, 16 - p.shape[0]), (0, -p.shape[1] % 128))) for p in parts], axis=1
    )
    out = lambda shape, kind: jax.ShapeDtypeStruct(shape, kind)
    return pl.pallas_call(
        functools.partial(structure_kernel, sizes),
        in_specs=[pl.BlockSpec(memory_space=pltpu.HBM), pl.BlockSpec(memory_space=pltpu.VMEM)],
        out_shape=[out((2, modes), f32)] + [out((atoms, modes), f32)] * 2
        + [out((rows, modes), bf16)] * 4 + [out((rows, count), bf16)] * 4,
        scratch_shapes=[pltpu.VMEM((atoms, count), bf16)]
        + [pltpu.VMEM((atoms, modes), f32)] * 2 + [pltpu.SemaphoreType.DMA],
        compiler_params=pltpu.CompilerParams(vmem_limit_bytes=30 * MIB),
        cost_estimate=pl.CostEstimate(
            flops=16 * atoms * rows * (count * 4 + modes * 6),
            bytes_accessed=8 * atoms * modes, transcendentals=0,
        ),
    )(density, packed)


def far_kernel(
    normalizer, first, second, weight, cos_c, sin_c,
    wave_c_high, wave_c_low, wave_s_high, wave_s_low,
    point_c_high, point_c_low, point_s_high, point_s_low,
    keep, send, spread_c_high, spread_c_low, spread_s_high, spread_s_low, field,
):
    atoms, modes = cos_c.shape
    tile = min(MODE_TILE, modes)
    held_c = held_s = None
    for start in range(0, modes, tile):
        here = slice(start, start + tile)
        scaled = weight[:, here] * normalizer
        real = (first[0:1, here] + second[0:1, here]) * scaled
        imag = (first[1:2, here] + second[1:2, here]) * scaled
        for row in range(0, atoms, 16):
            rows = slice(row, row + 16)
            cosine, sine = cos_c[rows, here], sin_c[rows, here]
            spread_c_high[rows, here], spread_c_low[rows, here] = split(real * cosine - imag * sine)
            spread_s_high[rows, here], spread_s_low[rows, here] = split(-(real * sine + imag * cosine))
        part_c = dot_split(
            (spread_c_high[:, here], spread_c_low[:, here]),
            (wave_c_high[:, here], wave_c_low[:, here]), NT,
        )
        part_s = dot_split(
            (spread_s_high[:, here], spread_s_low[:, here]),
            (wave_s_high[:, here], wave_s_low[:, here]), NT,
        )
        held_c = part_c if held_c is None else held_c + part_c
        held_s = part_s if held_s is None else held_s + part_s
    field[...] = dot_split(
        split(held_c), (point_c_high[...], point_c_low[...])
    ) + dot_split(split(held_s), (point_s_high[...], point_s_low[...]))
    chip, core = lax.axis_index("z_lo"), lax.axis_index("core")
    chips, _, width = keep.shape
    for ahead in range(chips):
        other = jnp.bitwise_xor(chip, ahead)
        mine = pl.multiple_of((2 * other + core) * width, width)
        theirs = pl.multiple_of((2 * other + 1 - core) * width, width)
        keep[ahead] = field[:, pl.ds(mine, width)]
        send[ahead] = field[:, pl.ds(theirs, width)]


def far_partial(normalizer, first, second, weight, cos_c, sin_c, waves, points, chips):
    atoms, modes = cos_c.shape
    rows, count = points[0].shape
    width = count // (2 * chips)
    return pl.pallas_call(
        functools.partial(far_kernel, normalizer),
        out_shape=[jax.ShapeDtypeStruct((chips, atoms, width), jnp.float32)] * 2,
        scratch_shapes=[pltpu.VMEM((atoms, modes), jnp.bfloat16)] * 4
        + [pltpu.VMEM((atoms, count), jnp.float32)],
        compiler_params=pltpu.CompilerParams(vmem_limit_bytes=30 * MIB),
        cost_estimate=pl.CostEstimate(
            flops=2 * atoms * rows * 6 * (count + modes),
            bytes_accessed=8 * atoms * modes, transcendentals=0,
        ),
    )(first, second, weight, cos_c, sin_c, *waves, *points)


def near_kernel(group, is_halo, offsets, atoms_of, counts, near, start, *rest):
    given, (out, sources, values, picks, made) = rest[:-5], rest[-5:]
    classes, width, count = near.shape
    atoms = out.shape[0]
    used = atoms * len(given)
    wide = picks.shape[2] // group
    for i, block in enumerate(given):
        sources[i * atoms : (i + 1) * atoms, :] = block[...]
    core = lax.axis_index("core")
    blocks = lax.axis_size(BLOCK_AXES)
    shift = atoms_of[...] - (lax.axis_index(BLOCK_AXES) - 1) * atoms
    shift = jnp.where(shift < 0, shift + blocks * atoms, shift)
    shift = jnp.where(shift >= blocks * atoms, shift - blocks * atoms, shift)
    live = lax.broadcasted_iota(jnp.int32, shift.shape, 0) < counts[...]
    places = jnp.where(live, shift + 1, 0).astype(jnp.float32)
    of_slot = offsets[...]
    found = [
        jnp.sum(jnp.where(of_slot == one, places, 0.0), axis=0, keepdims=True)
        for one in range(classes)
    ]
    found.append(jnp.zeros((-classes % 8, atoms), jnp.float32))
    found = jnp.transpose(jnp.concatenate(found, axis=0))
    column = lax.broadcasted_iota(jnp.int32, (1, wide), 1)
    if is_halo:
        base = jnp.where(column < atoms, core * 2 * atoms, (1 - core) * 2 * atoms - atoms)
    else:
        base = atoms
    target = jnp.where(column < used, column + base + 1, -1).astype(jnp.float32)
    for slot in range(2):
        for one in range(group):
            values[slot, one * wide + used : (one + 1) * wide, :] = jnp.zeros(
                (wide - used, 2 * width), values.dtype
            )
    result = jnp.zeros((atoms, 2 * width), jnp.float32)
    steps = classes // group
    for step in range(steps + 1):
        slot = step % 2
        if step < steps:
            block = near[step * group : (step + 1) * group].reshape(group * width, count)
            made[slot] = dot(sources[...], block, NT)
            for one in range(group):
                own_class = step * group + one
                chosen = jnp.where(found[:, own_class : own_class + 1] == target, 1.0, 0.0)
                picks[slot, :, one * wide : (one + 1) * wide] = chosen.astype(jnp.bfloat16)
        if step > 0:
            result = result + dot(picks[1 - slot], values[1 - slot])
        if step < steps:
            for one in range(group):
                high, low = split(made[slot, :, one * width : (one + 1) * width])
                rows = slice(one * wide, one * wide + used)
                values[slot, rows, :width] = high
                values[slot, rows, width:] = low
    if is_halo:
        begin = start[...]
    else:
        member = lax.axis_index("z_lo") * 2 + core
        mine = pl.multiple_of(member * width, width)
        begin = 0.5 * start[:, pl.ds(mine, width)].astype(jnp.float32)
    out[...] = begin + (result[:, :width] + result[:, width:])


def near_part(is_halo, offsets, atoms_of, counts, near, start, given):
    atoms = offsets.shape[1]
    classes, width, count = near.shape
    group = CLASS_TILE if classes % CLASS_TILE == 0 else 1
    used = atoms * len(given)
    wide = -(-used // 128) * 128
    bf16, f32 = jnp.bfloat16, jnp.float32
    return pl.pallas_call(
        functools.partial(near_kernel, group, is_halo),
        scratch_shapes=[
            pltpu.VMEM((used, count), bf16), pltpu.VMEM((2, group * wide, 2 * width), bf16),
            pltpu.VMEM((2, atoms, group * wide), bf16), pltpu.VMEM((2, used, group * width), f32),
        ],
        out_shape=jax.ShapeDtypeStruct((atoms, width), f32),
        compiler_params=pltpu.CompilerParams(vmem_limit_bytes=30 * MIB),
        cost_estimate=pl.CostEstimate(
            flops=2 * used * classes * width * (count + 2 * atoms),
            bytes_accessed=2 * classes * width * count, transcendentals=0,
        ),
    )(offsets, atoms_of, counts, near, start, *given)


def fold_kernel(keep, taken, *outs):
    for ahead, out in enumerate(outs):
        out[...] = keep[ahead] + taken[ahead]


def fold(keep, taken):
    chips, atoms, width = keep.shape
    return pl.pallas_call(
        fold_kernel,
        out_shape=[jax.ShapeDtypeStruct((atoms, width), jnp.float32)] * chips,
        compiler_params=pltpu.CompilerParams(vmem_limit_bytes=8 * MIB),
    )(keep, taken)


def shifted(value, axis, by):
    count = lax.axis_size(axis)
    return lax.ppermute(value, axis, [(i, (i + by) % count) for i in range(count)])


def sum_over(value, axis):
    count = lax.axis_size(axis)
    return value + sum(shifted(value, axis, by) for by in range(1, count))


def shards(
    density, near_blocks, neighbour_atoms, neighbour_offsets, neighbour_counts,
    centers, local_points, wavevectors, spectral_weight,
):
    atoms, points = density.shape
    blocks = lax.axis_size(BLOCK_AXES)
    modes = wavevectors.shape[1]
    chips, cores = lax.axis_size("z_lo"), lax.axis_size("core")
    normalizer = 1.0 / math.sqrt(atoms * blocks * points * modes * chips * cores)

    halo_route = []
    ring = lax.axis_size("y")
    for source in range(blocks):
        for chip in range(chips):
            for core, target in ((0, (source + 1) % blocks), (1, (source - 1) % blocks)):
                to = chip if source // ring == target // ring else chips - 1 - chip
                halo_route.append(((source * chips + chip) * 2 + core, (target * chips + to) * 2 + core))
    halo = lax.ppermute(density, BLOCK_AXES + ("z_lo", "core"), halo_route)

    partial, cos_c, sin_c, *tables = partial_structure(density, centers, local_points, wavevectors)

    lists = (neighbour_offsets.T, neighbour_atoms.T, neighbour_counts[None, :])
    near_own = near_part(False, *lists, near_blocks, density, [density])

    structure = sum_over(partial, "y")
    structure = sum_over(structure, "x")
    other_half = shifted(structure, "z_hi", 1)
    halo_other = lax.ppermute(halo, "core", [(0, 1), (1, 0)])

    structure, near_own = lax.optimization_barrier((structure, near_own))
    keep, send = far_partial(
        normalizer, structure, other_half, spectral_weight[None, :], cos_c, sin_c,
        tables[:4], tables[4:], chips,
    )
    taken = lax.ppermute(send, "core", [(0, 1), (1, 0)])
    near_field = near_part(True, *lists, near_blocks, near_own, [halo, halo_other])
    pieces = fold(keep, taken)
    far_field = pieces[0]
    for by in range(1, chips):
        swap = [(i, i ^ by) for i in range(chips)]
        far_field = far_field + lax.ppermute(pieces[by], "z_lo", swap)
    return near_field + far_field


def solution(mesh):
    fine = Mesh(
        mesh.devices.reshape(4, 2, 4, 4, 2), ("x", "z_hi", "y", "z_lo", "core")
    )
    modes = ("z_lo", "core")
    placed = (
        P(BLOCK_AXES, None), P(None, modes, None), P(BLOCK_AXES, None), P(BLOCK_AXES, None),
        P(BLOCK_AXES), P(None, BLOCK_AXES), P(), P(None, modes), P(modes),
    )
    return jax.shard_map(
        shards, mesh=fine, in_specs=placed, out_specs=P(BLOCK_AXES, modes), check_vma=False
    )
```

time: 78.3 us -> 51.4 us (0.66); the launches traced: 77.3 us -> 51.3 us
  local copies, waits for them, and re-layouts: 15.1 us -> 0.04 us
  Pallas kernels: 25.2 us -> 16.2 us
  waiting for transfers between devices: 4.42 us -> 9.69 us
  other arithmetic: 5.54 us -> 1.67 us
  starting transfers between devices: 26.9 us -> 23.5 us
    unnamed x46 -> x12, local copies, waits for them, and re-layouts: 15.1 us -> 0.04 us
    pallas_call x4, Pallas kernels: 25.2 us -> 16.2 us  [the longest x2 8.81 us: near_part(): pl.pallas_call(functools.partial(near_kernel, group, is_halo), scratch_sh...]
    ppermute x10 -> x7, starting transfers between devices: 16.4 us -> 12.5 us  [shifted(): lax.ppermute(value, axis, [(i, (i + by) % count) for i in range(count)])]
    ppermute x10 -> x7, waiting for transfers between devices: 4.41 us -> 7.59 us  [shifted(): lax.ppermute(value, axis, [(i, (i + by) % count) for i in range(count)])]
    add x2, other arithmetic: 2.16 us -> 0.04 us  [sum_over(): return value + sum((shifted(value, axis, by) for by in range(1, count)))]
    another operation x2 -> x0, other arithmetic: 1.22 us -> none  [the longest x1 0.66 us: shards(): place = jnp.stack([chip, core]).astype(jnp.int32)]
    ppermute x1, waiting for transfers between devices: 0.01 us -> 1.11 us  [shards(): taken = lax.ppermute(send, 'core', [(0, 1), (1, 0)])]
    ppermute x1 -> x4, waiting for transfers between devices: 0.01 us -> 0.99 us  [the longest x3 0.99 us: shards(): far_field = far_field + lax.ppermute(pieces[by], 'z_lo', swap)]
  transfers between devices with their start and end apart: 13 -> 13, of which waited for: 3 -> 6; matrix products, arithmetic and copies ran while one was open for 9% -> 0% of each run, Pallas kernels for 24% -> 22%
where the time goes in v2:
time: 51.4 us; the launch traced here: 51.3 us
  starting transfers between devices  23.5 us (46%)
  Pallas kernels  16.2 us (32%)
  waiting for transfers between devices  9.69 us (19%)
  other arithmetic  1.67 us (3%)
    ppermute x7, starting transfers between devices, shifted(): lax.ppermute(value, axis, [(i, (i + by) % count) for i in range(count)])  12.5 us
    pallas_call x2, Pallas kernels, near_part(): pl.pallas_call(functools.partial(near_kernel, group, is_halo), scratch_sh...  8.81 us
    ppermute x7, waiting for transfers between devices, shifted(): lax.ppermute(value, axis, [(i, (i + by) % count) for i in range(count)])  7.59 us
    ppermute x1, starting transfers between devices, shards(): halo = lax.ppermute(density, BLOCK_AXES + ('z_lo', 'core'), halo_route)  6.02 us
    pallas_call x1, Pallas kernels, partial_structure(): pl.pallas_call(functools.partial(structure_kernel, sizes), in_specs=[pl.B...  5.01 us
    ppermute x3, starting transfers between devices, shards(): far_field = far_field + lax.ppermute(pieces[by], 'z_lo', swap)  4.47 us
    pallas_call x1, Pallas kernels, far_partial(): pl.pallas_call(functools.partial(far_kernel, normalizer), out_shape=[jax....  2.38 us
    ppermute x1, waiting for transfers between devices, shards(): taken = lax.ppermute(send, 'core', [(0, 1), (1, 0)])  1.11 us
  transfers between devices with their start and end apart: 13, of which 6 were waited for; matrix products, arithmetic and copies ran while one was open for 0% of the time, Pallas kernels for 22%

profile of v2, /device:TPU:24, one launch (start us, length us, event | category | flops | bytes accessed | tf_op | source)
XLA Modules:
  0.0 51.3 jit_solution(1276215450358539631)
XLA Ops:
  0.0 1.0 %fusion.packed = f32[16,3840]{1,0:T(8,128)S(1)} fusion(f32[2,160]{1,0:T(2,128)} %param.15, f32[2,1024]{1,0:T(2,128)} %param.16, f32[2,2048]{1,0:T(2,128)} %param.17, f32[16,512]{1,0:T(8,128)} %constant.5.clone), kind=kLoop, calls=%fused_computation.5 | loop fusion | flops 798720 | bytes 304384 | tf_op jit(solution)/shard_map/concatenate | solution.py:221
  1.0 5.0 %shard_map.100 = (f32[2,2048]{1,0:T(2,128)S(1)}, f32[160,2048]{1,0:T(8,128)S(1)}, f32[160,2048]{1,0:T(8,128)S(1)}, bf16[192,2048]{1,0:T(8,128)(2,1)S(1)}, bf16[1...) custom-call(bf16[160,1024]{1,0:T(8,128)(2,1)} %rest_0_.1, ...), custom_call_target="tpu_custom_call" | custom-call | flops 8053063680 | bytes 2621440 | tf_op jit(solution)/shard_map/pallas_call | solution.py:225
  6.0 2.0 %collective-permute-start = (f32[2,2048]{1,0:T(2,128)S(1)}, f32[2,2048]{1,0:T(2,128)S(1)}, u32[]{:S(2)}, u32[]{:S(2)}) collective-permute-start(f32[2,2048]{1,0:T(2,128)S(1)} %get-tuple-element.24), channel_id=1, source_target_pairs={{0,8},{8,16},{16,24},{24,0},{1,9},{9,17},{17,25},{25,1},{2,10},{10... | collective-permute-start | bytes 49160 | tf_op jit(solution)/shard_map/ppermute | solution.py:398
  8.1 0.8 %collective-permute-start.1 = (f32[2,2048]{1,0:T(2,128)S(1)}, f32[2,2048]{1,0:T(2,128)S(1)}, u32[]{:S(2)}, u32[]{:S(2)}) collective-permute-start(f32[2,2048]{1,0:T(2,128)S(1)} %get-tuple-element.24), channel_id=1, source_target_pairs={{0,16},{8,24},{16,0},{24,8},{1,17},{9,25},{17,1},{25,9},{2,18},{10... | collective-permute-start | bytes 49160 | tf_op jit(solution)/shard_map/ppermute | solution.py:398
  8.9 0.1 collective-permute-start.2
  9.0 0.8 %collective-permute-done = f32[2,2048]{1,0:T(2,128)S(1)} collective-permute-done((f32[2,2048]{1,0:T(2,128)S(1)}, f32[2,2048]{1,0:T(2,128)S(1)}, u32[]{:S(2)}, u32[]{:S(2)}) %collective-permute-start) | collective-permute-done | bytes 16416 | tf_op jit(solution)/shard_map/ppermute | solution.py:398
  9.9 3.5 %collective-permute-done.1 = f32[2,2048]{1,0:T(2,128)S(1)} collective-permute-done((f32[2,2048]{1,0:T(2,128)S(1)}, f32[2,2048]{1,0:T(2,128)S(1)}, u32[]{:S(2)}, u32[]{:S(2)}) %collective-permute-start.1) | collective-permute-done | bytes 16416 | tf_op jit(solution)/shard_map/ppermute | solution.py:398
  13.3 0.6 %collective-permute-done.2 = f32[2,2048]{1,0:T(2,128)S(1)} collective-permute-done((f32[2,2048]{1,0:T(2,128)S(1)}, f32[2,2048]{1,0:T(2,128)S(1)}, u32[]{:S(2)}, u32[]{:S(2)}) %collective-permute-start.2) | collective-permute-done | bytes 16416 | tf_op jit(solution)/shard_map/ppermute | solution.py:398
  13.9 1.6 %collective-permute-start.3 = (f32[2,2048]{1,0:T(2,128)S(1)}, f32[2,2048]{1,0:T(2,128)S(1)}, u32[]{:S(2)}, u32[]{:S(2)}) collective-permute-start(f32[2,2048]{1,0:T(2,128)S(1)} %add_add_fusion.2), channel_id=1, source_target_pairs={{0,64},{64,128},{128,192},{192,0},{1,65},{65,129},{129,193},{193,1... | collective-permute-start | bytes 49160 | tf_op jit(solution)/shard_map/ppermute | solution.py:398
  15.5 2.8 %collective-permute-start.4 = (f32[2,2048]{1,0:T(2,128)S(1)}, f32[2,2048]{1,0:T(2,128)S(1)}, u32[]{:S(2)}, u32[]{:S(2)}) collective-permute-start(f32[2,2048]{1,0:T(2,128)S(1)} %add_add_fusion.2), channel_id=1, source_target_pairs={{0,128},{64,192},{128,0},{192,64},{1,129},{65,193},{129,1},{193,65... | collective-permute-start | bytes 49160 | tf_op jit(solution)/shard_map/ppermute | solution.py:398
  18.3 1.4 %collective-permute-start.5 = (f32[2,2048]{1,0:T(2,128)S(1)}, f32[2,2048]{1,0:T(2,128)S(1)}, u32[]{:S(2)}, u32[]{:S(2)}) collective-permute-start(f32[2,2048]{1,0:T(2,128)S(1)} %add_add_fusion.2), channel_id=1, source_target_pairs={{0,192},{64,0},{128,64},{192,128},{1,193},{65,1},{129,65},{193,129... | collective-permute-start | bytes 49160 | tf_op jit(solution)/shard_map/ppermute | solution.py:398
  19.6 6.0 %collective-permute-start.6 = (bf16[160,1024]{1,0:T(8,128)(2,1)}, bf16[160,1024]{1,0:T(8,128)(2,1)S(1)}, u32[]{:S(2)}, u32[]{:S(2)}) collective-permute-start(bf16[160,1024]{1,0:T(8,128)(2,1)} %rest_0_.1), channel_id=1, source_target_pairs={{0,8},{1,255},{2,10},{3,253},{4,12},{5,251},{6,14},{7,249},{8,16},... | collective-permute-start | bytes 983048 | tf_op jit(solution)/shard_map/ppermute | solution.py:423
  25.7 3.7 %collective-permute-start.8 = (f32[2,2048]{1,0:T(2,128)S(1)}, f32[2,2048]{1,0:T(2,128)S(1)}, u32[]{:S(2)}, u32[]{:S(2)}) collective-permute-start(f32[2,2048]{1,0:T(2,128)S(1)} %add_add_fusion.1.first), channel_id=1, source_target_pairs={{0,32},{32,0},{1,33},{33,1},{2,34},{34,2},{3,35},{35,3},{4,36},{36... | collective-permute-start | bytes 49160 | tf_op jit(solution)/shard_map/ppermute | solution.py:398
  29.5 4.4 %shard_map.101.start = f32[160,128]{1,0:T(8,128)S(1)} custom-call(s32[27,160]{1,0:T(8,128)S(1)} %bitcast.6, s32[27,160]{1,0:T(8,128)S(1)} %bitcast.8, s32[1,160]{1,0:T(1,128)S(1)} %bitcast.11, bf16[27,128,1024]{2,1,0:T(8,128)(2,1)S(1)} %bitcast.5, bf16[160,1024]{1,0:T(8,128)(2,1)} %rest_0_.1, bf16[160,1024]{1,0:T(8,128)(2,1)} %rest_0_.1), custom_call_target="tpu_custom_call" | custom-call | flops 1486356480 | bytes 7077888 | tf_op jit(solution)/shard_map/pallas_call | solution.py:367
  33.8 2.7 %collective-permute-done.8.second = f32[2,2048]{1,0:T(2,128)S(1)} collective-permute-done((f32[2,2048]{1,0:T(2,128)S(1)}, f32[2,2048]{1,0:T(2,128)S(1)}, u32[]{:S(2)}, u32[]{:S(2)}) %collective-permute-start.8) | collective-permute-done | bytes 16416 | tf_op jit(solution)/shard_map/ppermute | solution.py:398
  36.6 2.4 %shard_map.103 = (f32[4,160,128]{2,1,0:T(8,128)S(1)}, f32[4,160,128]{2,1,0:T(8,128)S(1)}) custom-call(f32[2,2048]{1,0:T(2,128)S(1)} %add_add_fusion.1.first, f32[2,2048]{1,0:T(2,128)S(1)} %collective-permute-done.8.second, f32[1,2048]{1,0:T(1,128)S(1)} %bitcast.10, f32[160,2048]{1,0:T(8,128)S(1)} %get-tuple-element.27.cos_c, ...), custom_call_target="tpu_custom_call" | custom-call | flops 1132462080 | bytes 2621440 | tf_op jit(solution)/shard_map/pallas_call | solution.py:286
  39.1 0.5 collective-permute-start.7
  39.6 1.1 %collective-permute-done.9.taken = f32[4,160,128]{2,1,0:T(8,128)S(1)} collective-permute-done((f32[4,160,128]{2,1,0:T(8,128)S(1)}, f32[4,160,128]{2,1,0:T(8,128)S(1)}, u32[]{:S(2)}, u32[]{:S(2)}) %collective-permute-start.9) | collective-permute-done | bytes 327712 | tf_op jit(solution)/shard_map/ppermute | solution.py:440
  40.7 0.1 collective-permute-start.10
  40.8 2.5 %collective-permute-start.11 = (f32[160,128]{1,0:T(8,128)S(1)}, f32[160,128]{1,0:T(8,128)S(1)}, u32[]{:S(2)}, u32[]{:S(2)}) collective-permute-start(f32[160,128]{1,0:T(8,128)S(1)} %get-tuple-element.41), channel_id=1, source_target_pairs={{0,4},{2,6},{4,0},{6,2},{1,5},{3,7},{5,1},{7,3},{8,12},{10,14},{12... | collective-permute-start | bytes 245768 | tf_op jit(solution)/shard_map/ppermute | solution.py:446
  43.3 1.9 %collective-permute-start.12 = (f32[160,128]{1,0:T(8,128)S(1)}, f32[160,128]{1,0:T(8,128)S(1)}, u32[]{:S(2)}, u32[]{:S(2)}) collective-permute-start(f32[160,128]{1,0:T(8,128)S(1)} %get-tuple-element.42), channel_id=1, source_target_pairs={{0,6},{2,4},{4,2},{6,0},{1,7},{3,5},{5,3},{7,1},{8,14},{10,12},{12... | collective-permute-start | bytes 245768 | tf_op jit(solution)/shard_map/ppermute | solution.py:446
  45.2 4.4 %shard_map.102 = f32[160,128]{1,0:T(8,128)S(1)} custom-call(s32[27,160]{1,0:T(8,128)S(1)} %bitcast.7, s32[27,160]{1,0:T(8,128)S(1)} %bitcast.9, s32[1,160]{1,0:T(1,128)S(1)} %bitcast.12, bf16[27,128,1024]{2,1,0:T(8,128)(2,1)S(1)} %bitcast.5, f32[160,128]{1,0:T(8,128)S(1)} %shard_map.101.start, bf16[160,1024]{1,0:T(8,128)(2,1)S(1)} %collective-permute-done.6.rest_0_, ...), custom_call_target="tpu_custom_call" | custom-call | flops 2972712960 | bytes 7077888 | tf_op jit(solution)/shard_map/pallas_call | solution.py:367
  49.7 1.0 %collective-permute-done.11 = f32[160,128]{1,0:T(8,128)S(1)} collective-permute-done((f32[160,128]{1,0:T(8,128)S(1)}, f32[160,128]{1,0:T(8,128)S(1)}, u32[]{:S(2)}, u32[]{:S(2)}) %collective-permute-start.11) | collective-permute-done | bytes 81952 | tf_op jit(solution)/shard_map/ppermute | solution.py:446
  50.7 0.7 %add_add_fusion = f32[160,128]{1,0:T(8,128)} fusion(f32[160,128]{1,0:T(8,128)S(1)} %shard_map.102, f32[160,128]{1,0:T(8,128)S(1)} %collective-permute-done.12, f32[160,128]{1,0:T(8,128)S(1)} %collective-permute-done.11, f32[160,128]{1,0:T(8,128)S(1)} %get-tuple-element.39, f32[160,128]{1,0:T(8,128)S(1)} %collective-permute-done.10), kind=kLoop, calls=%fused_computation.10 | loop fusion | flops 81920 | bytes 491520 | tf_op jit(solution)/shard_map/add | solution.py:447
  (24 shorter events, 0.2 us)
Async XLA Ops:
  0.0 29.4 %slice-start = ((s8[7077888]{0:T(1024)(128)(4,1)}), s8[4194304]{0:T(1024)(128)(4,1)S(1)}, s32[]{:S(2)}) async-start(s8[7077888]{0:T(1024)(128)(4,1)} %bitcast.4), calls=%async_computation | async-start | bytes 8388608
  1.0 28.4 %slice-start.1 = ((s8[7077888]{0:T(1024)(128)(4,1)}), s8[2883584]{0:T(1024)(128)(4,1)S(1)}, s32[]{:S(2)}) async-start(s8[7077888]{0:T(1024)(128)(4,1)} %bitcast.4), calls=%async_computation.1 | async-start | bytes 5767168
  1.0 28.4 %copy-start = (s32[160,27]{0,1:T(8,128)S(1)}, s32[160,27]{0,1:T(8,128)}, u32[]{:S(2)}) copy-start(s32[160,27]{0,1:T(8,128)} %param.13) | copy-start | bytes 51844
  1.0 28.4 %copy-start.1 = (s32[160,27]{0,1:T(8,128)S(1)}, s32[160,27]{0,1:T(8,128)}, u32[]{:S(2)}) copy-start(s32[160,27]{0,1:T(8,128)} %param.12) | copy-start | bytes 51844
  1.0 28.4 %copy-start.3 = (s32[160]{0:T(256)S(1)}, s32[160]{0:T(256)}, u32[]{:S(2)}) copy-start(s32[160]{0:T(256)} %param.14) | copy-start | bytes 1924
  6.0 3.8 %collective-permute-start = (f32[2,2048]{1,0:T(2,128)S(1)}, f32[2,2048]{1,0:T(2,128)S(1)}, u32[]{:S(2)}, u32[]{:S(2)}) collective-permute-start(f32[2,2048]{1,0:T(2,128)S(1)} %get-tuple-element.24), channel_id=1, source_target_pairs={{0,8},{8,16},{16,24},{24,0},{1,9},{9,17},{17,25},{25,1},{2,10},{10... | collective-permute-start | bytes 49160 | tf_op jit(solution)/shard_map/ppermute | solution.py:398
  8.1 5.2 %collective-permute-start.1 = (f32[2,2048]{1,0:T(2,128)S(1)}, f32[2,2048]{1,0:T(2,128)S(1)}, u32[]{:S(2)}, u32[]{:S(2)}) collective-permute-start(f32[2,2048]{1,0:T(2,128)S(1)} %get-tuple-element.24), channel_id=1, source_target_pairs={{0,16},{8,24},{16,0},{24,8},{1,17},{9,25},{17,1},{25,9},{2,18},{10... | collective-permute-start | bytes 49160 | tf_op jit(solution)/shard_map/ppermute | solution.py:398
  8.9 4.9 %collective-permute-start.2 = (f32[2,2048]{1,0:T(2,128)S(1)}, f32[2,2048]{1,0:T(2,128)S(1)}, u32[]{:S(2)}, u32[]{:S(2)}) collective-permute-start(f32[2,2048]{1,0:T(2,128)S(1)} %get-tuple-element.24), channel_id=1, source_target_pairs={{0,24},{8,0},{16,8},{24,16},{1,25},{9,1},{17,9},{25,17},{2,26},{10... | collective-permute-start | bytes 49160 | tf_op jit(solution)/shard_map/ppermute | solution.py:398
  13.9 11.8 %collective-permute-start.3 = (f32[2,2048]{1,0:T(2,128)S(1)}, f32[2,2048]{1,0:T(2,128)S(1)}, u32[]{:S(2)}, u32[]{:S(2)}) collective-permute-start(f32[2,2048]{1,0:T(2,128)S(1)} %add_add_fusion.2), channel_id=1, source_target_pairs={{0,64},{64,128},{128,192},{192,0},{1,65},{65,129},{129,193},{193,1... | collective-permute-start | bytes 49160 | tf_op jit(solution)/shard_map/ppermute | solution.py:398
  15.5 10.2 %collective-permute-start.4 = (f32[2,2048]{1,0:T(2,128)S(1)}, f32[2,2048]{1,0:T(2,128)S(1)}, u32[]{:S(2)}, u32[]{:S(2)}) collective-permute-start(f32[2,2048]{1,0:T(2,128)S(1)} %add_add_fusion.2), channel_id=1, source_target_pairs={{0,128},{64,192},{128,0},{192,64},{1,129},{65,193},{129,1},{193,65... | collective-permute-start | bytes 49160 | tf_op jit(solution)/shard_map/ppermute | solution.py:398
  18.3 7.4 %collective-permute-start.5 = (f32[2,2048]{1,0:T(2,128)S(1)}, f32[2,2048]{1,0:T(2,128)S(1)}, u32[]{:S(2)}, u32[]{:S(2)}) collective-permute-start(f32[2,2048]{1,0:T(2,128)S(1)} %add_add_fusion.2), channel_id=1, source_target_pairs={{0,192},{64,0},{128,64},{192,128},{1,193},{65,1},{129,65},{193,129... | collective-permute-start | bytes 49160 | tf_op jit(solution)/shard_map/ppermute | solution.py:398
  19.6 19.4 %collective-permute-start.6 = (bf16[160,1024]{1,0:T(8,128)(2,1)}, bf16[160,1024]{1,0:T(8,128)(2,1)S(1)}, u32[]{:S(2)}, u32[]{:S(2)}) collective-permute-start(bf16[160,1024]{1,0:T(8,128)(2,1)} %rest_0_.1), channel_id=1, source_target_pairs={{0,8},{1,255},{2,10},{3,253},{4,12},{5,251},{6,14},{7,249},{8,16},... | collective-permute-start | bytes 983048 | tf_op jit(solution)/shard_map/ppermute | solution.py:423
  25.7 10.9 %collective-permute-start.8 = (f32[2,2048]{1,0:T(2,128)S(1)}, f32[2,2048]{1,0:T(2,128)S(1)}, u32[]{:S(2)}, u32[]{:S(2)}) collective-permute-start(f32[2,2048]{1,0:T(2,128)S(1)} %add_add_fusion.1.first), channel_id=1, source_target_pairs={{0,32},{32,0},{1,33},{33,1},{2,34},{34,2},{3,35},{35,3},{4,36},{36... | collective-permute-start | bytes 49160 | tf_op jit(solution)/shard_map/ppermute | solution.py:398
  29.5 7.1 %copy-start.2 = (f32[2048]{0:T(1024)S(1)}, f32[2048]{0:T(1024)}, u32[]{:S(2)}) copy-start(f32[2048]{0:T(1024)} %param.18) | copy-start | bytes 24580
  39.0 1.7 %collective-permute-start.9 = (f32[4,160,128]{2,1,0:T(8,128)S(1)}, f32[4,160,128]{2,1,0:T(8,128)S(1)}, u32[]{:S(2)}, u32[]{:S(2)}) collective-permute-start(f32[4,160,128]{2,1,0:T(8,128)S(1)} %get-tuple-element.38), channel_id=1, source_target_pairs={{0,1},{1,0},{2,3},{3,2},{4,5},{5,4},{6,7},{7,6},{8,9},{9,8},{10,11... | collective-permute-start | bytes 983048 | tf_op jit(solution)/shard_map/ppermute | solution.py:440
  39.1 6.1 %collective-permute-start.7 = (bf16[160,1024]{1,0:T(8,128)(2,1)S(1)}, bf16[160,1024]{1,0:T(8,128)(2,1)S(1)}, u32[]{:S(2)}, u32[]{:S(2)}) collective-permute-start(bf16[160,1024]{1,0:T(8,128)(2,1)S(1)} %collective-permute-done.6.rest_0_), channel_id=1, source_target_pairs={{0,1},{1,0},{2,3},{3,2},{4,5},{5,4},{6,7},{7,6},{8,9},{9,8},{10,11... | collective-permute-start | bytes 983048 | tf_op jit(solution)/shard_map/ppermute | solution.py:433
  40.7 8.9 %collective-permute-start.10 = (f32[160,128]{1,0:T(8,128)S(1)}, f32[160,128]{1,0:T(8,128)S(1)}, u32[]{:S(2)}, u32[]{:S(2)}) collective-permute-start(f32[160,128]{1,0:T(8,128)S(1)} %get-tuple-element.40), channel_id=1, source_target_pairs={{0,2},{2,0},{4,6},{6,4},{1,3},{3,1},{5,7},{7,5},{8,10},{10,8},{12,... | collective-permute-start | bytes 245768 | tf_op jit(solution)/shard_map/ppermute | solution.py:446
  40.8 9.8 %collective-permute-start.11 = (f32[160,128]{1,0:T(8,128)S(1)}, f32[160,128]{1,0:T(8,128)S(1)}, u32[]{:S(2)}, u32[]{:S(2)}) collective-permute-start(f32[160,128]{1,0:T(8,128)S(1)} %get-tuple-element.41), channel_id=1, source_target_pairs={{0,4},{2,6},{4,0},{6,2},{1,5},{3,7},{5,1},{7,3},{8,12},{10,14},{12... | collective-permute-start | bytes 245768 | tf_op jit(solution)/shard_map/ppermute | solution.py:446
  43.3 7.4 %collective-permute-start.12 = (f32[160,128]{1,0:T(8,128)S(1)}, f32[160,128]{1,0:T(8,128)S(1)}, u32[]{:S(2)}, u32[]{:S(2)}) collective-permute-start(f32[160,128]{1,0:T(8,128)S(1)} %get-tuple-element.42), channel_id=1, source_target_pairs={{0,6},{2,4},{4,2},{6,0},{1,7},{3,5},{5,3},{7,1},{8,14},{10,12},{12... | collective-permute-start | bytes 245768 | tf_op jit(solution)/shard_map/ppermute | solution.py:446

commit v3 on v2

--- a/solution.py
+++ b/solution.py
@@ -418,7 +418,7 @@
     for source in range(blocks):
         for chip in range(chips):
             for core, target in ((0, (source + 1) % blocks), (1, (source - 1) % blocks)):
-                to = chip if source // ring == target // ring else chips - 1 - chip
+                to = chip if source // ring == target // ring else (chip + chips // 2) % chips
                 halo_route.append(((source * chips + chip) * 2 + core, (target * chips + to) * 2 + core))
     halo = lax.ppermute(density, BLOCK_AXES + ("z_lo", "core"), halo_route)
 
@@ -439,11 +439,11 @@
     )
     taken = lax.ppermute(send, "core", [(0, 1), (1, 0)])
     near_field = near_part(True, *lists, near_blocks, near_own, [halo, halo_other])
-    pieces = fold(keep, taken)
-    far_field = pieces[0]
-    for by in range(1, chips):
+    far_field = keep[0] + taken[0]
+    for by in range(chips - 1, 0, -1):
         swap = [(i, i ^ by) for i in range(chips)]
-        far_field = far_field + lax.ppermute(pieces[by], "z_lo", swap)
+        piece = ((keep[by] + taken[by]) * (1.0 / 32.0)).astype(jnp.float16)
+        far_field = far_field + lax.ppermute(piece, "z_lo", swap).astype(jnp.float32) * 32.0
     return near_field + far_field
 
 

time: 51.4 us -> 48.5 us (0.944); the launches traced: 51.3 us -> 47.8 us
  waiting for transfers between devices: 9.69 us -> 6.14 us
    ppermute x7, waiting for transfers between devices: 7.59 us -> 5.02 us  [shifted(): lax.ppermute(value, axis, [(i, (i + by) % count) for i in range(count)])]
    ppermute x3, waiting for transfers between devices: 0.99 us -> 0.01 us  [shards(): lax.ppermute(piece, 'z_lo', swap).astype(jnp.float32) * 32.0]
  transfers between devices with their start and end apart: 13 -> 13, of which waited for: 6 -> 5; matrix products, arithmetic and copies ran while one was open for 0% -> 0% of each run, Pallas kernels for 22% -> 23%
where the time goes in v3:
time: 48.5 us; the launch traced here: 47.8 us
  starting transfers between devices  23.5 us (48%)
  Pallas kernels  16.2 us (33%)
  waiting for transfers between devices  6.14 us (13%)
  other arithmetic  1.73 us (4%)
    ppermute x7, starting transfers between devices, shifted(): lax.ppermute(value, axis, [(i, (i + by) % count) for i in range(count)])  12.1 us
    pallas_call x2, Pallas kernels, near_part(): pl.pallas_call(functools.partial(near_kernel, group, is_halo), scratch_sh...  8.81 us
    ppermute x1, starting transfers between devices, shards(): halo = lax.ppermute(density, BLOCK_AXES + ('z_lo', 'core'), halo_route)  6.42 us
    ppermute x7, waiting for transfers between devices, shifted(): lax.ppermute(value, axis, [(i, (i + by) % count) for i in range(count)])  5.02 us
    pallas_call x1, Pallas kernels, partial_structure(): pl.pallas_call(functools.partial(structure_kernel, sizes), in_specs=[pl.B...  5.01 us
    ppermute x3, starting transfers between devices, shards(): lax.ppermute(piece, 'z_lo', swap).astype(jnp.float32) * 32.0  4.47 us
    pallas_call x1, Pallas kernels, far_partial(): pl.pallas_call(functools.partial(far_kernel, normalizer), out_shape=[jax....  2.4 us
    ppermute x1, waiting for transfers between devices, shards(): taken = lax.ppermute(send, 'core', [(0, 1), (1, 0)])  1.11 us
  transfers between devices with their start and end apart: 13, of which 5 were waited for; matrix products, arithmetic and copies ran while one was open for 0% of the time, Pallas kernels for 23%

profile of v3, /device:TPU:24, one launch (start us, length us, event | category | flops | bytes accessed | tf_op | source)
XLA Modules:
  0.0 47.8 jit_solution(12199319288707823125)
XLA Ops:
  0.0 1.0 %fusion.packed = f32[16,3840]{1,0:T(8,128)S(1)} fusion(f32[2,160]{1,0:T(2,128)} %param.15, f32[2,1024]{1,0:T(2,128)} %param.16, f32[2,2048]{1,0:T(2,128)} %param.17, f32[16,512]{1,0:T(8,128)} %constant.9.clone), kind=kLoop, calls=%fused_computation.5 | loop fusion | flops 798720 | bytes 304384 | tf_op jit(solution)/shard_map/concatenate | solution.py:221
  1.0 5.0 %shard_map.100 = (f32[2,2048]{1,0:T(2,128)S(1)}, f32[160,2048]{1,0:T(8,128)S(1)}, f32[160,2048]{1,0:T(8,128)S(1)}, bf16[192,2048]{1,0:T(8,128)(2,1)S(1)}, bf16[1...) custom-call(bf16[160,1024]{1,0:T(8,128)(2,1)} %rest_0_.1, ...), custom_call_target="tpu_custom_call" | custom-call | flops 8053063680 | bytes 2621440 | tf_op jit(solution)/shard_map/pallas_call | solution.py:225
  6.0 2.0 %collective-permute-start = (f32[2,2048]{1,0:T(2,128)S(1)}, f32[2,2048]{1,0:T(2,128)S(1)}, u32[]{:S(2)}, u32[]{:S(2)}) collective-permute-start(f32[2,2048]{1,0:T(2,128)S(1)} %get-tuple-element.20), channel_id=1, source_target_pairs={{0,8},{8,16},{16,24},{24,0},{1,9},{9,17},{17,25},{25,1},{2,10},{10... | collective-permute-start | bytes 49160 | tf_op jit(solution)/shard_map/ppermute | solution.py:398
  8.1 0.8 %collective-permute-start.1 = (f32[2,2048]{1,0:T(2,128)S(1)}, f32[2,2048]{1,0:T(2,128)S(1)}, u32[]{:S(2)}, u32[]{:S(2)}) collective-permute-start(f32[2,2048]{1,0:T(2,128)S(1)} %get-tuple-element.20), channel_id=1, source_target_pairs={{0,16},{8,24},{16,0},{24,8},{1,17},{9,25},{17,1},{25,9},{2,18},{10... | collective-permute-start | bytes 49160 | tf_op jit(solution)/shard_map/ppermute | solution.py:398
  8.9 0.1 collective-permute-start.2
  9.0 0.8 %collective-permute-done = f32[2,2048]{1,0:T(2,128)S(1)} collective-permute-done((f32[2,2048]{1,0:T(2,128)S(1)}, f32[2,2048]{1,0:T(2,128)S(1)}, u32[]{:S(2)}, u32[]{:S(2)}) %collective-permute-start) | collective-permute-done | bytes 16416 | tf_op jit(solution)/shard_map/ppermute | solution.py:398
  9.9 3.5 %collective-permute-done.1 = f32[2,2048]{1,0:T(2,128)S(1)} collective-permute-done((f32[2,2048]{1,0:T(2,128)S(1)}, f32[2,2048]{1,0:T(2,128)S(1)}, u32[]{:S(2)}, u32[]{:S(2)}) %collective-permute-start.1) | collective-permute-done | bytes 16416 | tf_op jit(solution)/shard_map/ppermute | solution.py:398
  13.3 0.6 %collective-permute-done.2 = f32[2,2048]{1,0:T(2,128)S(1)} collective-permute-done((f32[2,2048]{1,0:T(2,128)S(1)}, f32[2,2048]{1,0:T(2,128)S(1)}, u32[]{:S(2)}, u32[]{:S(2)}) %collective-permute-start.2) | collective-permute-done | bytes 16416 | tf_op jit(solution)/shard_map/ppermute | solution.py:398
  13.9 1.6 %collective-permute-start.3 = (f32[2,2048]{1,0:T(2,128)S(1)}, f32[2,2048]{1,0:T(2,128)S(1)}, u32[]{:S(2)}, u32[]{:S(2)}) collective-permute-start(f32[2,2048]{1,0:T(2,128)S(1)} %add_add_fusion.1), channel_id=1, source_target_pairs={{0,64},{64,128},{128,192},{192,0},{1,65},{65,129},{129,193},{193,1... | collective-permute-start | bytes 49160 | tf_op jit(solution)/shard_map/ppermute | solution.py:398
  15.5 2.8 %collective-permute-start.4 = (f32[2,2048]{1,0:T(2,128)S(1)}, f32[2,2048]{1,0:T(2,128)S(1)}, u32[]{:S(2)}, u32[]{:S(2)}) collective-permute-start(f32[2,2048]{1,0:T(2,128)S(1)} %add_add_fusion.1), channel_id=1, source_target_pairs={{0,128},{64,192},{128,0},{192,64},{1,129},{65,193},{129,1},{193,65... | collective-permute-start | bytes 49160 | tf_op jit(solution)/shard_map/ppermute | solution.py:398
  18.3 1.4 %collective-permute-start.5 = (f32[2,2048]{1,0:T(2,128)S(1)}, f32[2,2048]{1,0:T(2,128)S(1)}, u32[]{:S(2)}, u32[]{:S(2)}) collective-permute-start(f32[2,2048]{1,0:T(2,128)S(1)} %add_add_fusion.1), channel_id=1, source_target_pairs={{0,192},{64,0},{128,64},{192,128},{1,193},{65,1},{129,65},{193,129... | collective-permute-start | bytes 49160 | tf_op jit(solution)/shard_map/ppermute | solution.py:398
  19.6 6.4 %collective-permute-start.6 = (bf16[160,1024]{1,0:T(8,128)(2,1)}, bf16[160,1024]{1,0:T(8,128)(2,1)S(1)}, u32[]{:S(2)}, u32[]{:S(2)}) collective-permute-start(bf16[160,1024]{1,0:T(8,128)(2,1)} %rest_0_.1), channel_id=1, source_target_pairs={{0,8},{1,253},{2,10},{3,255},{4,12},{5,249},{6,14},{7,251},{8,16},... | collective-permute-start | bytes 983048 | tf_op jit(solution)/shard_map/ppermute | solution.py:423
  26.1 3.3 %collective-permute-start.8 = (f32[2,2048]{1,0:T(2,128)S(1)}, f32[2,2048]{1,0:T(2,128)S(1)}, u32[]{:S(2)}, u32[]{:S(2)}) collective-permute-start(f32[2,2048]{1,0:T(2,128)S(1)} %add_add_fusion.first), channel_id=1, source_target_pairs={{0,32},{32,0},{1,33},{33,1},{2,34},{34,2},{3,35},{35,3},{4,36},{36... | collective-permute-start | bytes 49160 | tf_op jit(solution)/shard_map/ppermute | solution.py:398
  29.5 4.4 %shard_map.101.start = f32[160,128]{1,0:T(8,128)S(1)} custom-call(s32[27,160]{1,0:T(8,128)S(1)} %bitcast.22, s32[27,160]{1,0:T(8,128)S(1)} %bitcast.24, s32[1,160]{1,0:T(1,128)S(1)} %bitcast.27, bf16[27,128,1024]{2,1,0:T(8,128)(2,1)S(1)} %bitcast.21, bf16[160,1024]{1,0:T(8,128)(2,1)} %rest_0_.1, bf16[160,1024]{1,0:T(8,128)(2,1)} %rest_0_.1), custom_call_target="tpu_custom_call" | custom-call | flops 1486356480 | bytes 7077888 | tf_op jit(solution)/shard_map/pallas_call | solution.py:367
  33.8 0.2 collective-permute-done.8.second
  34.0 2.4 %shard_map.103 = (f32[4,160,128]{2,1,0:T(8,128)S(1)}, f32[4,160,128]{2,1,0:T(8,128)S(1)}) custom-call(f32[2,2048]{1,0:T(2,128)S(1)} %add_add_fusion.first, f32[2,2048]{1,0:T(2,128)S(1)} %collective-permute-done.8.second, f32[1,2048]{1,0:T(1,128)S(1)} %bitcast.26, f32[160,2048]{1,0:T(8,128)S(1)} %get-tuple-element.23.cos_c, ...), custom_call_target="tpu_custom_call" | custom-call | flops 1132462080 | bytes 2621440 | tf_op jit(solution)/shard_map/pallas_call | solution.py:286
  36.4 0.1 collective-permute-start.9
  36.5 0.5 %collective-permute-start.7 = (bf16[160,1024]{1,0:T(8,128)(2,1)S(1)}, bf16[160,1024]{1,0:T(8,128)(2,1)S(1)}, u32[]{:S(2)}, u32[]{:S(2)}) collective-permute-start(bf16[160,1024]{1,0:T(8,128)(2,1)S(1)} %collective-permute-done.6.rest_0_), channel_id=1, source_target_pairs={{0,1},{1,0},{2,3},{3,2},{4,5},{5,4},{6,7},{7,6},{8,9},{9,8},{10,11... | collective-permute-start | bytes 983048 | tf_op jit(solution)/shard_map/ppermute | solution.py:433
  37.0 1.1 %collective-permute-done.9 = f32[4,160,128]{2,1,0:T(8,128)S(1)} collective-permute-done((f32[4,160,128]{2,1,0:T(8,128)S(1)}, f32[4,160,128]{2,1,0:T(8,128)S(1)}, u32[]{:S(2)}, u32[]{:S(2)}) %collective-permute-start.9) | collective-permute-done | bytes 327712 | tf_op jit(solution)/shard_map/ppermute | solution.py:440
  38.2 2.0 %collective-permute-start.10 = (f16[160,128]{1,0:T(8,128)(2,1)S(1)}, f16[160,128]{1,0:T(8,128)(2,1)S(1)}, u32[]{:S(2)}, u32[]{:S(2)}) collective-permute-start(f16[160,128]{1,0:T(8,128)(2,1)S(1)} %get-tuple-element.35), channel_id=1, source_target_pairs={{0,6},{2,4},{4,2},{6,0},{1,7},{3,5},{5,3},{7,1},{8,14},{10,12},{12... | collective-permute-start | bytes 122888 | tf_op jit(solution)/shard_map/ppermute | solution.py:446
  40.1 0.6 %collective-permute-start.11 = (f16[160,128]{1,0:T(8,128)(2,1)S(1)}, f16[160,128]{1,0:T(8,128)(2,1)S(1)}, u32[]{:S(2)}, u32[]{:S(2)}) collective-permute-start(f16[160,128]{1,0:T(8,128)(2,1)S(1)} %get-tuple-element.37), channel_id=1, source_target_pairs={{0,4},{2,6},{4,0},{6,2},{1,5},{3,7},{5,1},{7,3},{8,12},{10,14},{12... | collective-permute-start | bytes 122888 | tf_op jit(solution)/shard_map/ppermute | solution.py:446
  40.8 1.9 %collective-permute-start.12 = (f16[160,128]{1,0:T(8,128)(2,1)S(1)}, f16[160,128]{1,0:T(8,128)(2,1)S(1)}, u32[]{:S(2)}, u32[]{:S(2)}) collective-permute-start(f16[160,128]{1,0:T(8,128)(2,1)S(1)} %get-tuple-element.36), channel_id=1, source_target_pairs={{0,2},{2,0},{4,6},{6,4},{1,3},{3,1},{5,7},{7,5},{8,10},{10,8},{12,... | collective-permute-start | bytes 122888 | tf_op jit(solution)/shard_map/ppermute | solution.py:446
  42.7 4.4 %shard_map.102 = f32[160,128]{1,0:T(8,128)S(1)} custom-call(s32[27,160]{1,0:T(8,128)S(1)} %bitcast.23, s32[27,160]{1,0:T(8,128)S(1)} %bitcast.25, s32[1,160]{1,0:T(1,128)S(1)} %bitcast.28, bf16[27,128,1024]{2,1,0:T(8,128)(2,1)S(1)} %bitcast.21, f32[160,128]{1,0:T(8,128)S(1)} %shard_map.101.start, bf16[160,1024]{1,0:T(8,128)(2,1)S(1)} %collective-permute-done.6.rest_0_, ...), custom_call_target="tpu_custom_call" | custom-call | flops 2972712960 | bytes 7077888 | tf_op jit(solution)/shard_map/pallas_call | solution.py:367
  47.1 0.7 %fusion.13 = f32[160,128]{1,0:T(8,128)} fusion(f32[160,128]{1,0:T(8,128)S(1)} %shard_map.102, f32[4,160,128]{2,1,0:T(8,128)S(1)} %collective-permute-done.9, f16[160,128]{1,0:T(8,128)(2,1)S(1)} %collective-permute-done.12, f16[160,128]{1,0:T(8,128)(2,1)S(1)} %collective-permute-done.11, f16[160,128]{1,0:T(8,128)(2,1)S(1)} %collective-permute-done.10, ...), kind=kLoop, calls=%fused_computation.24 | loop fusion | flops 225280 | bytes 450560 | tf_op jit(solution)/shard_map/add | solution.py:447
  (24 shorter events, 0.1 us)
Async XLA Ops:
  0.0 29.4 %slice-start = ((s8[7077888]{0:T(1024)(128)(4,1)}), s8[4194304]{0:T(1024)(128)(4,1)S(1)}, s32[]{:S(2)}) async-start(s8[7077888]{0:T(1024)(128)(4,1)} %bitcast.20), calls=%async_computation | async-start | bytes 8388608
  1.0 28.4 %slice-start.1 = ((s8[7077888]{0:T(1024)(128)(4,1)}), s8[2883584]{0:T(1024)(128)(4,1)S(1)}, s32[]{:S(2)}) async-start(s8[7077888]{0:T(1024)(128)(4,1)} %bitcast.20), calls=%async_computation.1 | async-start | bytes 5767168
  1.0 28.4 %copy-start = (s32[160,27]{0,1:T(8,128)S(1)}, s32[160,27]{0,1:T(8,128)}, u32[]{:S(2)}) copy-start(s32[160,27]{0,1:T(8,128)} %param.13) | copy-start | bytes 51844
  1.0 28.4 %copy-start.1 = (s32[160,27]{0,1:T(8,128)S(1)}, s32[160,27]{0,1:T(8,128)}, u32[]{:S(2)}) copy-start(s32[160,27]{0,1:T(8,128)} %param.12) | copy-start | bytes 51844
  1.0 28.4 %copy-start.3 = (s32[160]{0:T(256)S(1)}, s32[160]{0:T(256)}, u32[]{:S(2)}) copy-start(s32[160]{0:T(256)} %param.14) | copy-start | bytes 1924
  6.0 3.8 %collective-permute-start = (f32[2,2048]{1,0:T(2,128)S(1)}, f32[2,2048]{1,0:T(2,128)S(1)}, u32[]{:S(2)}, u32[]{:S(2)}) collective-permute-start(f32[2,2048]{1,0:T(2,128)S(1)} %get-tuple-element.20), channel_id=1, source_target_pairs={{0,8},{8,16},{16,24},{24,0},{1,9},{9,17},{17,25},{25,1},{2,10},{10... | collective-permute-start | bytes 49160 | tf_op jit(solution)/shard_map/ppermute | solution.py:398
  8.1 5.2 %collective-permute-start.1 = (f32[2,2048]{1,0:T(2,128)S(1)}, f32[2,2048]{1,0:T(2,128)S(1)}, u32[]{:S(2)}, u32[]{:S(2)}) collective-permute-start(f32[2,2048]{1,0:T(2,128)S(1)} %get-tuple-element.20), channel_id=1, source_target_pairs={{0,16},{8,24},{16,0},{24,8},{1,17},{9,25},{17,1},{25,9},{2,18},{10... | collective-permute-start | bytes 49160 | tf_op jit(solution)/shard_map/ppermute | solution.py:398
  8.9 4.9 %collective-permute-start.2 = (f32[2,2048]{1,0:T(2,128)S(1)}, f32[2,2048]{1,0:T(2,128)S(1)}, u32[]{:S(2)}, u32[]{:S(2)}) collective-permute-start(f32[2,2048]{1,0:T(2,128)S(1)} %get-tuple-element.20), channel_id=1, source_target_pairs={{0,24},{8,0},{16,8},{24,16},{1,25},{9,1},{17,9},{25,17},{2,26},{10... | collective-permute-start | bytes 49160 | tf_op jit(solution)/shard_map/ppermute | solution.py:398
  13.9 12.2 %collective-permute-start.3 = (f32[2,2048]{1,0:T(2,128)S(1)}, f32[2,2048]{1,0:T(2,128)S(1)}, u32[]{:S(2)}, u32[]{:S(2)}) collective-permute-start(f32[2,2048]{1,0:T(2,128)S(1)} %add_add_fusion.1), channel_id=1, source_target_pairs={{0,64},{64,128},{128,192},{192,0},{1,65},{65,129},{129,193},{193,1... | collective-permute-start | bytes 49160 | tf_op jit(solution)/shard_map/ppermute | solution.py:398
  15.5 10.6 %collective-permute-start.4 = (f32[2,2048]{1,0:T(2,128)S(1)}, f32[2,2048]{1,0:T(2,128)S(1)}, u32[]{:S(2)}, u32[]{:S(2)}) collective-permute-start(f32[2,2048]{1,0:T(2,128)S(1)} %add_add_fusion.1), channel_id=1, source_target_pairs={{0,128},{64,192},{128,0},{192,64},{1,129},{65,193},{129,1},{193,65... | collective-permute-start | bytes 49160 | tf_op jit(solution)/shard_map/ppermute | solution.py:398
  18.3 7.8 %collective-permute-start.5 = (f32[2,2048]{1,0:T(2,128)S(1)}, f32[2,2048]{1,0:T(2,128)S(1)}, u32[]{:S(2)}, u32[]{:S(2)}) collective-permute-start(f32[2,2048]{1,0:T(2,128)S(1)} %add_add_fusion.1), channel_id=1, source_target_pairs={{0,192},{64,0},{128,64},{192,128},{1,193},{65,1},{129,65},{193,129... | collective-permute-start | bytes 49160 | tf_op jit(solution)/shard_map/ppermute | solution.py:398
  19.6 16.9 %collective-permute-start.6 = (bf16[160,1024]{1,0:T(8,128)(2,1)}, bf16[160,1024]{1,0:T(8,128)(2,1)S(1)}, u32[]{:S(2)}, u32[]{:S(2)}) collective-permute-start(bf16[160,1024]{1,0:T(8,128)(2,1)} %rest_0_.1), channel_id=1, source_target_pairs={{0,8},{1,253},{2,10},{3,255},{4,12},{5,249},{6,14},{7,251},{8,16},... | collective-permute-start | bytes 983048 | tf_op jit(solution)/shard_map/ppermute | solution.py:423
  26.1 7.9 %collective-permute-start.8 = (f32[2,2048]{1,0:T(2,128)S(1)}, f32[2,2048]{1,0:T(2,128)S(1)}, u32[]{:S(2)}, u32[]{:S(2)}) collective-permute-start(f32[2,2048]{1,0:T(2,128)S(1)} %add_add_fusion.first), channel_id=1, source_target_pairs={{0,32},{32,0},{1,33},{33,1},{2,34},{34,2},{3,35},{35,3},{4,36},{36... | collective-permute-start | bytes 49160 | tf_op jit(solution)/shard_map/ppermute | solution.py:398
  29.5 4.6 %copy-start.2 = (f32[2048]{0:T(1024)S(1)}, f32[2048]{0:T(1024)}, u32[]{:S(2)}) copy-start(f32[2048]{0:T(1024)} %param.18) | copy-start | bytes 24580
  36.4 1.7 %collective-permute-start.9 = (f32[4,160,128]{2,1,0:T(8,128)S(1)}, f32[4,160,128]{2,1,0:T(8,128)S(1)}, u32[]{:S(2)}, u32[]{:S(2)}) collective-permute-start(f32[4,160,128]{2,1,0:T(8,128)S(1)} %get-tuple-element.34), channel_id=1, source_target_pairs={{0,1},{1,0},{2,3},{3,2},{4,5},{5,4},{6,7},{7,6},{8,9},{9,8},{10,11... | collective-permute-start | bytes 983048 | tf_op jit(solution)/shard_map/ppermute | solution.py:440
  36.5 6.1 %collective-permute-start.7 = (bf16[160,1024]{1,0:T(8,128)(2,1)S(1)}, bf16[160,1024]{1,0:T(8,128)(2,1)S(1)}, u32[]{:S(2)}, u32[]{:S(2)}) collective-permute-start(bf16[160,1024]{1,0:T(8,128)(2,1)S(1)} %collective-permute-done.6.rest_0_), channel_id=1, source_target_pairs={{0,1},{1,0},{2,3},{3,2},{4,5},{5,4},{6,7},{7,6},{8,9},{9,8},{10,11... | collective-permute-start | bytes 983048 | tf_op jit(solution)/shard_map/ppermute | solution.py:433
  38.2 8.9 %collective-permute-start.10 = (f16[160,128]{1,0:T(8,128)(2,1)S(1)}, f16[160,128]{1,0:T(8,128)(2,1)S(1)}, u32[]{:S(2)}, u32[]{:S(2)}) collective-permute-start(f16[160,128]{1,0:T(8,128)(2,1)S(1)} %get-tuple-element.35), channel_id=1, source_target_pairs={{0,6},{2,4},{4,2},{6,0},{1,7},{3,5},{5,3},{7,1},{8,14},{10,12},{12... | collective-permute-start | bytes 122888 | tf_op jit(solution)/shard_map/ppermute | solution.py:446
  40.1 7.0 %collective-permute-start.11 = (f16[160,128]{1,0:T(8,128)(2,1)S(1)}, f16[160,128]{1,0:T(8,128)(2,1)S(1)}, u32[]{:S(2)}, u32[]{:S(2)}) collective-permute-start(f16[160,128]{1,0:T(8,128)(2,1)S(1)} %get-tuple-element.37), channel_id=1, source_target_pairs={{0,4},{2,6},{4,0},{6,2},{1,5},{3,7},{5,1},{7,3},{8,12},{10,14},{12... | collective-permute-start | bytes 122888 | tf_op jit(solution)/shard_map/ppermute | solution.py:446
  40.8 6.4 %collective-permute-start.12 = (f16[160,128]{1,0:T(8,128)(2,1)S(1)}, f16[160,128]{1,0:T(8,128)(2,1)S(1)}, u32[]{:S(2)}, u32[]{:S(2)}) collective-permute-start(f16[160,128]{1,0:T(8,128)(2,1)S(1)} %get-tuple-element.36), channel_id=1, source_target_pairs={{0,2},{2,0},{4,6},{6,4},{1,3},{3,1},{5,7},{7,5},{8,10},{10,8},{12,... | collective-permute-start | bytes 122888 | tf_op jit(solution)/shard_map/ppermute | solution.py:446

commit v4 on v3

--- a/solution.py
+++ b/solution.py
@@ -55,7 +55,8 @@
     60.167831693053074, -25.96831316496443, 6.52961023180932,
 )
 MODE_TILE = 512
-CLASS_TILE = 9
+OWN_CLASSES = 4
+HALO_CLASSES = 8
 NT = (((1,), (1,)), ((), ()))
 NN = (((1,), (0,)), ((), ()))
 BLOCK_AXES = ("x", "z_hi", "y")
@@ -296,8 +297,31 @@
     )(first, second, weight, cos_c, sin_c, *waves, *points)
 
 
-def near_kernel(group, is_halo, offsets, atoms_of, counts, near, start, *rest):
-    given, (out, sources, values, picks, made) = rest[:-5], rest[-5:]
+def find_places(offsets, atoms_of, counts, atoms):
+    classes = offsets.shape[0]
+    blocks = lax.axis_size(BLOCK_AXES)
+    shift = atoms_of[...] - (lax.axis_index(BLOCK_AXES) - 1) * atoms
+    shift = jnp.where(shift < 0, shift + blocks * atoms, shift)
+    shift = jnp.where(shift >= blocks * atoms, shift - blocks * atoms, shift)
+    live = lax.broadcasted_iota(jnp.int32, shift.shape, 0) < counts[...]
+    places = jnp.where(live, shift + 1, 0).astype(jnp.float32)
+    of_slot = offsets[...]
+    rows = [
+        jnp.sum(jnp.where(of_slot == one, places, 0.0), axis=0, keepdims=True)
+        for one in range(classes)
+    ]
+    rows.append(jnp.zeros((-classes % 8, atoms), jnp.float32))
+    return jnp.transpose(jnp.concatenate(rows, axis=0))
+
+
+def near_kernel(group, is_halo, *rest):
+    rest, (sources, values, picks, made) = rest[:-4], rest[-4:]
+    if is_halo:
+        (found, near, start), given, out = rest[:3], rest[3:-1], rest[-1]
+    else:
+        (offsets, atoms_of, counts, near, start), given = rest[:5], rest[5:-2]
+        out, found = rest[-2:]
+        found[...] = find_places(offsets, atoms_of, counts, out.shape[0])
     classes, width, count = near.shape
     atoms = out.shape[0]
     used = atoms * len(given)
@@ -305,19 +329,6 @@
     for i, block in enumerate(given):
         sources[i * atoms : (i + 1) * atoms, :] = block[...]
     core = lax.axis_index("core")
-    blocks = lax.axis_size(BLOCK_AXES)
-    shift = atoms_of[...] - (lax.axis_index(BLOCK_AXES) - 1) * atoms
-    shift = jnp.where(shift < 0, shift + blocks * atoms, shift)
-    shift = jnp.where(shift >= blocks * atoms, shift - blocks * atoms, shift)
-    live = lax.broadcasted_iota(jnp.int32, shift.shape, 0) < counts[...]
-    places = jnp.where(live, shift + 1, 0).astype(jnp.float32)
-    of_slot = offsets[...]
-    found = [
-        jnp.sum(jnp.where(of_slot == one, places, 0.0), axis=0, keepdims=True)
-        for one in range(classes)
-    ]
-    found.append(jnp.zeros((-classes % 8, atoms), jnp.float32))
-    found = jnp.transpose(jnp.concatenate(found, axis=0))
     column = lax.broadcasted_iota(jnp.int32, (1, wide), 1)
     if is_halo:
         base = jnp.where(column < atoms, core * 2 * atoms, (1 - core) * 2 * atoms - atoms)
@@ -330,20 +341,24 @@
                 (wide - used, 2 * width), values.dtype
             )
     result = jnp.zeros((atoms, 2 * width), jnp.float32)
-    steps = classes // group
+    steps = -(-classes // group)
     for step in range(steps + 1):
         slot = step % 2
+        size = min(group, classes - step * group)
+        before = group if step < steps else classes - (steps - 1) * group
         if step < steps:
-            block = near[step * group : (step + 1) * group].reshape(group * width, count)
-            made[slot] = dot(sources[...], block, NT)
-            for one in range(group):
+            block = near[step * group : step * group + size].reshape(size * width, count)
+            made[slot, :, : size * width] = dot(sources[...], block, NT)
+            for one in range(size):
                 own_class = step * group + one
                 chosen = jnp.where(found[:, own_class : own_class + 1] == target, 1.0, 0.0)
                 picks[slot, :, one * wide : (one + 1) * wide] = chosen.astype(jnp.bfloat16)
         if step > 0:
-            result = result + dot(picks[1 - slot], values[1 - slot])
+            result = result + dot(
+                picks[1 - slot, :, : before * wide], values[1 - slot, : before * wide]
+            )
         if step < steps:
-            for one in range(group):
+            for one in range(size):
                 high, low = split(made[slot, :, one * width : (one + 1) * width])
                 rows = slice(one * wide, one * wide + used)
                 values[slot, rows, :width] = high
@@ -357,26 +372,28 @@
     out[...] = begin + (result[:, :width] + result[:, width:])
 
 
-def near_part(is_halo, offsets, atoms_of, counts, near, start, given):
-    atoms = offsets.shape[1]
+def near_part(is_halo, lists, near, start, given):
+    atoms = given[0].shape[0]
     classes, width, count = near.shape
-    group = CLASS_TILE if classes % CLASS_TILE == 0 else 1
+    group = min(HALO_CLASSES if is_halo else OWN_CLASSES, classes)
     used = atoms * len(given)
     wide = -(-used // 128) * 128
     bf16, f32 = jnp.bfloat16, jnp.float32
+    out = jax.ShapeDtypeStruct((atoms, width), f32)
+    found = jax.ShapeDtypeStruct((atoms, -(-classes // 8) * 8), f32)
     return pl.pallas_call(
         functools.partial(near_kernel, group, is_halo),
         scratch_shapes=[
             pltpu.VMEM((used, count), bf16), pltpu.VMEM((2, group * wide, 2 * width), bf16),
             pltpu.VMEM((2, atoms, group * wide), bf16), pltpu.VMEM((2, used, group * width), f32),
         ],
-        out_shape=jax.ShapeDtypeStruct((atoms, width), f32),
+        out_shape=out if is_halo else [out, found],
         compiler_params=pltpu.CompilerParams(vmem_limit_bytes=30 * MIB),
         cost_estimate=pl.CostEstimate(
             flops=2 * used * classes * width * (count + 2 * atoms),
             bytes_accessed=2 * classes * width * count, transcendentals=0,
         ),
-    )(offsets, atoms_of, counts, near, start, *given)
+    )(*lists, near, start, *given)
 
 
 def fold_kernel(keep, taken, *outs):
@@ -425,7 +442,7 @@
     partial, cos_c, sin_c, *tables = partial_structure(density, centers, local_points, wavevectors)
 
     lists = (neighbour_offsets.T, neighbour_atoms.T, neighbour_counts[None, :])
-    near_own = near_part(False, *lists, near_blocks, density, [density])
+    near_own, found = near_part(False, lists, near_blocks, density, [density])
 
     structure = sum_over(partial, "y")
     structure = sum_over(structure, "x")
@@ -438,7 +455,7 @@
         tables[:4], tables[4:], chips,
     )
     taken = lax.ppermute(send, "core", [(0, 1), (1, 0)])
-    near_field = near_part(True, *lists, near_blocks, near_own, [halo, halo_other])
+    near_field = near_part(True, [found], near_blocks, near_own, [halo, halo_other])
     far_field = keep[0] + taken[0]
     for by in range(chips - 1, 0, -1):
         swap = [(i, i ^ by) for i in range(chips)]

time: 48.5 us -> 47.8 us (0.986)
  Pallas kernels: 16.2 us -> 15.6 us
    pallas_call x2, Pallas kernels: 8.81 us -> 8.15 us  [near_part(): pl.pallas_call(functools.partial(near_kernel, group, is_halo), scratch_sh...]
  transfers between devices with their start and end apart: 13 -> 13, of which waited for: 5 -> 5; matrix products, arithmetic and copies ran while one was open for 0% -> 0% of each run, Pallas kernels for 23% -> 22%
where the time goes in v4:
time: 47.8 us; the launch traced here: 47.3 us
  starting transfers between devices  23.5 us (49%)
  Pallas kernels  15.6 us (33%)
  waiting for transfers between devices  6.25 us (13%)
  other arithmetic  1.73 us (4%)
    ppermute x7, starting transfers between devices, shifted(): lax.ppermute(value, axis, [(i, (i + by) % count) for i in range(count)])  12.1 us
    pallas_call x2, Pallas kernels, near_part(): pl.pallas_call(functools.partial(near_kernel, group, is_halo), scratch_sh...  8.15 us
    ppermute x1, starting transfers between devices, shards(): halo = lax.ppermute(density, BLOCK_AXES + ('z_lo', 'core'), halo_route)  6.42 us
    ppermute x7, waiting for transfers between devices, shifted(): lax.ppermute(value, axis, [(i, (i + by) % count) for i in range(count)])  5.13 us
    pallas_call x1, Pallas kernels, partial_structure(): pl.pallas_call(functools.partial(structure_kernel, sizes), in_specs=[pl.B...  5.01 us
    ppermute x3, starting transfers between devices, shards(): lax.ppermute(piece, 'z_lo', swap).astype(jnp.float32) * 32.0  4.47 us
    pallas_call x1, Pallas kernels, far_partial(): pl.pallas_call(functools.partial(far_kernel, normalizer), out_shape=[jax....  2.4 us
    ppermute x1, waiting for transfers between devices, shards(): taken = lax.ppermute(send, 'core', [(0, 1), (1, 0)])  1.11 us
  transfers between devices with their start and end apart: 13, of which 5 were waited for; matrix products, arithmetic and copies ran while one was open for 0% of the time, Pallas kernels for 22%

profile of v4, /device:TPU:24, one launch (start us, length us, event | category | flops | bytes accessed | tf_op | source)
XLA Modules:
  0.0 47.3 jit_solution(7761677863017117504)
XLA Ops:
  0.0 1.0 %fusion.packed = f32[16,3840]{1,0:T(8,128)S(1)} fusion(f32[2,160]{1,0:T(2,128)} %param.15, f32[2,1024]{1,0:T(2,128)} %param.16, f32[2,2048]{1,0:T(2,128)} %param.17, f32[16,512]{1,0:T(8,128)} %constant.9.clone), kind=kLoop, calls=%fused_computation.5 | loop fusion | flops 798720 | bytes 304384 | tf_op jit(solution)/shard_map/concatenate | solution.py:222
  1.0 5.0 %shard_map.101 = (f32[2,2048]{1,0:T(2,128)S(1)}, f32[160,2048]{1,0:T(8,128)S(1)}, f32[160,2048]{1,0:T(8,128)S(1)}, bf16[192,2048]{1,0:T(8,128)(2,1)S(1)}, bf16[1...) custom-call(bf16[160,1024]{1,0:T(8,128)(2,1)} %density_far.1, ...), custom_call_target="tpu_custom_call" | custom-call | flops 8053063680 | bytes 2621440 | tf_op jit(solution)/shard_map/pallas_call | solution.py:226
  6.0 2.0 %collective-permute-start = (f32[2,2048]{1,0:T(2,128)S(1)}, f32[2,2048]{1,0:T(2,128)S(1)}, u32[]{:S(2)}, u32[]{:S(2)}) collective-permute-start(f32[2,2048]{1,0:T(2,128)S(1)} %get-tuple-element.23), channel_id=1, source_target_pairs={{0,8},{8,16},{16,24},{24,0},{1,9},{9,17},{17,25},{25,1},{2,10},{10... | collective-permute-start | bytes 49160 | tf_op jit(solution)/shard_map/ppermute | solution.py:415
  8.1 0.8 %collective-permute-start.1 = (f32[2,2048]{1,0:T(2,128)S(1)}, f32[2,2048]{1,0:T(2,128)S(1)}, u32[]{:S(2)}, u32[]{:S(2)}) collective-permute-start(f32[2,2048]{1,0:T(2,128)S(1)} %get-tuple-element.23), channel_id=1, source_target_pairs={{0,16},{8,24},{16,0},{24,8},{1,17},{9,25},{17,1},{25,9},{2,18},{10... | collective-permute-start | bytes 49160 | tf_op jit(solution)/shard_map/ppermute | solution.py:415
  8.9 0.1 collective-permute-start.2
  9.0 0.8 %collective-permute-done = f32[2,2048]{1,0:T(2,128)S(1)} collective-permute-done((f32[2,2048]{1,0:T(2,128)S(1)}, f32[2,2048]{1,0:T(2,128)S(1)}, u32[]{:S(2)}, u32[]{:S(2)}) %collective-permute-start) | collective-permute-done | bytes 16416 | tf_op jit(solution)/shard_map/ppermute | solution.py:415
  9.9 3.5 %collective-permute-done.1 = f32[2,2048]{1,0:T(2,128)S(1)} collective-permute-done((f32[2,2048]{1,0:T(2,128)S(1)}, f32[2,2048]{1,0:T(2,128)S(1)}, u32[]{:S(2)}, u32[]{:S(2)}) %collective-permute-start.1) | collective-permute-done | bytes 16416 | tf_op jit(solution)/shard_map/ppermute | solution.py:415
  13.3 0.6 %collective-permute-done.2 = f32[2,2048]{1,0:T(2,128)S(1)} collective-permute-done((f32[2,2048]{1,0:T(2,128)S(1)}, f32[2,2048]{1,0:T(2,128)S(1)}, u32[]{:S(2)}, u32[]{:S(2)}) %collective-permute-start.2) | collective-permute-done | bytes 16416 | tf_op jit(solution)/shard_map/ppermute | solution.py:415
  13.9 1.6 %collective-permute-start.3 = (f32[2,2048]{1,0:T(2,128)S(1)}, f32[2,2048]{1,0:T(2,128)S(1)}, u32[]{:S(2)}, u32[]{:S(2)}) collective-permute-start(f32[2,2048]{1,0:T(2,128)S(1)} %add_add_fusion.1), channel_id=1, source_target_pairs={{0,64},{64,128},{128,192},{192,0},{1,65},{65,129},{129,193},{193,1... | collective-permute-start | bytes 49160 | tf_op jit(solution)/shard_map/ppermute | solution.py:415
  15.5 2.8 %collective-permute-start.4 = (f32[2,2048]{1,0:T(2,128)S(1)}, f32[2,2048]{1,0:T(2,128)S(1)}, u32[]{:S(2)}, u32[]{:S(2)}) collective-permute-start(f32[2,2048]{1,0:T(2,128)S(1)} %add_add_fusion.1), channel_id=1, source_target_pairs={{0,128},{64,192},{128,0},{192,64},{1,129},{65,193},{129,1},{193,65... | collective-permute-start | bytes 49160 | tf_op jit(solution)/shard_map/ppermute | solution.py:415
  18.3 1.4 %collective-permute-start.5 = (f32[2,2048]{1,0:T(2,128)S(1)}, f32[2,2048]{1,0:T(2,128)S(1)}, u32[]{:S(2)}, u32[]{:S(2)}) collective-permute-start(f32[2,2048]{1,0:T(2,128)S(1)} %add_add_fusion.1), channel_id=1, source_target_pairs={{0,192},{64,0},{128,64},{192,128},{1,193},{65,1},{129,65},{193,129... | collective-permute-start | bytes 49160 | tf_op jit(solution)/shard_map/ppermute | solution.py:415
  19.6 6.4 %collective-permute-start.6 = (bf16[160,1024]{1,0:T(8,128)(2,1)}, bf16[160,1024]{1,0:T(8,128)(2,1)S(1)}, u32[]{:S(2)}, u32[]{:S(2)}) collective-permute-start(bf16[160,1024]{1,0:T(8,128)(2,1)} %density_far.1), channel_id=1, source_target_pairs={{0,8},{1,253},{2,10},{3,255},{4,12},{5,249},{6,14},{7,251},{8,16},... | collective-permute-start | bytes 983048 | tf_op jit(solution)/shard_map/ppermute | solution.py:440
  26.1 3.3 %collective-permute-start.8 = (f32[2,2048]{1,0:T(2,128)S(1)}, f32[2,2048]{1,0:T(2,128)S(1)}, u32[]{:S(2)}, u32[]{:S(2)}) collective-permute-start(f32[2,2048]{1,0:T(2,128)S(1)} %add_add_fusion.first), channel_id=1, source_target_pairs={{0,32},{32,0},{1,33},{33,1},{2,34},{34,2},{3,35},{35,3},{4,36},{36... | collective-permute-start | bytes 49160 | tf_op jit(solution)/shard_map/ppermute | solution.py:415
  29.5 4.3 %shard_map.100 = (f32[160,128]{1,0:T(8,128)S(1)}, f32[160,32]{1,0:T(8,128)S(1)}) custom-call(s32[27,160]{1,0:T(8,128)S(1)} %bitcast.22, s32[27,160]{1,0:T(8,128)S(1)} %bitcast.23, s32[1,160]{1,0:T(1,128)S(1)} %bitcast.25, bf16[27,128,1024]{2,1,0:T(8,128)(2,1)S(1)} %bitcast.21, bf16[160,1024]{1,0:T(8,128)(2,1)} %density_far.1, bf16[160,1024]{1,0:T(8,128)(2,1)} %density_far.1), custom_call_target="tpu_custom_call" | custom-call | flops 1486356480 | bytes 7077888 | tf_op jit(solution)/shard_map/pallas_call | solution.py:384
  33.7 0.3 collective-permute-done.8.second
  34.0 2.4 %shard_map.103 = (f32[4,160,128]{2,1,0:T(8,128)S(1)}, f32[4,160,128]{2,1,0:T(8,128)S(1)}) custom-call(f32[2,2048]{1,0:T(2,128)S(1)} %add_add_fusion.first, f32[2,2048]{1,0:T(2,128)S(1)} %collective-permute-done.8.second, f32[1,2048]{1,0:T(1,128)S(1)} %bitcast.24, f32[160,2048]{1,0:T(8,128)S(1)} %get-tuple-element.27.cos_c, ...), custom_call_target="tpu_custom_call" | custom-call | flops 1132462080 | bytes 2621440 | tf_op jit(solution)/shard_map/pallas_call | solution.py:287
  36.4 0.1 collective-permute-start.9
  36.5 0.5 %collective-permute-start.7 = (bf16[160,1024]{1,0:T(8,128)(2,1)S(1)}, bf16[160,1024]{1,0:T(8,128)(2,1)S(1)}, u32[]{:S(2)}, u32[]{:S(2)}) collective-permute-start(bf16[160,1024]{1,0:T(8,128)(2,1)S(1)} %collective-permute-done.6.rest_3_), channel_id=1, source_target_pairs={{0,1},{1,0},{2,3},{3,2},{4,5},{5,4},{6,7},{7,6},{8,9},{9,8},{10,11... | collective-permute-start | bytes 983048 | tf_op jit(solution)/shard_map/ppermute | solution.py:450
  37.0 1.1 %collective-permute-done.9 = f32[4,160,128]{2,1,0:T(8,128)S(1)} collective-permute-done((f32[4,160,128]{2,1,0:T(8,128)S(1)}, f32[4,160,128]{2,1,0:T(8,128)S(1)}, u32[]{:S(2)}, u32[]{:S(2)}) %collective-permute-start.9) | collective-permute-done | bytes 327712 | tf_op jit(solution)/shard_map/ppermute | solution.py:457
  38.2 2.0 %collective-permute-start.10 = (f16[160,128]{1,0:T(8,128)(2,1)S(1)}, f16[160,128]{1,0:T(8,128)(2,1)S(1)}, u32[]{:S(2)}, u32[]{:S(2)}) collective-permute-start(f16[160,128]{1,0:T(8,128)(2,1)S(1)} %get-tuple-element.39), channel_id=1, source_target_pairs={{0,6},{2,4},{4,2},{6,0},{1,7},{3,5},{5,3},{7,1},{8,14},{10,12},{12... | collective-permute-start | bytes 122888 | tf_op jit(solution)/shard_map/ppermute | solution.py:463
  40.1 0.6 %collective-permute-start.11 = (f16[160,128]{1,0:T(8,128)(2,1)S(1)}, f16[160,128]{1,0:T(8,128)(2,1)S(1)}, u32[]{:S(2)}, u32[]{:S(2)}) collective-permute-start(f16[160,128]{1,0:T(8,128)(2,1)S(1)} %get-tuple-element.41), channel_id=1, source_target_pairs={{0,4},{2,6},{4,0},{6,2},{1,5},{3,7},{5,1},{7,3},{8,12},{10,14},{12... | collective-permute-start | bytes 122888 | tf_op jit(solution)/shard_map/ppermute | solution.py:463
  40.8 1.9 %collective-permute-start.12 = (f16[160,128]{1,0:T(8,128)(2,1)S(1)}, f16[160,128]{1,0:T(8,128)(2,1)S(1)}, u32[]{:S(2)}, u32[]{:S(2)}) collective-permute-start(f16[160,128]{1,0:T(8,128)(2,1)S(1)} %get-tuple-element.40), channel_id=1, source_target_pairs={{0,2},{2,0},{4,6},{6,4},{1,3},{3,1},{5,7},{7,5},{8,10},{10,8},{12,... | collective-permute-start | bytes 122888 | tf_op jit(solution)/shard_map/ppermute | solution.py:463
  42.7 3.9 %shard_map.102 = f32[160,128]{1,0:T(8,128)S(1)} custom-call(f32[160,32]{1,0:T(8,128)S(1)} %get-tuple-element.22.rest_0_, bf16[27,128,1024]{2,1,0:T(8,128)(2,1)S(1)} %bitcast.21, f32[160,128]{1,0:T(8,128)S(1)} %get-tuple-element.25.rest_2_, bf16[160,1024]{1,0:T(8,128)(2,1)S(1)} %collective-permute-done.6.rest_3_, ...), custom_call_target="tpu_custom_call" | custom-call | flops 2972712960 | bytes 7077888 | tf_op jit(solution)/shard_map/pallas_call | solution.py:384
  46.6 0.7 %fusion.13 = f32[160,128]{1,0:T(8,128)} fusion(f32[160,128]{1,0:T(8,128)S(1)} %shard_map.102, f32[4,160,128]{2,1,0:T(8,128)S(1)} %collective-permute-done.9, f16[160,128]{1,0:T(8,128)(2,1)S(1)} %collective-permute-done.12, f16[160,128]{1,0:T(8,128)(2,1)S(1)} %collective-permute-done.11, f16[160,128]{1,0:T(8,128)(2,1)S(1)} %collective-permute-done.10, ...), kind=kLoop, calls=%fused_computation.24 | loop fusion | flops 225280 | bytes 450560 | tf_op jit(solution)/shard_map/add | solution.py:464
  (24 shorter events, 0.1 us)
Async XLA Ops:
  0.0 29.4 %slice-start = ((s8[7077888]{0:T(1024)(128)(4,1)}), s8[4194304]{0:T(1024)(128)(4,1)S(1)}, s32[]{:S(2)}) async-start(s8[7077888]{0:T(1024)(128)(4,1)} %bitcast.20), calls=%async_computation | async-start | bytes 8388608
  1.0 28.4 %slice-start.1 = ((s8[7077888]{0:T(1024)(128)(4,1)}), s8[2883584]{0:T(1024)(128)(4,1)S(1)}, s32[]{:S(2)}) async-start(s8[7077888]{0:T(1024)(128)(4,1)} %bitcast.20), calls=%async_computation.1 | async-start | bytes 5767168
  1.0 28.4 %copy-start = (s32[160,27]{0,1:T(8,128)S(1)}, s32[160,27]{0,1:T(8,128)}, u32[]{:S(2)}) copy-start(s32[160,27]{0,1:T(8,128)} %param.13) | copy-start | bytes 51844
  1.0 28.4 %copy-start.1 = (s32[160,27]{0,1:T(8,128)S(1)}, s32[160,27]{0,1:T(8,128)}, u32[]{:S(2)}) copy-start(s32[160,27]{0,1:T(8,128)} %param.12) | copy-start | bytes 51844
  1.0 28.4 %copy-start.3 = (s32[160]{0:T(256)S(1)}, s32[160]{0:T(256)}, u32[]{:S(2)}) copy-start(s32[160]{0:T(256)} %param.14) | copy-start | bytes 1924
  6.0 3.8 %collective-permute-start = (f32[2,2048]{1,0:T(2,128)S(1)}, f32[2,2048]{1,0:T(2,128)S(1)}, u32[]{:S(2)}, u32[]{:S(2)}) collective-permute-start(f32[2,2048]{1,0:T(2,128)S(1)} %get-tuple-element.23), channel_id=1, source_target_pairs={{0,8},{8,16},{16,24},{24,0},{1,9},{9,17},{17,25},{25,1},{2,10},{10... | collective-permute-start | bytes 49160 | tf_op jit(solution)/shard_map/ppermute | solution.py:415
  8.1 5.2 %collective-permute-start.1 = (f32[2,2048]{1,0:T(2,128)S(1)}, f32[2,2048]{1,0:T(2,128)S(1)}, u32[]{:S(2)}, u32[]{:S(2)}) collective-permute-start(f32[2,2048]{1,0:T(2,128)S(1)} %get-tuple-element.23), channel_id=1, source_target_pairs={{0,16},{8,24},{16,0},{24,8},{1,17},{9,25},{17,1},{25,9},{2,18},{10... | collective-permute-start | bytes 49160 | tf_op jit(solution)/shard_map/ppermute | solution.py:415
  8.9 4.9 %collective-permute-start.2 = (f32[2,2048]{1,0:T(2,128)S(1)}, f32[2,2048]{1,0:T(2,128)S(1)}, u32[]{:S(2)}, u32[]{:S(2)}) collective-permute-start(f32[2,2048]{1,0:T(2,128)S(1)} %get-tuple-element.23), channel_id=1, source_target_pairs={{0,24},{8,0},{16,8},{24,16},{1,25},{9,1},{17,9},{25,17},{2,26},{10... | collective-permute-start | bytes 49160 | tf_op jit(solution)/shard_map/ppermute | solution.py:415
  13.9 12.2 %collective-permute-start.3 = (f32[2,2048]{1,0:T(2,128)S(1)}, f32[2,2048]{1,0:T(2,128)S(1)}, u32[]{:S(2)}, u32[]{:S(2)}) collective-permute-start(f32[2,2048]{1,0:T(2,128)S(1)} %add_add_fusion.1), channel_id=1, source_target_pairs={{0,64},{64,128},{128,192},{192,0},{1,65},{65,129},{129,193},{193,1... | collective-permute-start | bytes 49160 | tf_op jit(solution)/shard_map/ppermute | solution.py:415
  15.5 10.6 %collective-permute-start.4 = (f32[2,2048]{1,0:T(2,128)S(1)}, f32[2,2048]{1,0:T(2,128)S(1)}, u32[]{:S(2)}, u32[]{:S(2)}) collective-permute-start(f32[2,2048]{1,0:T(2,128)S(1)} %add_add_fusion.1), channel_id=1, source_target_pairs={{0,128},{64,192},{128,0},{192,64},{1,129},{65,193},{129,1},{193,65... | collective-permute-start | bytes 49160 | tf_op jit(solution)/shard_map/ppermute | solution.py:415
  18.3 7.8 %collective-permute-start.5 = (f32[2,2048]{1,0:T(2,128)S(1)}, f32[2,2048]{1,0:T(2,128)S(1)}, u32[]{:S(2)}, u32[]{:S(2)}) collective-permute-start(f32[2,2048]{1,0:T(2,128)S(1)} %add_add_fusion.1), channel_id=1, source_target_pairs={{0,192},{64,0},{128,64},{192,128},{1,193},{65,1},{129,65},{193,129... | collective-permute-start | bytes 49160 | tf_op jit(solution)/shard_map/ppermute | solution.py:415
  19.6 16.9 %collective-permute-start.6 = (bf16[160,1024]{1,0:T(8,128)(2,1)}, bf16[160,1024]{1,0:T(8,128)(2,1)S(1)}, u32[]{:S(2)}, u32[]{:S(2)}) collective-permute-start(bf16[160,1024]{1,0:T(8,128)(2,1)} %density_far.1), channel_id=1, source_target_pairs={{0,8},{1,253},{2,10},{3,255},{4,12},{5,249},{6,14},{7,251},{8,16},... | collective-permute-start | bytes 983048 | tf_op jit(solution)/shard_map/ppermute | solution.py:440
  26.1 7.9 %collective-permute-start.8 = (f32[2,2048]{1,0:T(2,128)S(1)}, f32[2,2048]{1,0:T(2,128)S(1)}, u32[]{:S(2)}, u32[]{:S(2)}) collective-permute-start(f32[2,2048]{1,0:T(2,128)S(1)} %add_add_fusion.first), channel_id=1, source_target_pairs={{0,32},{32,0},{1,33},{33,1},{2,34},{34,2},{3,35},{35,3},{4,36},{36... | collective-permute-start | bytes 49160 | tf_op jit(solution)/shard_map/ppermute | solution.py:415
  29.5 4.6 %copy-start.2 = (f32[2048]{0:T(1024)S(1)}, f32[2048]{0:T(1024)}, u32[]{:S(2)}) copy-start(f32[2048]{0:T(1024)} %param.18) | copy-start | bytes 24580
  36.4 1.7 %collective-permute-start.9 = (f32[4,160,128]{2,1,0:T(8,128)S(1)}, f32[4,160,128]{2,1,0:T(8,128)S(1)}, u32[]{:S(2)}, u32[]{:S(2)}) collective-permute-start(f32[4,160,128]{2,1,0:T(8,128)S(1)} %get-tuple-element.38), channel_id=1, source_target_pairs={{0,1},{1,0},{2,3},{3,2},{4,5},{5,4},{6,7},{7,6},{8,9},{9,8},{10,11... | collective-permute-start | bytes 983048 | tf_op jit(solution)/shard_map/ppermute | solution.py:457
  36.5 6.1 %collective-permute-start.7 = (bf16[160,1024]{1,0:T(8,128)(2,1)S(1)}, bf16[160,1024]{1,0:T(8,128)(2,1)S(1)}, u32[]{:S(2)}, u32[]{:S(2)}) collective-permute-start(bf16[160,1024]{1,0:T(8,128)(2,1)S(1)} %collective-permute-done.6.rest_3_), channel_id=1, source_target_pairs={{0,1},{1,0},{2,3},{3,2},{4,5},{5,4},{6,7},{7,6},{8,9},{9,8},{10,11... | collective-permute-start | bytes 983048 | tf_op jit(solution)/shard_map/ppermute | solution.py:450
  38.2 8.4 %collective-permute-start.10 = (f16[160,128]{1,0:T(8,128)(2,1)S(1)}, f16[160,128]{1,0:T(8,128)(2,1)S(1)}, u32[]{:S(2)}, u32[]{:S(2)}) collective-permute-start(f16[160,128]{1,0:T(8,128)(2,1)S(1)} %get-tuple-element.39), channel_id=1, source_target_pairs={{0,6},{2,4},{4,2},{6,0},{1,7},{3,5},{5,3},{7,1},{8,14},{10,12},{12... | collective-permute-start | bytes 122888 | tf_op jit(solution)/shard_map/ppermute | solution.py:463
  40.1 6.4 %collective-permute-start.11 = (f16[160,128]{1,0:T(8,128)(2,1)S(1)}, f16[160,128]{1,0:T(8,128)(2,1)S(1)}, u32[]{:S(2)}, u32[]{:S(2)}) collective-permute-start(f16[160,128]{1,0:T(8,128)(2,1)S(1)} %get-tuple-element.41), channel_id=1, source_target_pairs={{0,4},{2,6},{4,0},{6,2},{1,5},{3,7},{5,1},{7,3},{8,12},{10,14},{12... | collective-permute-start | bytes 122888 | tf_op jit(solution)/shard_map/ppermute | solution.py:463
  40.8 5.8 %collective-permute-start.12 = (f16[160,128]{1,0:T(8,128)(2,1)S(1)}, f16[160,128]{1,0:T(8,128)(2,1)S(1)}, u32[]{:S(2)}, u32[]{:S(2)}) collective-permute-start(f16[160,128]{1,0:T(8,128)(2,1)S(1)} %get-tuple-element.40), channel_id=1, source_target_pairs={{0,2},{2,0},{4,6},{6,4},{1,3},{3,1},{5,7},{7,5},{8,10},{10,8},{12,... | collective-permute-start | bytes 122888 | tf_op jit(solution)/shard_map/ppermute | solution.py:463

commit v5 on v4

--- a/solution.py
+++ b/solution.py
@@ -162,9 +162,9 @@
 
 def structure_kernel(
     sizes, density_far, packed,
-    partial, cos_out, sin_out, wave_c_high, wave_c_low, wave_s_high, wave_s_low,
+    density, partial, cos_out, sin_out, wave_c_high, wave_c_low, wave_s_high, wave_s_low,
     point_c_high, point_c_low, point_s_high, point_s_low,
-    density, form_c, form_s, arrived,
+    form_c, form_s, arrived,
 ):
     copy = pltpu.make_async_copy(density_far, density, arrived)
     copy.start()
@@ -226,10 +226,9 @@
     return pl.pallas_call(
         functools.partial(structure_kernel, sizes),
         in_specs=[pl.BlockSpec(memory_space=pltpu.HBM), pl.BlockSpec(memory_space=pltpu.VMEM)],
-        out_shape=[out((2, modes), f32)] + [out((atoms, modes), f32)] * 2
+        out_shape=[out((atoms, count), bf16), out((2, modes), f32)] + [out((atoms, modes), f32)] * 2
         + [out((rows, modes), bf16)] * 4 + [out((rows, count), bf16)] * 4,
-        scratch_shapes=[pltpu.VMEM((atoms, count), bf16)]
-        + [pltpu.VMEM((atoms, modes), f32)] * 2 + [pltpu.SemaphoreType.DMA],
+        scratch_shapes=[pltpu.VMEM((atoms, modes), f32)] * 2 + [pltpu.SemaphoreType.DMA],
         compiler_params=pltpu.CompilerParams(vmem_limit_bytes=30 * MIB),
         cost_estimate=pl.CostEstimate(
             flops=16 * atoms * rows * (count * 4 + modes * 6),
@@ -319,7 +318,7 @@
     if is_halo:
         (found, near, start), given, out = rest[:3], rest[3:-1], rest[-1]
     else:
-        (offsets, atoms_of, counts, near, start), given = rest[:5], rest[5:-2]
+        (offsets, atoms_of, counts, near), given = rest[:4], rest[4:-2]
         out, found = rest[-2:]
         found[...] = find_places(offsets, atoms_of, counts, out.shape[0])
     classes, width, count = near.shape
@@ -368,7 +367,7 @@
     else:
         member = lax.axis_index("z_lo") * 2 + core
         mine = pl.multiple_of(member * width, width)
-        begin = 0.5 * start[:, pl.ds(mine, width)].astype(jnp.float32)
+        begin = 0.5 * given[0][:, pl.ds(mine, width)].astype(jnp.float32)
     out[...] = begin + (result[:, :width] + result[:, width:])
 
 
@@ -393,7 +392,7 @@
             flops=2 * used * classes * width * (count + 2 * atoms),
             bytes_accessed=2 * classes * width * count, transcendentals=0,
         ),
-    )(*lists, near, start, *given)
+    )(*lists, near, *start, *given)
 
 
 def fold_kernel(keep, taken, *outs):
@@ -439,10 +438,10 @@
                 halo_route.append(((source * chips + chip) * 2 + core, (target * chips + to) * 2 + core))
     halo = lax.ppermute(density, BLOCK_AXES + ("z_lo", "core"), halo_route)
 
-    partial, cos_c, sin_c, *tables = partial_structure(density, centers, local_points, wavevectors)
+    own, partial, cos_c, sin_c, *tables = partial_structure(density, centers, local_points, wavevectors)
 
     lists = (neighbour_offsets.T, neighbour_atoms.T, neighbour_counts[None, :])
-    near_own, found = near_part(False, lists, near_blocks, density, [density])
+    near_own, found = near_part(False, lists, near_blocks, [], [own])
 
     structure = sum_over(partial, "y")
     structure = sum_over(structure, "x")
@@ -455,7 +454,7 @@
         tables[:4], tables[4:], chips,
     )
     taken = lax.ppermute(send, "core", [(0, 1), (1, 0)])
-    near_field = near_part(True, [found], near_blocks, near_own, [halo, halo_other])
+    near_field = near_part(True, [found], near_blocks, [near_own], [halo, halo_other])
     far_field = keep[0] + taken[0]
     for by in range(chips - 1, 0, -1):
         swap = [(i, i ^ by) for i in range(chips)]

time: 47.8 us -> 47.5 us (level)
  Pallas kernels: 15.6 us -> 14.3 us
  waiting for transfers between devices: 6.25 us -> 7.37 us
    pallas_call x2, Pallas kernels: 8.15 us -> 6.96 us  [near_part(): pl.pallas_call(functools.partial(near_kernel, group, is_halo), scratch_sh...]
    ppermute x7, waiting for transfers between devices: 5.13 us -> 6.25 us  [shifted(): lax.ppermute(value, axis, [(i, (i + by) % count) for i in range(count)])]
  transfers between devices with their start and end apart: 13 -> 13, of which waited for: 5 -> 5; matrix products, arithmetic and copies ran while one was open for 0% -> 0% of each run, Pallas kernels for 22% -> 20%
where the time goes in v5:
time: 47.5 us; the launch traced here: 47.1 us
  starting transfers between devices  23.5 us (49%)
  Pallas kernels  14.3 us (30%)
  waiting for transfers between devices  7.37 us (16%)
  other arithmetic  1.72 us (4%)
    ppermute x7, starting transfers between devices, shifted(): lax.ppermute(value, axis, [(i, (i + by) % count) for i in range(count)])  12 us
    pallas_call x2, Pallas kernels, near_part(): pl.pallas_call(functools.partial(near_kernel, group, is_halo), scratch_sh...  6.96 us
    ppermute x1, starting transfers between devices, shards(): halo = lax.ppermute(density, BLOCK_AXES + ('z_lo', 'core'), halo_route)  6.42 us
    ppermute x7, waiting for transfers between devices, shifted(): lax.ppermute(value, axis, [(i, (i + by) % count) for i in range(count)])  6.25 us
    pallas_call x1, Pallas kernels, partial_structure(): pl.pallas_call(functools.partial(structure_kernel, sizes), in_specs=[pl.B...  4.95 us
    ppermute x3, starting transfers between devices, shards(): lax.ppermute(piece, 'z_lo', swap).astype(jnp.float32) * 32.0  4.47 us
    pallas_call x1, Pallas kernels, far_partial(): pl.pallas_call(functools.partial(far_kernel, normalizer), out_shape=[jax....  2.42 us
    ppermute x1, waiting for transfers between devices, shards(): taken = lax.ppermute(send, 'core', [(0, 1), (1, 0)])  1.11 us
  transfers between devices with their start and end apart: 13, of which 5 were waited for; matrix products, arithmetic and copies ran while one was open for 0% of the time, Pallas kernels for 20%

profile of v5, /device:TPU:24, one launch (start us, length us, event | category | flops | bytes accessed | tf_op | source)
XLA Modules:
  0.0 47.1 jit_solution(687886252615020058)
XLA Ops:
  0.0 1.0 %fusion.packed = f32[16,3840]{1,0:T(8,128)S(1)} fusion(f32[2,160]{1,0:T(2,128)} %param.15, f32[2,1024]{1,0:T(2,128)} %param.16, f32[2,2048]{1,0:T(2,128)} %param.17, f32[16,512]{1,0:T(8,128)} %constant.9.clone), kind=kLoop, calls=%fused_computation.5 | loop fusion | flops 798720 | bytes 304384 | tf_op jit(solution)/shard_map/concatenate | solution.py:222
  1.0 4.9 %shard_map.100 = (bf16[160,1024]{1,0:T(8,128)(2,1)S(1)}, f32[2,2048]{1,0:T(2,128)S(1)}, f32[160,2048]{1,0:T(8,128)S(1)}, f32[160,2048]{1,0:T(8,128)S(1)}, bf16[1...) custom-call(bf16[160,1024]{1,0:T(8,128)(2,1)} %density_far.1, ...), custom_call_target="tpu_custom_call" | custom-call | flops 8053063680 | bytes 2621440 | tf_op jit(solution)/shard_map/pallas_call | solution.py:226
  6.0 2.0 %collective-permute-start = (f32[2,2048]{1,0:T(2,128)S(1)}, f32[2,2048]{1,0:T(2,128)S(1)}, u32[]{:S(2)}, u32[]{:S(2)}) collective-permute-start(f32[2,2048]{1,0:T(2,128)S(1)} %get-tuple-element.25), channel_id=1, source_target_pairs={{0,8},{8,16},{16,24},{24,0},{1,9},{9,17},{17,25},{25,1},{2,10},{10... | collective-permute-start | bytes 49160 | tf_op jit(solution)/shard_map/ppermute | solution.py:414
  8.0 0.9 %collective-permute-start.1 = (f32[2,2048]{1,0:T(2,128)S(1)}, f32[2,2048]{1,0:T(2,128)S(1)}, u32[]{:S(2)}, u32[]{:S(2)}) collective-permute-start(f32[2,2048]{1,0:T(2,128)S(1)} %get-tuple-element.25), channel_id=1, source_target_pairs={{0,16},{8,24},{16,0},{24,8},{1,17},{9,25},{17,1},{25,9},{2,18},{10... | collective-permute-start | bytes 49160 | tf_op jit(solution)/shard_map/ppermute | solution.py:414
  8.9 0.1 collective-permute-start.2
  9.0 0.8 %collective-permute-done = f32[2,2048]{1,0:T(2,128)S(1)} collective-permute-done((f32[2,2048]{1,0:T(2,128)S(1)}, f32[2,2048]{1,0:T(2,128)S(1)}, u32[]{:S(2)}, u32[]{:S(2)}) %collective-permute-start) | collective-permute-done | bytes 16416 | tf_op jit(solution)/shard_map/ppermute | solution.py:414
  9.8 3.5 %collective-permute-done.1 = f32[2,2048]{1,0:T(2,128)S(1)} collective-permute-done((f32[2,2048]{1,0:T(2,128)S(1)}, f32[2,2048]{1,0:T(2,128)S(1)}, u32[]{:S(2)}, u32[]{:S(2)}) %collective-permute-start.1) | collective-permute-done | bytes 16416 | tf_op jit(solution)/shard_map/ppermute | solution.py:414
  13.3 0.6 %collective-permute-done.2 = f32[2,2048]{1,0:T(2,128)S(1)} collective-permute-done((f32[2,2048]{1,0:T(2,128)S(1)}, f32[2,2048]{1,0:T(2,128)S(1)}, u32[]{:S(2)}, u32[]{:S(2)}) %collective-permute-start.2) | collective-permute-done | bytes 16416 | tf_op jit(solution)/shard_map/ppermute | solution.py:414
  13.8 1.6 %collective-permute-start.3 = (f32[2,2048]{1,0:T(2,128)S(1)}, f32[2,2048]{1,0:T(2,128)S(1)}, u32[]{:S(2)}, u32[]{:S(2)}) collective-permute-start(f32[2,2048]{1,0:T(2,128)S(1)} %add_add_fusion.1), channel_id=1, source_target_pairs={{0,64},{64,128},{128,192},{192,0},{1,65},{65,129},{129,193},{193,1... | collective-permute-start | bytes 49160 | tf_op jit(solution)/shard_map/ppermute | solution.py:414
  15.4 2.8 %collective-permute-start.4 = (f32[2,2048]{1,0:T(2,128)S(1)}, f32[2,2048]{1,0:T(2,128)S(1)}, u32[]{:S(2)}, u32[]{:S(2)}) collective-permute-start(f32[2,2048]{1,0:T(2,128)S(1)} %add_add_fusion.1), channel_id=1, source_target_pairs={{0,128},{64,192},{128,0},{192,64},{1,129},{65,193},{129,1},{193,65... | collective-permute-start | bytes 49160 | tf_op jit(solution)/shard_map/ppermute | solution.py:414
  18.2 1.4 %collective-permute-start.5 = (f32[2,2048]{1,0:T(2,128)S(1)}, f32[2,2048]{1,0:T(2,128)S(1)}, u32[]{:S(2)}, u32[]{:S(2)}) collective-permute-start(f32[2,2048]{1,0:T(2,128)S(1)} %add_add_fusion.1), channel_id=1, source_target_pairs={{0,192},{64,0},{128,64},{192,128},{1,193},{65,1},{129,65},{193,129... | collective-permute-start | bytes 49160 | tf_op jit(solution)/shard_map/ppermute | solution.py:414
  19.6 6.4 %collective-permute-start.6 = (bf16[160,1024]{1,0:T(8,128)(2,1)}, bf16[160,1024]{1,0:T(8,128)(2,1)S(1)}, u32[]{:S(2)}, u32[]{:S(2)}) collective-permute-start(bf16[160,1024]{1,0:T(8,128)(2,1)} %density_far.1), channel_id=1, source_target_pairs={{0,8},{1,253},{2,10},{3,255},{4,12},{5,249},{6,14},{7,251},{8,16},... | collective-permute-start | bytes 983048 | tf_op jit(solution)/shard_map/ppermute | solution.py:439
  26.0 3.3 %collective-permute-start.8 = (f32[2,2048]{1,0:T(2,128)S(1)}, f32[2,2048]{1,0:T(2,128)S(1)}, u32[]{:S(2)}, u32[]{:S(2)}) collective-permute-start(f32[2,2048]{1,0:T(2,128)S(1)} %add_add_fusion.first), channel_id=1, source_target_pairs={{0,32},{32,0},{1,33},{33,1},{2,34},{34,2},{3,35},{35,3},{4,36},{36... | collective-permute-start | bytes 49160 | tf_op jit(solution)/shard_map/ppermute | solution.py:414
  29.4 3.2 %shard_map.101 = (f32[160,128]{1,0:T(8,128)S(1)}, f32[160,32]{1,0:T(8,128)S(1)}) custom-call(s32[27,160]{1,0:T(8,128)S(1)} %bitcast.22, s32[27,160]{1,0:T(8,128)S(1)} %bitcast.23, s32[1,160]{1,0:T(1,128)S(1)} %bitcast.25, bf16[27,128,1024]{2,1,0:T(8,128)(2,1)S(1)} %bitcast.21, bf16[160,1024]{1,0:T(8,128)(2,1)S(1)} %get-tuple-element.23.rest_4_), custom_call_target="tpu_custom_call" | custom-call | flops 1486356480 | bytes 7077888 | tf_op jit(solution)/shard_map/pallas_call | solution.py:383
  32.6 1.4 %collective-permute-done.8.second = f32[2,2048]{1,0:T(2,128)S(1)} collective-permute-done((f32[2,2048]{1,0:T(2,128)S(1)}, f32[2,2048]{1,0:T(2,128)S(1)}, u32[]{:S(2)}, u32[]{:S(2)}) %collective-permute-start.8) | collective-permute-done | bytes 16416 | tf_op jit(solution)/shard_map/ppermute | solution.py:414
  34.0 2.4 %shard_map.103 = (f32[4,160,128]{2,1,0:T(8,128)S(1)}, f32[4,160,128]{2,1,0:T(8,128)S(1)}) custom-call(f32[2,2048]{1,0:T(2,128)S(1)} %add_add_fusion.first, f32[2,2048]{1,0:T(2,128)S(1)} %collective-permute-done.8.second, f32[1,2048]{1,0:T(1,128)S(1)} %bitcast.24, f32[160,2048]{1,0:T(8,128)S(1)} %get-tuple-element.29.cos_c, ...), custom_call_target="tpu_custom_call" | custom-call | flops 1132462080 | bytes 2621440 | tf_op jit(solution)/shard_map/pallas_call | solution.py:286
  36.4 0.1 collective-permute-start.9
  36.5 0.5 %collective-permute-start.7 = (bf16[160,1024]{1,0:T(8,128)(2,1)S(1)}, bf16[160,1024]{1,0:T(8,128)(2,1)S(1)}, u32[]{:S(2)}, u32[]{:S(2)}) collective-permute-start(bf16[160,1024]{1,0:T(8,128)(2,1)S(1)} %collective-permute-done.6.rest_3_), channel_id=1, source_target_pairs={{0,1},{1,0},{2,3},{3,2},{4,5},{5,4},{6,7},{7,6},{8,9},{9,8},{10,11... | collective-permute-start | bytes 983048 | tf_op jit(solution)/shard_map/ppermute | solution.py:449
  37.0 1.1 %collective-permute-done.9 = f32[4,160,128]{2,1,0:T(8,128)S(1)} collective-permute-done((f32[4,160,128]{2,1,0:T(8,128)S(1)}, f32[4,160,128]{2,1,0:T(8,128)S(1)}, u32[]{:S(2)}, u32[]{:S(2)}) %collective-permute-start.9) | collective-permute-done | bytes 327712 | tf_op jit(solution)/shard_map/ppermute | solution.py:456
  38.1 1.9 %collective-permute-start.10 = (f16[160,128]{1,0:T(8,128)(2,1)S(1)}, f16[160,128]{1,0:T(8,128)(2,1)S(1)}, u32[]{:S(2)}, u32[]{:S(2)}) collective-permute-start(f16[160,128]{1,0:T(8,128)(2,1)S(1)} %get-tuple-element.41), channel_id=1, source_target_pairs={{0,6},{2,4},{4,2},{6,0},{1,7},{3,5},{5,3},{7,1},{8,14},{10,12},{12... | collective-permute-start | bytes 122888 | tf_op jit(solution)/shard_map/ppermute | solution.py:462
  40.1 0.6 %collective-permute-start.11 = (f16[160,128]{1,0:T(8,128)(2,1)S(1)}, f16[160,128]{1,0:T(8,128)(2,1)S(1)}, u32[]{:S(2)}, u32[]{:S(2)}) collective-permute-start(f16[160,128]{1,0:T(8,128)(2,1)S(1)} %get-tuple-element.43), channel_id=1, source_target_pairs={{0,4},{2,6},{4,0},{6,2},{1,5},{3,7},{5,1},{7,3},{8,12},{10,14},{12... | collective-permute-start | bytes 122888 | tf_op jit(solution)/shard_map/ppermute | solution.py:462
  40.7 1.9 %collective-permute-start.12 = (f16[160,128]{1,0:T(8,128)(2,1)S(1)}, f16[160,128]{1,0:T(8,128)(2,1)S(1)}, u32[]{:S(2)}, u32[]{:S(2)}) collective-permute-start(f16[160,128]{1,0:T(8,128)(2,1)S(1)} %get-tuple-element.42), channel_id=1, source_target_pairs={{0,2},{2,0},{4,6},{6,4},{1,3},{3,1},{5,7},{7,5},{8,10},{10,8},{12,... | collective-permute-start | bytes 122888 | tf_op jit(solution)/shard_map/ppermute | solution.py:462
  42.6 3.8 %shard_map.102 = f32[160,128]{1,0:T(8,128)S(1)} custom-call(f32[160,32]{1,0:T(8,128)S(1)} %get-tuple-element.24.rest_0_, bf16[27,128,1024]{2,1,0:T(8,128)(2,1)S(1)} %bitcast.21, f32[160,128]{1,0:T(8,128)S(1)} %get-tuple-element.27.rest_2_, bf16[160,1024]{1,0:T(8,128)(2,1)S(1)} %collective-permute-done.6.rest_3_, ...), custom_call_target="tpu_custom_call" | custom-call | flops 2972712960 | bytes 7077888 | tf_op jit(solution)/shard_map/pallas_call | solution.py:383
  46.5 0.7 %fusion.13 = f32[160,128]{1,0:T(8,128)} fusion(f32[160,128]{1,0:T(8,128)S(1)} %shard_map.102, f32[4,160,128]{2,1,0:T(8,128)S(1)} %collective-permute-done.9, f16[160,128]{1,0:T(8,128)(2,1)S(1)} %collective-permute-done.12, f16[160,128]{1,0:T(8,128)(2,1)S(1)} %collective-permute-done.11, f16[160,128]{1,0:T(8,128)(2,1)S(1)} %collective-permute-done.10, ...), kind=kLoop, calls=%fused_computation.24 | loop fusion | flops 225280 | bytes 450560 | tf_op jit(solution)/shard_map/add | solution.py:463
  (24 shorter events, 0.1 us)
Async XLA Ops:
  0.0 29.4 %slice-start = ((s8[7077888]{0:T(1024)(128)(4,1)}), s8[4194304]{0:T(1024)(128)(4,1)S(1)}, s32[]{:S(2)}) async-start(s8[7077888]{0:T(1024)(128)(4,1)} %bitcast.20), calls=%async_computation | async-start | bytes 8388608
  1.0 28.4 %slice-start.1 = ((s8[7077888]{0:T(1024)(128)(4,1)}), s8[2883584]{0:T(1024)(128)(4,1)S(1)}, s32[]{:S(2)}) async-start(s8[7077888]{0:T(1024)(128)(4,1)} %bitcast.20), calls=%async_computation.1 | async-start | bytes 5767168
  1.0 28.4 %copy-start = (s32[160,27]{0,1:T(8,128)S(1)}, s32[160,27]{0,1:T(8,128)}, u32[]{:S(2)}) copy-start(s32[160,27]{0,1:T(8,128)} %param.13) | copy-start | bytes 51844
  1.0 28.4 %copy-start.1 = (s32[160,27]{0,1:T(8,128)S(1)}, s32[160,27]{0,1:T(8,128)}, u32[]{:S(2)}) copy-start(s32[160,27]{0,1:T(8,128)} %param.12) | copy-start | bytes 51844
  1.0 28.4 %copy-start.3 = (s32[160]{0:T(256)S(1)}, s32[160]{0:T(256)}, u32[]{:S(2)}) copy-start(s32[160]{0:T(256)} %param.14) | copy-start | bytes 1924
  6.0 3.8 %collective-permute-start = (f32[2,2048]{1,0:T(2,128)S(1)}, f32[2,2048]{1,0:T(2,128)S(1)}, u32[]{:S(2)}, u32[]{:S(2)}) collective-permute-start(f32[2,2048]{1,0:T(2,128)S(1)} %get-tuple-element.25), channel_id=1, source_target_pairs={{0,8},{8,16},{16,24},{24,0},{1,9},{9,17},{17,25},{25,1},{2,10},{10... | collective-permute-start | bytes 49160 | tf_op jit(solution)/shard_map/ppermute | solution.py:414
  8.0 5.2 %collective-permute-start.1 = (f32[2,2048]{1,0:T(2,128)S(1)}, f32[2,2048]{1,0:T(2,128)S(1)}, u32[]{:S(2)}, u32[]{:S(2)}) collective-permute-start(f32[2,2048]{1,0:T(2,128)S(1)} %get-tuple-element.25), channel_id=1, source_target_pairs={{0,16},{8,24},{16,0},{24,8},{1,17},{9,25},{17,1},{25,9},{2,18},{10... | collective-permute-start | bytes 49160 | tf_op jit(solution)/shard_map/ppermute | solution.py:414
  8.9 4.9 %collective-permute-start.2 = (f32[2,2048]{1,0:T(2,128)S(1)}, f32[2,2048]{1,0:T(2,128)S(1)}, u32[]{:S(2)}, u32[]{:S(2)}) collective-permute-start(f32[2,2048]{1,0:T(2,128)S(1)} %get-tuple-element.25), channel_id=1, source_target_pairs={{0,24},{8,0},{16,8},{24,16},{1,25},{9,1},{17,9},{25,17},{2,26},{10... | collective-permute-start | bytes 49160 | tf_op jit(solution)/shard_map/ppermute | solution.py:414
  13.8 12.2 %collective-permute-start.3 = (f32[2,2048]{1,0:T(2,128)S(1)}, f32[2,2048]{1,0:T(2,128)S(1)}, u32[]{:S(2)}, u32[]{:S(2)}) collective-permute-start(f32[2,2048]{1,0:T(2,128)S(1)} %add_add_fusion.1), channel_id=1, source_target_pairs={{0,64},{64,128},{128,192},{192,0},{1,65},{65,129},{129,193},{193,1... | collective-permute-start | bytes 49160 | tf_op jit(solution)/shard_map/ppermute | solution.py:414
  15.4 10.6 %collective-permute-start.4 = (f32[2,2048]{1,0:T(2,128)S(1)}, f32[2,2048]{1,0:T(2,128)S(1)}, u32[]{:S(2)}, u32[]{:S(2)}) collective-permute-start(f32[2,2048]{1,0:T(2,128)S(1)} %add_add_fusion.1), channel_id=1, source_target_pairs={{0,128},{64,192},{128,0},{192,64},{1,129},{65,193},{129,1},{193,65... | collective-permute-start | bytes 49160 | tf_op jit(solution)/shard_map/ppermute | solution.py:414
  18.2 7.8 %collective-permute-start.5 = (f32[2,2048]{1,0:T(2,128)S(1)}, f32[2,2048]{1,0:T(2,128)S(1)}, u32[]{:S(2)}, u32[]{:S(2)}) collective-permute-start(f32[2,2048]{1,0:T(2,128)S(1)} %add_add_fusion.1), channel_id=1, source_target_pairs={{0,192},{64,0},{128,64},{192,128},{1,193},{65,1},{129,65},{193,129... | collective-permute-start | bytes 49160 | tf_op jit(solution)/shard_map/ppermute | solution.py:414
  19.6 16.9 %collective-permute-start.6 = (bf16[160,1024]{1,0:T(8,128)(2,1)}, bf16[160,1024]{1,0:T(8,128)(2,1)S(1)}, u32[]{:S(2)}, u32[]{:S(2)}) collective-permute-start(bf16[160,1024]{1,0:T(8,128)(2,1)} %density_far.1), channel_id=1, source_target_pairs={{0,8},{1,253},{2,10},{3,255},{4,12},{5,249},{6,14},{7,251},{8,16},... | collective-permute-start | bytes 983048 | tf_op jit(solution)/shard_map/ppermute | solution.py:439
  26.0 7.9 %collective-permute-start.8 = (f32[2,2048]{1,0:T(2,128)S(1)}, f32[2,2048]{1,0:T(2,128)S(1)}, u32[]{:S(2)}, u32[]{:S(2)}) collective-permute-start(f32[2,2048]{1,0:T(2,128)S(1)} %add_add_fusion.first), channel_id=1, source_target_pairs={{0,32},{32,0},{1,33},{33,1},{2,34},{34,2},{3,35},{35,3},{4,36},{36... | collective-permute-start | bytes 49160 | tf_op jit(solution)/shard_map/ppermute | solution.py:414
  29.4 4.6 %copy-start.2 = (f32[2048]{0:T(1024)S(1)}, f32[2048]{0:T(1024)}, u32[]{:S(2)}) copy-start(f32[2048]{0:T(1024)} %param.18) | copy-start | bytes 24580
  36.4 1.7 %collective-permute-start.9 = (f32[4,160,128]{2,1,0:T(8,128)S(1)}, f32[4,160,128]{2,1,0:T(8,128)S(1)}, u32[]{:S(2)}, u32[]{:S(2)}) collective-permute-start(f32[4,160,128]{2,1,0:T(8,128)S(1)} %get-tuple-element.40), channel_id=1, source_target_pairs={{0,1},{1,0},{2,3},{3,2},{4,5},{5,4},{6,7},{7,6},{8,9},{9,8},{10,11... | collective-permute-start | bytes 983048 | tf_op jit(solution)/shard_map/ppermute | solution.py:456
  36.5 6.1 %collective-permute-start.7 = (bf16[160,1024]{1,0:T(8,128)(2,1)S(1)}, bf16[160,1024]{1,0:T(8,128)(2,1)S(1)}, u32[]{:S(2)}, u32[]{:S(2)}) collective-permute-start(bf16[160,1024]{1,0:T(8,128)(2,1)S(1)} %collective-permute-done.6.rest_3_), channel_id=1, source_target_pairs={{0,1},{1,0},{2,3},{3,2},{4,5},{5,4},{6,7},{7,6},{8,9},{9,8},{10,11... | collective-permute-start | bytes 983048 | tf_op jit(solution)/shard_map/ppermute | solution.py:449
  38.1 8.3 %collective-permute-start.10 = (f16[160,128]{1,0:T(8,128)(2,1)S(1)}, f16[160,128]{1,0:T(8,128)(2,1)S(1)}, u32[]{:S(2)}, u32[]{:S(2)}) collective-permute-start(f16[160,128]{1,0:T(8,128)(2,1)S(1)} %get-tuple-element.41), channel_id=1, source_target_pairs={{0,6},{2,4},{4,2},{6,0},{1,7},{3,5},{5,3},{7,1},{8,14},{10,12},{12... | collective-permute-start | bytes 122888 | tf_op jit(solution)/shard_map/ppermute | solution.py:462
  40.1 6.4 %collective-permute-start.11 = (f16[160,128]{1,0:T(8,128)(2,1)S(1)}, f16[160,128]{1,0:T(8,128)(2,1)S(1)}, u32[]{:S(2)}, u32[]{:S(2)}) collective-permute-start(f16[160,128]{1,0:T(8,128)(2,1)S(1)} %get-tuple-element.43), channel_id=1, source_target_pairs={{0,4},{2,6},{4,0},{6,2},{1,5},{3,7},{5,1},{7,3},{8,12},{10,14},{12... | collective-permute-start | bytes 122888 | tf_op jit(solution)/shard_map/ppermute | solution.py:462
  40.7 5.7 %collective-permute-start.12 = (f16[160,128]{1,0:T(8,128)(2,1)S(1)}, f16[160,128]{1,0:T(8,128)(2,1)S(1)}, u32[]{:S(2)}, u32[]{:S(2)}) collective-permute-start(f16[160,128]{1,0:T(8,128)(2,1)S(1)} %get-tuple-element.42), channel_id=1, source_target_pairs={{0,2},{2,0},{4,6},{6,4},{1,3},{3,1},{5,7},{7,5},{8,10},{10,8},{12,... | collective-permute-start | bytes 122888 | tf_op jit(solution)/shard_map/ppermute | solution.py:462

commit v6 on v5

--- a/solution.py
+++ b/solution.py
@@ -443,8 +443,8 @@
     lists = (neighbour_offsets.T, neighbour_atoms.T, neighbour_counts[None, :])
     near_own, found = near_part(False, lists, near_blocks, [], [own])
 
-    structure = sum_over(partial, "y")
-    structure = sum_over(structure, "x")
+    structure = sum_over(partial, "x")
+    structure = sum_over(structure, "y")
     other_half = shifted(structure, "z_hi", 1)
     halo_other = lax.ppermute(halo, "core", [(0, 1), (1, 0)])
 

time: 47.5 us -> 47.7 us (level)
  waiting for transfers between devices: 7.37 us -> 4.78 us
  starting transfers between devices: 23.5 us -> 26 us
    ppermute x7, waiting for transfers between devices: 6.25 us -> 3.65 us  [shifted(): lax.ppermute(value, axis, [(i, (i + by) % count) for i in range(count)])]
    ppermute x1, starting transfers between devices: 6.42 us -> 8.92 us  [shards(): halo = lax.ppermute(density, BLOCK_AXES + ('z_lo', 'core'), halo_route)]
  transfers between devices with their start and end apart: 13 -> 13, of which waited for: 5 -> 4; matrix products, arithmetic and copies ran while one was open for 0% -> 0% of each run, Pallas kernels for 20% -> 20%
where the time goes in v6:
time: 47.7 us; the launch traced here: 47 us
  starting transfers between devices  26 us (55%)
  Pallas kernels  14.3 us (30%)
  waiting for transfers between devices  4.78 us (10%)
  other arithmetic  1.72 us (4%)
    ppermute x7, starting transfers between devices, shifted(): lax.ppermute(value, axis, [(i, (i + by) % count) for i in range(count)])  12 us
    ppermute x1, starting transfers between devices, shards(): halo = lax.ppermute(density, BLOCK_AXES + ('z_lo', 'core'), halo_route)  8.92 us
    pallas_call x2, Pallas kernels, near_part(): pl.pallas_call(functools.partial(near_kernel, group, is_halo), scratch_sh...  6.96 us
    pallas_call x1, Pallas kernels, partial_structure(): pl.pallas_call(functools.partial(structure_kernel, sizes), in_specs=[pl.B...  4.95 us
    ppermute x3, starting transfers between devices, shards(): lax.ppermute(piece, 'z_lo', swap).astype(jnp.float32) * 32.0  4.47 us
    ppermute x7, waiting for transfers between devices, shifted(): lax.ppermute(value, axis, [(i, (i + by) % count) for i in range(count)])  3.65 us
    pallas_call x1, Pallas kernels, far_partial(): pl.pallas_call(functools.partial(far_kernel, normalizer), out_shape=[jax....  2.36 us
    ppermute x1, waiting for transfers between devices, shards(): taken = lax.ppermute(send, 'core', [(0, 1), (1, 0)])  1.11 us
  transfers between devices with their start and end apart: 13, of which 4 were waited for; matrix products, arithmetic and copies ran while one was open for 0% of the time, Pallas kernels for 20%

profile of v6, /device:TPU:24, one launch (start us, length us, event | category | flops | bytes accessed | tf_op | source)
XLA Modules:
  0.0 47.0 jit_solution(12440636398152897238)
XLA Ops:
  0.0 1.0 %fusion.packed = f32[16,3840]{1,0:T(8,128)S(1)} fusion(f32[2,160]{1,0:T(2,128)} %param.15, f32[2,1024]{1,0:T(2,128)} %param.16, f32[2,2048]{1,0:T(2,128)} %param.17, f32[16,512]{1,0:T(8,128)} %constant.9.clone), kind=kLoop, calls=%fused_computation.5 | loop fusion | flops 798720 | bytes 304384 | tf_op jit(solution)/shard_map/concatenate | solution.py:222
  1.0 0.0 slice-start.1
  1.0 0.0 copy-start.1
  1.0 4.9 %shard_map.100 = (bf16[160,1024]{1,0:T(8,128)(2,1)S(1)}, f32[2,2048]{1,0:T(2,128)S(1)}, f32[160,2048]{1,0:T(8,128)S(1)}, f32[160,2048]{1,0:T(8,128)S(1)}, bf16[1...) custom-call(bf16[160,1024]{1,0:T(8,128)(2,1)} %density_far.1, ...), custom_call_target="tpu_custom_call" | custom-call | flops 8053063680 | bytes 2621440 | tf_op jit(solution)/shard_map/pallas_call | solution.py:226
  6.0 1.6 %collective-permute-start = (f32[2,2048]{1,0:T(2,128)S(1)}, f32[2,2048]{1,0:T(2,128)S(1)}, u32[]{:S(2)}, u32[]{:S(2)}) collective-permute-start(f32[2,2048]{1,0:T(2,128)S(1)} %get-tuple-element.25), channel_id=1, source_target_pairs={{0,64},{64,128},{128,192},{192,0},{1,65},{65,129},{129,193},{193,1... | collective-permute-start | bytes 49160 | tf_op jit(solution)/shard_map/ppermute | solution.py:414
  7.6 2.8 %collective-permute-start.1 = (f32[2,2048]{1,0:T(2,128)S(1)}, f32[2,2048]{1,0:T(2,128)S(1)}, u32[]{:S(2)}, u32[]{:S(2)}) collective-permute-start(f32[2,2048]{1,0:T(2,128)S(1)} %get-tuple-element.25), channel_id=1, source_target_pairs={{0,128},{64,192},{128,0},{192,64},{1,129},{65,193},{129,1},{193,65... | collective-permute-start | bytes 49160 | tf_op jit(solution)/shard_map/ppermute | solution.py:414
  10.3 1.4 %collective-permute-start.2 = (f32[2,2048]{1,0:T(2,128)S(1)}, f32[2,2048]{1,0:T(2,128)S(1)}, u32[]{:S(2)}, u32[]{:S(2)}) collective-permute-start(f32[2,2048]{1,0:T(2,128)S(1)} %get-tuple-element.25), channel_id=1, source_target_pairs={{0,192},{64,0},{128,64},{192,128},{1,193},{65,1},{129,65},{193,129... | collective-permute-start | bytes 49160 | tf_op jit(solution)/shard_map/ppermute | solution.py:414
  11.7 1.1 %collective-permute-done.1 = f32[2,2048]{1,0:T(2,128)S(1)} collective-permute-done((f32[2,2048]{1,0:T(2,128)S(1)}, f32[2,2048]{1,0:T(2,128)S(1)}, u32[]{:S(2)}, u32[]{:S(2)}) %collective-permute-start.1) | collective-permute-done | bytes 16416 | tf_op jit(solution)/shard_map/ppermute | solution.py:414
  12.8 1.3 %collective-permute-done.2 = f32[2,2048]{1,0:T(2,128)S(1)} collective-permute-done((f32[2,2048]{1,0:T(2,128)S(1)}, f32[2,2048]{1,0:T(2,128)S(1)}, u32[]{:S(2)}, u32[]{:S(2)}) %collective-permute-start.2) | collective-permute-done | bytes 16416 | tf_op jit(solution)/shard_map/ppermute | solution.py:414
  14.1 0.3 collective-permute-start.3
  14.4 2.6 %collective-permute-start.4 = (f32[2,2048]{1,0:T(2,128)S(1)}, f32[2,2048]{1,0:T(2,128)S(1)}, u32[]{:S(2)}, u32[]{:S(2)}) collective-permute-start(f32[2,2048]{1,0:T(2,128)S(1)} %add_add_fusion.1), channel_id=1, source_target_pairs={{0,16},{8,24},{16,0},{24,8},{1,17},{9,25},{17,1},{25,9},{2,18},{10... | collective-permute-start | bytes 49160 | tf_op jit(solution)/shard_map/ppermute | solution.py:414
  17.0 8.9 %collective-permute-start.6 = (bf16[160,1024]{1,0:T(8,128)(2,1)}, bf16[160,1024]{1,0:T(8,128)(2,1)S(1)}, u32[]{:S(2)}, u32[]{:S(2)}) collective-permute-start(bf16[160,1024]{1,0:T(8,128)(2,1)} %density_far.1), channel_id=1, source_target_pairs={{0,8},{1,253},{2,10},{3,255},{4,12},{5,249},{6,14},{7,251},{8,16},... | collective-permute-start | bytes 983048 | tf_op jit(solution)/shard_map/ppermute | solution.py:439
  25.9 3.4 %collective-permute-start.8 = (f32[2,2048]{1,0:T(2,128)S(1)}, f32[2,2048]{1,0:T(2,128)S(1)}, u32[]{:S(2)}, u32[]{:S(2)}) collective-permute-start(f32[2,2048]{1,0:T(2,128)S(1)} %add_add_fusion.first), channel_id=1, source_target_pairs={{0,32},{32,0},{1,33},{33,1},{2,34},{34,2},{3,35},{35,3},{4,36},{36... | collective-permute-start | bytes 49160 | tf_op jit(solution)/shard_map/ppermute | solution.py:414
  29.4 3.2 %shard_map.101 = (f32[160,128]{1,0:T(8,128)S(1)}, f32[160,32]{1,0:T(8,128)S(1)}) custom-call(s32[27,160]{1,0:T(8,128)S(1)} %bitcast.22, s32[27,160]{1,0:T(8,128)S(1)} %bitcast.23, s32[1,160]{1,0:T(1,128)S(1)} %bitcast.25, bf16[27,128,1024]{2,1,0:T(8,128)(2,1)S(1)} %bitcast.21, bf16[160,1024]{1,0:T(8,128)(2,1)S(1)} %get-tuple-element.23.rest_4_), custom_call_target="tpu_custom_call" | custom-call | flops 1486356480 | bytes 7077888 | tf_op jit(solution)/shard_map/pallas_call | solution.py:383
  32.6 1.3 %collective-permute-done.8.second = f32[2,2048]{1,0:T(2,128)S(1)} collective-permute-done((f32[2,2048]{1,0:T(2,128)S(1)}, f32[2,2048]{1,0:T(2,128)S(1)}, u32[]{:S(2)}, u32[]{:S(2)}) %collective-permute-start.8) | collective-permute-done | bytes 16416 | tf_op jit(solution)/shard_map/ppermute | solution.py:414
  33.9 2.4 %shard_map.103 = (f32[4,160,128]{2,1,0:T(8,128)S(1)}, f32[4,160,128]{2,1,0:T(8,128)S(1)}) custom-call(f32[2,2048]{1,0:T(2,128)S(1)} %add_add_fusion.first, f32[2,2048]{1,0:T(2,128)S(1)} %collective-permute-done.8.second, f32[1,2048]{1,0:T(1,128)S(1)} %bitcast.24, f32[160,2048]{1,0:T(8,128)S(1)} %get-tuple-element.29.cos_c, ...), custom_call_target="tpu_custom_call" | custom-call | flops 1132462080 | bytes 2621440 | tf_op jit(solution)/shard_map/pallas_call | solution.py:286
  36.2 0.1 collective-permute-start.9
  36.3 0.5 %collective-permute-start.7 = (bf16[160,1024]{1,0:T(8,128)(2,1)S(1)}, bf16[160,1024]{1,0:T(8,128)(2,1)S(1)}, u32[]{:S(2)}, u32[]{:S(2)}) collective-permute-start(bf16[160,1024]{1,0:T(8,128)(2,1)S(1)} %collective-permute-done.6.rest_3_), channel_id=1, source_target_pairs={{0,1},{1,0},{2,3},{3,2},{4,5},{5,4},{6,7},{7,6},{8,9},{9,8},{10,11... | collective-permute-start | bytes 983048 | tf_op jit(solution)/shard_map/ppermute | solution.py:449
  36.8 1.1 %collective-permute-done.9 = f32[4,160,128]{2,1,0:T(8,128)S(1)} collective-permute-done((f32[4,160,128]{2,1,0:T(8,128)S(1)}, f32[4,160,128]{2,1,0:T(8,128)S(1)}, u32[]{:S(2)}, u32[]{:S(2)}) %collective-permute-start.9) | collective-permute-done | bytes 327712 | tf_op jit(solution)/shard_map/ppermute | solution.py:456
  38.0 2.1 %collective-permute-start.10 = (f16[160,128]{1,0:T(8,128)(2,1)S(1)}, f16[160,128]{1,0:T(8,128)(2,1)S(1)}, u32[]{:S(2)}, u32[]{:S(2)}) collective-permute-start(f16[160,128]{1,0:T(8,128)(2,1)S(1)} %get-tuple-element.41), channel_id=1, source_target_pairs={{0,6},{2,4},{4,2},{6,0},{1,7},{3,5},{5,3},{7,1},{8,14},{10,12},{12... | collective-permute-start | bytes 122888 | tf_op jit(solution)/shard_map/ppermute | solution.py:462
  40.1 0.6 %collective-permute-start.11 = (f16[160,128]{1,0:T(8,128)(2,1)S(1)}, f16[160,128]{1,0:T(8,128)(2,1)S(1)}, u32[]{:S(2)}, u32[]{:S(2)}) collective-permute-start(f16[160,128]{1,0:T(8,128)(2,1)S(1)} %get-tuple-element.43), channel_id=1, source_target_pairs={{0,4},{2,6},{4,0},{6,2},{1,5},{3,7},{5,1},{7,3},{8,12},{10,14},{12... | collective-permute-start | bytes 122888 | tf_op jit(solution)/shard_map/ppermute | solution.py:462
  40.7 1.8 %collective-permute-start.12 = (f16[160,128]{1,0:T(8,128)(2,1)S(1)}, f16[160,128]{1,0:T(8,128)(2,1)S(1)}, u32[]{:S(2)}, u32[]{:S(2)}) collective-permute-start(f16[160,128]{1,0:T(8,128)(2,1)S(1)} %get-tuple-element.42), channel_id=1, source_target_pairs={{0,2},{2,0},{4,6},{6,4},{1,3},{3,1},{5,7},{7,5},{8,10},{10,8},{12,... | collective-permute-start | bytes 122888 | tf_op jit(solution)/shard_map/ppermute | solution.py:462
  42.5 3.8 %shard_map.102 = f32[160,128]{1,0:T(8,128)S(1)} custom-call(f32[160,32]{1,0:T(8,128)S(1)} %get-tuple-element.24.rest_0_, bf16[27,128,1024]{2,1,0:T(8,128)(2,1)S(1)} %bitcast.21, f32[160,128]{1,0:T(8,128)S(1)} %get-tuple-element.27.rest_2_, bf16[160,1024]{1,0:T(8,128)(2,1)S(1)} %collective-permute-done.6.rest_3_, ...), custom_call_target="tpu_custom_call" | custom-call | flops 2972712960 | bytes 7077888 | tf_op jit(solution)/shard_map/pallas_call | solution.py:383
  46.3 0.7 %fusion.13 = f32[160,128]{1,0:T(8,128)} fusion(f32[160,128]{1,0:T(8,128)S(1)} %shard_map.102, f32[4,160,128]{2,1,0:T(8,128)S(1)} %collective-permute-done.9, f16[160,128]{1,0:T(8,128)(2,1)S(1)} %collective-permute-done.12, f16[160,128]{1,0:T(8,128)(2,1)S(1)} %collective-permute-done.11, f16[160,128]{1,0:T(8,128)(2,1)S(1)} %collective-permute-done.10, ...), kind=kLoop, calls=%fused_computation.24 | loop fusion | flops 225280 | bytes 450560 | tf_op jit(solution)/shard_map/add | solution.py:463
  (24 shorter events, 0.1 us)
Async XLA Ops:
  0.0 29.4 %slice-start = ((s8[7077888]{0:T(1024)(128)(4,1)}), s8[4194304]{0:T(1024)(128)(4,1)S(1)}, s32[]{:S(2)}) async-start(s8[7077888]{0:T(1024)(128)(4,1)} %bitcast.20), calls=%async_computation | async-start | bytes 8388608
  1.0 28.4 %slice-start.1 = ((s8[7077888]{0:T(1024)(128)(4,1)}), s8[2883584]{0:T(1024)(128)(4,1)S(1)}, s32[]{:S(2)}) async-start(s8[7077888]{0:T(1024)(128)(4,1)} %bitcast.20), calls=%async_computation.1 | async-start | bytes 5767168
  1.0 28.4 %copy-start = (s32[160,27]{0,1:T(8,128)S(1)}, s32[160,27]{0,1:T(8,128)}, u32[]{:S(2)}) copy-start(s32[160,27]{0,1:T(8,128)} %param.13) | copy-start | bytes 51844
  1.0 28.4 %copy-start.1 = (s32[160,27]{0,1:T(8,128)S(1)}, s32[160,27]{0,1:T(8,128)}, u32[]{:S(2)}) copy-start(s32[160,27]{0,1:T(8,128)} %param.12) | copy-start | bytes 51844
  1.0 28.4 %copy-start.3 = (s32[160]{0:T(256)S(1)}, s32[160]{0:T(256)}, u32[]{:S(2)}) copy-start(s32[160]{0:T(256)} %param.14) | copy-start | bytes 1924
  6.0 5.7 %collective-permute-start = (f32[2,2048]{1,0:T(2,128)S(1)}, f32[2,2048]{1,0:T(2,128)S(1)}, u32[]{:S(2)}, u32[]{:S(2)}) collective-permute-start(f32[2,2048]{1,0:T(2,128)S(1)} %get-tuple-element.25), channel_id=1, source_target_pairs={{0,64},{64,128},{128,192},{192,0},{1,65},{65,129},{129,193},{193,1... | collective-permute-start | bytes 49160 | tf_op jit(solution)/shard_map/ppermute | solution.py:414
  7.6 5.2 %collective-permute-start.1 = (f32[2,2048]{1,0:T(2,128)S(1)}, f32[2,2048]{1,0:T(2,128)S(1)}, u32[]{:S(2)}, u32[]{:S(2)}) collective-permute-start(f32[2,2048]{1,0:T(2,128)S(1)} %get-tuple-element.25), channel_id=1, source_target_pairs={{0,128},{64,192},{128,0},{192,64},{1,129},{65,193},{129,1},{193,65... | collective-permute-start | bytes 49160 | tf_op jit(solution)/shard_map/ppermute | solution.py:414
  10.3 3.7 %collective-permute-start.2 = (f32[2,2048]{1,0:T(2,128)S(1)}, f32[2,2048]{1,0:T(2,128)S(1)}, u32[]{:S(2)}, u32[]{:S(2)}) collective-permute-start(f32[2,2048]{1,0:T(2,128)S(1)} %get-tuple-element.25), channel_id=1, source_target_pairs={{0,192},{64,0},{128,64},{192,128},{1,193},{65,1},{129,65},{193,129... | collective-permute-start | bytes 49160 | tf_op jit(solution)/shard_map/ppermute | solution.py:414
  14.1 11.8 %collective-permute-start.3 = (f32[2,2048]{1,0:T(2,128)S(1)}, f32[2,2048]{1,0:T(2,128)S(1)}, u32[]{:S(2)}, u32[]{:S(2)}) collective-permute-start(f32[2,2048]{1,0:T(2,128)S(1)} %add_add_fusion.1), channel_id=1, source_target_pairs={{0,8},{8,16},{16,24},{24,0},{1,9},{9,17},{17,25},{25,1},{2,10},{10... | collective-permute-start | bytes 49160 | tf_op jit(solution)/shard_map/ppermute | solution.py:414
  14.4 11.6 %collective-permute-start.4 = (f32[2,2048]{1,0:T(2,128)S(1)}, f32[2,2048]{1,0:T(2,128)S(1)}, u32[]{:S(2)}, u32[]{:S(2)}) collective-permute-start(f32[2,2048]{1,0:T(2,128)S(1)} %add_add_fusion.1), channel_id=1, source_target_pairs={{0,16},{8,24},{16,0},{24,8},{1,17},{9,25},{17,1},{25,9},{2,18},{10... | collective-permute-start | bytes 49160 | tf_op jit(solution)/shard_map/ppermute | solution.py:414
  17.0 8.9 %collective-permute-start.5 = (f32[2,2048]{1,0:T(2,128)S(1)}, f32[2,2048]{1,0:T(2,128)S(1)}, u32[]{:S(2)}, u32[]{:S(2)}) collective-permute-start(f32[2,2048]{1,0:T(2,128)S(1)} %add_add_fusion.1), channel_id=1, source_target_pairs={{0,24},{8,0},{16,8},{24,16},{1,25},{9,1},{17,9},{25,17},{2,26},{10... | collective-permute-start | bytes 49160 | tf_op jit(solution)/shard_map/ppermute | solution.py:414
  17.0 19.4 %collective-permute-start.6 = (bf16[160,1024]{1,0:T(8,128)(2,1)}, bf16[160,1024]{1,0:T(8,128)(2,1)S(1)}, u32[]{:S(2)}, u32[]{:S(2)}) collective-permute-start(bf16[160,1024]{1,0:T(8,128)(2,1)} %density_far.1), channel_id=1, source_target_pairs={{0,8},{1,253},{2,10},{3,255},{4,12},{5,249},{6,14},{7,251},{8,16},... | collective-permute-start | bytes 983048 | tf_op jit(solution)/shard_map/ppermute | solution.py:439
  25.9 7.9 %collective-permute-start.8 = (f32[2,2048]{1,0:T(2,128)S(1)}, f32[2,2048]{1,0:T(2,128)S(1)}, u32[]{:S(2)}, u32[]{:S(2)}) collective-permute-start(f32[2,2048]{1,0:T(2,128)S(1)} %add_add_fusion.first), channel_id=1, source_target_pairs={{0,32},{32,0},{1,33},{33,1},{2,34},{34,2},{3,35},{35,3},{4,36},{36... | collective-permute-start | bytes 49160 | tf_op jit(solution)/shard_map/ppermute | solution.py:414
  29.4 4.5 %copy-start.2 = (f32[2048]{0:T(1024)S(1)}, f32[2048]{0:T(1024)}, u32[]{:S(2)}) copy-start(f32[2048]{0:T(1024)} %param.18) | copy-start | bytes 24580
  36.2 1.7 %collective-permute-start.9 = (f32[4,160,128]{2,1,0:T(8,128)S(1)}, f32[4,160,128]{2,1,0:T(8,128)S(1)}, u32[]{:S(2)}, u32[]{:S(2)}) collective-permute-start(f32[4,160,128]{2,1,0:T(8,128)S(1)} %get-tuple-element.40), channel_id=1, source_target_pairs={{0,1},{1,0},{2,3},{3,2},{4,5},{5,4},{6,7},{7,6},{8,9},{9,8},{10,11... | collective-permute-start | bytes 983048 | tf_op jit(solution)/shard_map/ppermute | solution.py:456
  36.3 6.1 %collective-permute-start.7 = (bf16[160,1024]{1,0:T(8,128)(2,1)S(1)}, bf16[160,1024]{1,0:T(8,128)(2,1)S(1)}, u32[]{:S(2)}, u32[]{:S(2)}) collective-permute-start(bf16[160,1024]{1,0:T(8,128)(2,1)S(1)} %collective-permute-done.6.rest_3_), channel_id=1, source_target_pairs={{0,1},{1,0},{2,3},{3,2},{4,5},{5,4},{6,7},{7,6},{8,9},{9,8},{10,11... | collective-permute-start | bytes 983048 | tf_op jit(solution)/shard_map/ppermute | solution.py:449
  38.0 8.3 %collective-permute-start.10 = (f16[160,128]{1,0:T(8,128)(2,1)S(1)}, f16[160,128]{1,0:T(8,128)(2,1)S(1)}, u32[]{:S(2)}, u32[]{:S(2)}) collective-permute-start(f16[160,128]{1,0:T(8,128)(2,1)S(1)} %get-tuple-element.41), channel_id=1, source_target_pairs={{0,6},{2,4},{4,2},{6,0},{1,7},{3,5},{5,3},{7,1},{8,14},{10,12},{12... | collective-permute-start | bytes 122888 | tf_op jit(solution)/shard_map/ppermute | solution.py:462
  40.1 6.2 %collective-permute-start.11 = (f16[160,128]{1,0:T(8,128)(2,1)S(1)}, f16[160,128]{1,0:T(8,128)(2,1)S(1)}, u32[]{:S(2)}, u32[]{:S(2)}) collective-permute-start(f16[160,128]{1,0:T(8,128)(2,1)S(1)} %get-tuple-element.43), channel_id=1, source_target_pairs={{0,4},{2,6},{4,0},{6,2},{1,5},{3,7},{5,1},{7,3},{8,12},{10,14},{12... | collective-permute-start | bytes 122888 | tf_op jit(solution)/shard_map/ppermute | solution.py:462
  40.7 5.6 %collective-permute-start.12 = (f16[160,128]{1,0:T(8,128)(2,1)S(1)}, f16[160,128]{1,0:T(8,128)(2,1)S(1)}, u32[]{:S(2)}, u32[]{:S(2)}) collective-permute-start(f16[160,128]{1,0:T(8,128)(2,1)S(1)} %get-tuple-element.42), channel_id=1, source_target_pairs={{0,2},{2,0},{4,6},{6,4},{1,3},{3,1},{5,7},{7,5},{8,10},{10,8},{12,... | collective-permute-start | bytes 122888 | tf_op jit(solution)/shard_map/ppermute | solution.py:462
